TPU v7x, 512 devices: a whole 4x4x16 slice. The times are simulated.
512 devices in a mesh: seq: 32 (over z, core), tensor: 4 (over x), dp: 4 (over y).
Axes of the slice: x: 4, y: 4, z: 16, core: 2. Of those that a mesh axis runs over, the one named last changes fastest.
Arguments:
- prefix: bfloat16 [4, 16384, 2048], P('dp', 'seq'), may hold values from -6 to 6
- key_weight: bfloat16 [2048, 2048], P('seq', 'tensor'), may hold values from -0.125 to 0.125
- value_weight: bfloat16 [2048, 2048], P('seq', 'tensor'), may hold values from -0.125 to 0.125
- query_weight: bfloat16 [2048, 2048], P('seq', 'tensor'), may hold values from -0.125 to 0.125
- queries: bfloat16 [4, 1024, 2048], P('dp', 'seq', 'tensor'), may hold values from -6 to 6
- out_grad: bfloat16 [4, 1024, 2048], P('dp', 'seq', 'tensor'), may hold values from -6 to 6
- attn_out: bfloat16 [4, 1024, 2048], P('dp', 'seq', 'tensor'), may hold values from -6 to 6
- shifted_lse: float32 [4, 1024, 16], P('dp', 'seq', 'tensor'), may hold values from 0 to 1
- latent_in: bfloat16 [4, 1024, 2048], P('dp', None, 'seq'), may hold values from -6 to 6
Outputs:
- key_grad: bfloat16 [4, 16384, 2048], P('dp', 'seq', 'tensor')
- value_grad: bfloat16 [4, 16384, 2048], P('dp', 'seq', 'tensor')
- latent_grad: bfloat16 [4, 1024, 2048], P('dp', 'tensor', 'seq')
- query_weight_grad: float32 [2048, 2048], P('seq', 'tensor')
All inputs are finite; a program needn't handle non-finite values.
Results may differ from a plain program's by a relative error of at most 0.015.
The roundings to bfloat16 on the way count: a program that leaves them out, or rounds other values in their place, can miss the bound.
Values may be sent and summed in bfloat16 or wider, within the bound.
No kernel may reach another device: no remote copies, remote signals or barrier semaphores. Data moves between devices by JAX's collectives and lax.ppermute only.
A program may use at most 64 MiB of HBM per device.

v0:
```python
import math

import jax
import jax.numpy as jnp
from jax import lax
from jax.sharding import PartitionSpec as P


def local(
    prefix,
    key_weight,
    value_weight,
    query_weight,
    queries,
    out_grad,
    attn_out,
    shifted_lse,
    latent_in,
):
    tokens_in = prefix[0]
    token_count = tokens_in.shape[0]
    columns = key_weight.shape[1]
    head_count = shifted_lse.shape[2]
    head_size = columns // head_count
    scaling = 1.0 / math.sqrt(head_size)
    ranks = lax.axis_size("seq")
    groups = lax.axis_size("dp")
    key_sum = jnp.dot(
        tokens_in,
        lax.all_gather(key_weight, "seq", axis=0, tiled=True),
        preferred_element_type=jnp.float32,
    )
    value_sum = jnp.dot(
        tokens_in,
        lax.all_gather(value_weight, "seq", axis=0, tiled=True),
        preferred_element_type=jnp.float32,
    )
    key_rows = key_sum.astype(jnp.bfloat16).reshape(token_count, head_count, head_size)
    value_rows = value_sum.astype(jnp.bfloat16).reshape(token_count, head_count, head_size)
    local_grad = out_grad[0]
    row_delta = jnp.sum(
        (local_grad.astype(jnp.float32) * attn_out[0].astype(jnp.float32)).reshape(
            local_grad.shape[0], head_count, head_size
        ),
        axis=2,
    )
    query_all, grad_all = (
        lax.all_gather(queries, "seq", axis=1, tiled=True),
        lax.all_gather(out_grad, "seq", axis=1, tiled=True),
    )
    lse_all, delta_all = (
        lax.all_gather(shifted_lse, "seq", axis=1, tiled=True),
        lax.all_gather(row_delta[None], "seq", axis=1, tiled=True),
    )
    latent_count = query_all.shape[1]
    block_rows = min(latent_count, 512)
    query_heads = query_all[0].reshape(latent_count, head_count, head_size)
    grad_heads = grad_all[0].reshape(latent_count, head_count, head_size)
    lse_table = lse_all[0]
    delta_table = delta_all[0]
    prefix_factor = 1.0 / math.sqrt(token_count * ranks)
    latent_factor = 1.0 / math.sqrt(latent_count)

    def block_step(block_index, carried):
        key_acc, value_acc, query_acc = carried
        first = block_index * block_rows
        query_block = lax.dynamic_slice_in_dim(query_heads, first, block_rows, 0)
        grad_block = lax.dynamic_slice_in_dim(grad_heads, first, block_rows, 0)
        lse_block = lax.dynamic_slice_in_dim(lse_table, first, block_rows, 0)
        delta_block = lax.dynamic_slice_in_dim(delta_table, first, block_rows, 0)
        scores = (
            jnp.einsum("ihd,jhd->hij", query_block, key_rows, preferred_element_type=jnp.float32)
            * scaling
        )
        weights = jnp.exp(scores - jnp.transpose(lse_block)[:, :, None])
        grad_probs = jnp.einsum(
            "ihd,jhd->hij", grad_block, value_rows, preferred_element_type=jnp.float32
        )
        score_grad = weights * (grad_probs - jnp.transpose(delta_block)[:, :, None])
        weight_bf = weights.astype(jnp.bfloat16)
        score_bf = score_grad.astype(jnp.bfloat16)
        value_acc = value_acc + jnp.einsum(
            "hij,ihd->jhd", weight_bf, grad_block, preferred_element_type=jnp.float32
        )
        key_acc = key_acc + jnp.einsum(
            "hij,ihd->jhd", score_bf, query_block, preferred_element_type=jnp.float32
        )
        query_part = jnp.einsum(
            "hij,jhd->ihd", score_bf, key_rows, preferred_element_type=jnp.float32
        ) * (scaling * prefix_factor)
        query_acc = lax.dynamic_update_slice_in_dim(
            query_acc, query_part.reshape(block_rows, columns), first, 0
        )
        return (key_acc, value_acc, query_acc)

    zeros_heads = jnp.zeros((token_count, head_count, head_size), jnp.float32)
    zeros_query = jnp.zeros((latent_count, columns), jnp.float32)
    key_acc, value_acc, query_acc = lax.fori_loop(
        0, latent_count // block_rows, block_step, (zeros_heads, zeros_heads, zeros_query)
    )
    key_grad = (
        (key_acc * (scaling * latent_factor))
        .astype(jnp.bfloat16)
        .reshape(token_count, columns)[None]
    )
    value_grad = (
        (value_acc * latent_factor).astype(jnp.bfloat16).reshape(token_count, columns)[None]
    )
    query_full = lax.psum(query_acc, "seq").astype(jnp.bfloat16)
    latent_part = jnp.einsum(
        "ik,ck->ic", query_full, query_weight, preferred_element_type=jnp.float32
    )
    latent_grad = lax.psum_scatter(
        latent_part.astype(jnp.bfloat16), "tensor", scatter_dimension=0, tiled=True
    )[None]
    weight_part = jnp.einsum(
        "ic,ik->ck", latent_in[0], query_full, preferred_element_type=jnp.float32
    )
    weight_factor = 1.0 / math.sqrt(latent_count * groups)
    weight_grad = (
        lax.psum(weight_part.astype(jnp.bfloat16), "dp").astype(jnp.float32) * weight_factor
    )
    return (key_grad, value_grad, latent_grad, weight_grad)


def solution(mesh):
    return jax.shard_map(
        local,
        mesh=mesh,
        in_specs=(
            P("dp", "seq", None),
            P("seq", "tensor"),
            P("seq", "tensor"),
            P("seq", "tensor"),
            P("dp", "seq", "tensor"),
            P("dp", "seq", "tensor"),
            P("dp", "seq", "tensor"),
            P("dp", "seq", "tensor"),
            P("dp", None, "seq"),
        ),
        out_specs=(
            P("dp", "seq", "tensor"),
            P("dp", "seq", "tensor"),
            P("dp", "tensor", "seq"),
            P("seq", "tensor"),
        ),
        check_vma=False,
    )
```

profile of v0, /device:TPU:1, one launch (start us, length us, event | category | flops | bytes accessed | tf_op | source)
XLA Modules:
  0.0 527.6 jit_solution(7756528463311864271)
XLA Ops:
  11.8 37.7 %all-gather.1 = f32[32,32,4]{1,2,0:T(4,128)S(1)} all-gather(f32[1,32,4]{1,2,0:T(4,128)S(1)} %bitcast.76), channel_id=2, replica_groups=mesh['seq'=32,'tensor'=4,'dp'=4] {'seq'}, dimensions={0}, use_global_device_ids=true | all-gather | bytes 16896 | tf_op jit(solution)/shard_map/all_gather | solution.py:53
  49.6 28.6 %all_gather.20 = f32[1,1024,4]{2,0,1:T(1,128)S(1)} all-gather(f32[1,32,4]{2,0,1:T(1,128)S(1)} %copy.34), channel_id=1, replica_groups=mesh['seq'=32,'tensor'=4,'dp'=4] {'seq'}, dimensions={1}, use_global_device_ids=true | all-gather | bytes 16896 | tf_op jit(solution)/shard_map/all_gather | solution.py:52
  78.4 8.2 %all-gather.7.cloned.1.call-done = bf16[1,1024,512]{2,1,0:T(8,128)(2,1)} async-done(((bf16[1,32,512]{2,1,0:T(8,128)(2,1)}), bf16[1,1024,512]{2,1,0:T(8,128)(2,1)}) %all-gather.7.cloned.1.call-update) | async-done | bytes 1048592 | tf_op jit(solution)/shard_map/all_gather | solution.py:48
  86.6 2.3 copy.33
  88.9 67.7 %all-gather.11.cloned.1.call-done = bf16[1,1024,512]{2,1,0:T(8,128)(2,1)} async-done(((bf16[1,32,512]{2,1,0:T(8,128)(2,1)}), bf16[1,1024,512]{2,1,0:T(8,128)(2,1)}) %all-gather.11.cloned.1.call-update) | async-done | bytes 1048592 | tf_op jit(solution)/shard_map/all_gather | solution.py:49
  156.6 2.3 copy.35
  158.9 68.8 %all-gather.13.cloned.1.call-done = bf16[2048,512]{1,0:T(8,128)(2,1)} async-done(((bf16[64,512]{1,0:T(8,128)(2,1)}), bf16[2048,512]{1,0:T(8,128)(2,1)}) %all-gather.13.cloned.1.call-update) | async-done | bytes 2097168 | tf_op jit(solution)/shard_map/all_gather | solution.py:35
  227.7 2.9 fusion.29
  230.9 67.5 %all-gather.9.cloned.1.call-done = bf16[2048,512]{1,0:T(8,128)(2,1)} async-done(((bf16[64,512]{1,0:T(8,128)(2,1)}), bf16[2048,512]{1,0:T(8,128)(2,1)}) %all-gather.9.cloned.1.call-update) | async-done | bytes 2097168 | tf_op jit(solution)/shard_map/all_gather | solution.py:30
  298.4 2.9 fusion.26
  301.3 1.6 broadcast_in_dim.19
  302.9 18.2 %while.18 = (s32[]{:T(128)}, f32[512,4,128]{0,2,1:T(8,128)}, f32[512,4,128]{0,2,1:T(8,128)}, f32[1024,512]{0,1:T(8,128)}, bf16[1024,4,128]{0,2,1:T(8,128)(2,1)},...) while((s32[]{:T(128)}, f32[512,4,128]{0,2,1:T(8,128)}, ...), condition=%wide.region_2.0_spmd.clone, body=%wide.region_1.0_spmd.clone.sunk | while | flops 1351876608 | bytes 71885248 | solution.py:98
  302.9 1.9 fusion.69
  304.9 1.2 fusion.71
  306.1 1.5 multiply_convert_fusion.4
  309.4 1.1 copy-done.8
  310.7 1.3 copy-done.9
  312.0 1.9 fusion.69
  314.0 1.2 fusion.71
  315.2 1.5 multiply_convert_fusion.4
  317.7 0.8 convolution_multiply_fusion.2
  318.5 1.1 copy-done.8
  319.8 1.3 copy-done.9
  321.1 112.0 %all-reduce.4 = bf16[1024,512]{0,1:T(8,128)(2,1)} all-reduce(f32[1024,512]{0,1:T(8,128)} %get-tuple-element.177), channel_id=1, replica_groups=mesh['seq'=32,'tensor'=4,'dp'=4] {'seq'}, use_global_device_ids=true, to_apply=%region_3.0 | all-reduce | flops 524288 | bytes 3145728 | tf_op jit(solution)/shard_map/psum | solution.py:109
  433.1 2.4 fusion.32
  435.6 2.2 convolution_convert_fusion
  437.8 2.5 multiply_convert_fusion.1
  440.3 2.0 copy.48
  442.3 2.0 copy.47
  444.4 44.6 %all-reduce.3.cloned.1.call-done = bf16[64,512]{1,0:T(8,128)(2,1)} async-done(((bf16[64,512]{1,0:T(8,128)(2,1)}), bf16[64,512]{1,0:T(8,128)(2,1)}) %all-reduce.3.cloned.1.call-update) | async-done | bytes 65552 | tf_op jit(solution)/shard_map/psum | solution.py:121
  488.9 1.5 convert_multiply_fusion
  490.4 30.3 %reduce-scatter.2.cloned.1.call-done = bf16[256,64]{0,1:T(8,128)(2,1)} async-done(((bf16[1024,64]{0,1:T(8,128)(2,1)}), bf16[256,64]{0,1:T(8,128)(2,1)}) %reduce-scatter.2.cloned.1.call-update) | async-done | bytes 32784 | tf_op jit(solution)/shard_map/reduce_scatter | solution.py:113
  (66 shorter events, 8.1 us)
Async XLA Ops:
  7.2 220.6 %copy-start = (bf16[1,512,2048]{2,1,0:T(8,128)(2,1)S(1)}, bf16[1,512,2048]{2,1,0:T(8,128)(2,1)}, u32[]{:S(2)}) copy-start(bf16[1,512,2048]{2,1,0:T(8,128)(2,1)} %param.11) | copy-start | bytes 6291460
  7.2 79.5 %all-gather.7.cloned.1.call-start = ((), (), s32[]{:S(2)}) async-start(), calls=%async_computation.1 | async-start | bytes 1081344 | tf_op jit(solution)/shard_map/all_gather | solution.py:48
  7.9 148.7 %all-gather.11.cloned.1.call-start = ((), (), s32[]{:S(2)}) async-start(), calls=%async_computation.3 | async-start | bytes 1081344 | tf_op jit(solution)/shard_map/all_gather | solution.py:49
  8.7 219.1 %all-gather.13.cloned.1.call-start = ((), (), s32[]{:S(2)}) async-start(), calls=%async_computation.4 | async-start | bytes 2162688 | tf_op jit(solution)/shard_map/all_gather | solution.py:35
  9.4 289.0 %all-gather.9.cloned.1.call-start = ((), (), s32[]{:S(2)}) async-start(), calls=%async_computation.2 | async-start | bytes 2162688 | tf_op jit(solution)/shard_map/all_gather | solution.py:30
  10.0 479.0 %all-reduce.3.cloned.1.call-start = ((), (), s32[]{:S(2)}) async-start(), calls=%async_computation.6 | async-start | bytes 131072 | tf_op jit(solution)/shard_map/psum | solution.py:121
  302.9 2.0 copy-start.4
  302.9 2.0 copy-start.7
  306.1 1.5 copy-start.5
  306.1 1.6 copy-start.1
  306.1 1.9 copy-start.6
  308.6 2.1 copy-start.2
  308.6 2.0 copy-start.8
  310.7 1.3 copy-start.9
  312.0 2.0 copy-start.4
  312.0 2.0 copy-start.7
  315.2 1.5 copy-start.5
  315.2 1.6 copy-start.1
  315.2 1.9 copy-start.6
  317.7 2.1 copy-start.2
  317.7 2.0 copy-start.8
  319.8 1.3 copy-start.9
  321.1 112.0 %copy-start.10 = (bf16[1,1024,64]{1,2,0:T(8,128)(2,1)S(1)}, bf16[1,1024,64]{1,2,0:T(8,128)(2,1)}, u32[]{:S(2)}) copy-start(bf16[1,1024,64]{1,2,0:T(8,128)(2,1)} %param.19) | copy-start | bytes 393220
  321.1 114.5 %copy-start.11 = (bf16[64,512]{1,0:T(8,128)(2,1)S(1)}, bf16[64,512]{1,0:T(8,128)(2,1)}, u32[]{:S(2)}) copy-start(bf16[64,512]{1,0:T(8,128)(2,1)} %param.14) | copy-start | bytes 196612
  433.1 4.7 copy-start.3
  435.5 85.2 %reduce-scatter.2.cloned.1.call-start = ((), (), s32[]{:S(2)}) async-start(), calls=%async_computation.5 | async-start | bytes 163840 | tf_op jit(solution)/shard_map/reduce_scatter | solution.py:113
Sparse Core Ops, SparseCore 0:
  10.1 76.4 all-gather.6
  88.7 67.8 all-gather.10
  158.8 68.9 all-gather.12
  229.7 68.6 all-gather.8
  435.6 53.2 all-reduce.2
  492.4 28.2 reduce-scatter.1
where the time goes:
time: 530 us; the launch traced here: 528 us
  waiting for transfers between devices  290 us (55%)
  blocking collectives  178 us (34%)
  matrix products  22.3 us (4%)
  local copies, waits for them, and re-layouts  17.6 us (3%)
  between operations  14.2 us (3%)
    psum x1, blocking collectives, local(): query_full = lax.psum(query_acc, 'seq').astype(jnp.bfloat16)  112 us
    all_gather x1, waiting for transfers between devices, local(): lax.all_gather(value_weight, 'seq', axis=0, tiled=True)  68.8 us
    all_gather x1, waiting for transfers between devices, local(): lax.all_gather(out_grad, 'seq', axis=1, tiled=True)  67.7 us
    all_gather x1, waiting for transfers between devices, local(): lax.all_gather(key_weight, 'seq', axis=0, tiled=True)  67.5 us
    psum x1, waiting for transfers between devices, local(): lax.psum(weight_part.astype(jnp.bfloat16), 'dp').astype(jnp.float32)  44.6 us
    all_gather x1, blocking collectives, local(): lax.all_gather(row_delta[None], 'seq', axis=1, tiled=True)  37.7 us
    reduce_scatter x1, waiting for transfers between devices, local(): lax.psum_scatter(latent_part.astype(jnp.bfloat16), 'tensor', scatter_dime...  30.3 us
    all_gather x1, blocking collectives, local(): lax.all_gather(shifted_lse, 'seq', axis=1, tiled=True)  28.6 us
  transfers between devices with their start and end apart: 6, of which 6 were waited for; matrix products, arithmetic and copies ran while one was open for 4% of the time, Pallas kernels for 0%

commit v1 on v0

v1 whole, which is shorter than its diff:
```python
import math

import jax
import jax.numpy as jnp
from jax import lax
from jax.experimental import pallas as pl
from jax.experimental.pallas import tpu as pltpu
from jax.sharding import Mesh, PartitionSpec as P

BF = jnp.bfloat16
F32 = jnp.float32
SEQ = ("zh", "zl", "core")
SWAP = [(0, 1), (1, 0)]


def dot(a, b):
    return jnp.dot(a, b, preferred_element_type=F32)


def dot_nt(a, b):
    return lax.dot_general(a, b, (((1,), (1,)), ((), ())), preferred_element_type=F32)


def project_kernel(own_ref, other_ref, weight_ref, out_ref):
    step = pl.program_id(0)
    half = pl.num_programs(0) // 2
    size = weight_ref.shape[2]

    def run(rows):
        for pair in range(2):
            weight = jnp.concatenate([weight_ref[2 * pair], weight_ref[2 * pair + 1]], axis=1)
            out_ref[:, 2 * pair * size : 2 * (pair + 1) * size] = dot(rows, weight).astype(BF)

    @pl.when(step < half)
    def _():
        run(own_ref[...])

    @pl.when(step >= half)
    def _():
        run(other_ref[...])


def project(own, other, weight):
    rows, width = own.shape
    slabs, _, size = weight.shape
    block = 256
    half = rows // block
    return pl.pallas_call(
        project_kernel,
        grid=(2 * half,),
        in_specs=[
            pl.BlockSpec((block, width), lambda t: (jnp.minimum(t, half - 1), 0)),
            pl.BlockSpec((block, width), lambda t: (jnp.maximum(t - half, 0), 0)),
            pl.BlockSpec((slabs, width, size), lambda t: (0, 0, 0)),
        ],
        out_specs=pl.BlockSpec((block, slabs * size), lambda t: (t, 0)),
        out_shape=jax.ShapeDtypeStruct((2 * rows, slabs * size), BF),
        compiler_params=pltpu.CompilerParams(vmem_limit_bytes=40 * 2**20),
        cost_estimate=pl.CostEstimate(
            flops=4 * rows * width * slabs * size, bytes_accessed=8 * 2**20, transcendentals=0
        ),
    )(own, other, weight)


def attend_kernel(
    core_ref, kv_ref, query_ref, grad_ref, stat_ref, own_ref, other_ref, part_ref, qt, gt, total,
    *, size, scaling, latent_factor, prefix_factor,
):
    step = pl.program_id(0)
    last = pl.num_programs(0) - 1
    half = pl.num_programs(0) // 2

    @pl.when(step == 0)
    def _():
        qt[...] = query_ref[...].T
        gt[...] = grad_ref[...].T
        total[...] = jnp.zeros_like(total)

    key_out, value_out = [], []
    for head in range(2):
        cols = slice(head * size, (head + 1) * size)
        keys = kv_ref[:, cols]
        values = kv_ref[:, (2 + head) * size : (3 + head) * size]
        scores = dot(keys, qt[cols, :]) * scaling
        weights = jnp.exp(scores - stat_ref[2 * head : 2 * head + 1, :])
        probs = dot(values, gt[cols, :])
        score_grad = (weights * (probs - stat_ref[2 * head + 1 : 2 * head + 2, :])).astype(BF)
        value_out.append(dot(weights.astype(BF), grad_ref[:, cols]) * latent_factor)
        key_out.append(dot(score_grad, query_ref[:, cols]) * (scaling * latent_factor))
        total[cols, :] += dot(keys.T, score_grad)
    result = jnp.concatenate(key_out + value_out, axis=1).astype(BF)

    @pl.when(step < half)
    def _():
        own_ref[...] = result

    @pl.when(step >= half)
    def _():
        other_ref[...] = result

    @pl.when(step == last)
    def _():
        count, _, width = part_ref.shape
        for i in range(count):
            part_ref[i] = (
                total[:, i * width : (i + 1) * width] * (scaling * prefix_factor)
            ).astype(BF)


def attend(core, kv, gathered, stats, groups, prefix_count):
    tokens, columns = kv.shape
    latents = gathered.shape[0]
    size = columns // 4
    block = 256
    half = tokens // block // 2
    kernel = lambda *refs: attend_kernel(
        *refs,
        size=size,
        scaling=1.0 / math.sqrt(size),
        latent_factor=1.0 / math.sqrt(latents),
        prefix_factor=1.0 / math.sqrt(prefix_count),
    )
    return pl.pallas_call(
        kernel,
        grid_spec=pltpu.PrefetchScalarGridSpec(
            num_scalar_prefetch=1,
            grid=(tokens // block,),
            in_specs=[
                pl.BlockSpec((block, columns), lambda t, c: (t, 0)),
                pl.BlockSpec((latents, 2 * size), lambda t, c: (0, c[0])),
                pl.BlockSpec((latents, 2 * size), lambda t, c: (0, c[0] + 2)),
                pl.BlockSpec(stats.shape, lambda t, c: (0, 0)),
            ],
            out_specs=[
                pl.BlockSpec((block, columns), lambda t, c: (jnp.minimum(t, half - 1), 0)),
                pl.BlockSpec((block, columns), lambda t, c: (jnp.maximum(t - half, 0), 0)),
                pl.BlockSpec((groups, 2 * size, latents // groups), lambda t, c: (0, 0, 0)),
            ],
            scratch_shapes=[
                pltpu.VMEM((2 * size, latents), BF),
                pltpu.VMEM((2 * size, latents), BF),
                pltpu.VMEM((2 * size, latents), F32),
            ],
        ),
        out_shape=[
            jax.ShapeDtypeStruct((tokens // 2, columns), BF),
            jax.ShapeDtypeStruct((tokens // 2, columns), BF),
            jax.ShapeDtypeStruct((groups, 2 * size, latents // groups), BF),
        ],
        compiler_params=pltpu.CompilerParams(vmem_limit_bytes=48 * 2**20),
        cost_estimate=pl.CostEstimate(
            flops=20 * tokens * latents * size,
            bytes_accessed=6 * 2**20,
            transcendentals=2 * tokens * latents,
        ),
    )(core, kv, gathered, gathered, stats)


def exchange(x, axes):
    return lax.all_to_all(x, axes, 0, 0, tiled=True)


def spread(x, axes):
    count = lax.axis_size(axes)
    return exchange(jnp.broadcast_to(x[None], (count,) + x.shape), axes)


def halves(x):
    return jnp.transpose(x.reshape(x.shape[0], 2, x.shape[1] // 2), (1, 0, 2))


def two_parts(x):
    high = lax.reduce_precision(x, 8, 7)
    return high.astype(BF), (x - high).astype(BF)


def local(
    prefix, key_weight, value_weight, query_weight, queries, out_grad, attn_out, shifted_lse, latent_in
):
    core = lax.axis_index("core")
    batch = lax.axis_index("dp")
    first = core == 0
    ranks = lax.axis_size(SEQ)
    batches = lax.axis_size("dp")
    tokens_in = prefix[0]
    token_count = tokens_in.shape[0]
    rows, columns = queries.shape[1:]
    heads = shifted_lse.shape[2]
    size = columns // heads
    latents = rows * ranks

    gathered = lax.all_gather(
        jnp.concatenate([queries[0], out_grad[0]], axis=1), SEQ, axis=0, tiled=True
    )
    other_tokens = lax.ppermute(tokens_in, "core", SWAP)
    latent_own = latent_in[0].T
    query_halves = halves(query_weight)
    query_mine = jnp.where(first, query_halves[0], query_halves[1])
    query_theirs = jnp.where(first, query_halves[1], query_halves[0])
    swapped = lax.ppermute(jnp.concatenate([latent_own, query_theirs], axis=1), "core", SWAP)
    latent_other, query_other = swapped[:, :latents], swapped[:, latents:]

    def in_order(own, other):
        return jnp.where(first, jnp.concatenate([own, other], 0), jnp.concatenate([other, own], 0))

    latent_both = in_order(latent_own, latent_other)
    query_both = in_order(query_mine, query_other)

    row_delta = jnp.sum(
        (out_grad[0].astype(F32) * attn_out[0].astype(F32)).reshape(rows, heads, size), axis=2
    )
    stats = jnp.stack([shifted_lse[0], row_delta]).reshape(2, rows, 2, heads // 2)
    high, low = two_parts(stats)
    packed = jnp.transpose(jnp.stack([high, low]), (3, 1, 0, 4, 2))
    packed = packed.reshape(2, 2, 2 * (heads // 2) * rows)
    packed = jnp.pad(packed, ((0, 0), (0, 14), (0, 0)))
    slabs = jnp.concatenate([halves(key_weight), halves(value_weight)], axis=2)
    slab = lax.dynamic_slice_in_dim(slabs, batch * size, size, 2)
    block = jnp.concatenate([slab, packed], axis=1)
    block = jnp.broadcast_to(block[None], (ranks // 2,) + block.shape).reshape((ranks,) + block.shape[1:])
    landed = exchange(block, SEQ)
    depth = key_weight.shape[0]
    weight = spread(landed[:, :depth].reshape(depth * ranks, size), "dp")
    stats_all = landed[:, depth : depth + 2].astype(F32).reshape(ranks, 2, 2, heads // 2, rows)
    stats_all = jnp.transpose(stats_all[:, :, 0] + stats_all[:, :, 1], (2, 1, 0, 3))
    stats_all = stats_all.reshape(heads, latents)

    kv = project(tokens_in, other_tokens, weight)
    groups = lax.axis_size("zl")
    own_grads, other_grads, part = attend(
        jnp.reshape(core, (1,)).astype(jnp.int32), kv, gathered, stats_all, groups, token_count * ranks
    )
    theirs = lax.ppermute(other_grads, "core", SWAP)
    half = columns // 2

    def whole(lo):
        mine, other = own_grads[:, lo : lo + half], theirs[:, lo : lo + half]
        return jnp.where(
            first, jnp.concatenate([mine, other], 1), jnp.concatenate([other, mine], 1)
        )[None]

    near = jnp.sum(exchange(part, "zl").astype(F32), axis=0).astype(BF)
    full = jnp.sum(spread(near, "zh").astype(F32), axis=0).astype(BF)
    every = lax.all_gather(full, "zl", axis=1, tiled=True)

    latent_part = dot(query_both, every).astype(BF)
    latent_part = latent_part.reshape(2, columns // 8, lax.axis_size("tensor"), -1)
    latent_part = jnp.transpose(latent_part, (0, 2, 1, 3)).reshape(-1, columns // 8, latents // 4)
    latent_sum = jnp.sum(exchange(latent_part, ("core", "tensor")).astype(F32), axis=0)
    latent_grad = latent_sum.astype(BF).T[None]

    weight_part = dot_nt(latent_both, every).astype(BF)
    weight_part = weight_part.reshape(2, 1, columns // 8, half)
    weight_part = jnp.broadcast_to(weight_part, (2, batches, columns // 8, half))
    weight_sum = exchange(weight_part.reshape(-1, columns // 8, half), ("core", "dp"))
    weight_sum = jnp.sum(weight_sum.reshape(2, batches, columns // 8, half).astype(F32), axis=1)
    weight_factor = 1.0 / math.sqrt(latents * batches)
    weight_grad = jnp.transpose(weight_sum, (1, 0, 2)).reshape(columns // 8, columns) * weight_factor
    return (whole(0), whole(half), latent_grad, weight_grad)


def solution(mesh):
    fine = Mesh(
        mesh.devices.reshape(4, 4, 2, *mesh.devices.shape[1:]), SEQ + tuple(mesh.axis_names[1:])
    )
    return jax.shard_map(
        local,
        mesh=fine,
        in_specs=(
            P("dp", SEQ, None),
            P(SEQ, "tensor"),
            P(SEQ, "tensor"),
            P(SEQ, "tensor"),
            P("dp", SEQ, "tensor"),
            P("dp", SEQ, "tensor"),
            P("dp", SEQ, "tensor"),
            P("dp", SEQ, "tensor"),
            P("dp", None, SEQ),
        ),
        out_specs=(
            P("dp", SEQ, "tensor"),
            P("dp", SEQ, "tensor"),
            P("dp", "tensor", SEQ),
            P(SEQ, "tensor"),
        ),
        check_vma=False,
    )
```

time: 530 us -> 220 us (0.42)
  waiting for transfers between devices: 290 us -> 97.4 us
  blocking collectives: 178 us -> 31.7 us
  starting transfers between devices: 0.23 us -> 49.3 us
  matrix products: 22.3 us -> 0.55 us
  Pallas kernels: 0 us -> 11.7 us
  local copies, waits for them, and re-layouts: 17.6 us -> 9.65 us
    all_gather x4 -> x1, waiting for transfers between devices: 212 us -> 3.36 us  [local(): lax.all_gather(jnp.concatenate([queries[0], out_grad[0]], axis=1), SEQ, a...]
    psum x1 -> x0, blocking collectives: 112 us -> none  [local(): query_full = lax.psum(query_acc, 'seq').astype(jnp.bfloat16)]
    all_to_all x0 -> x5, waiting for transfers between devices: none -> 92.6 us  [exchange(): return lax.all_to_all(x, axes, 0, 0, tiled=True)]
    all_gather x2 -> x1, blocking collectives: 66.3 us -> 13.4 us  [local(): every = lax.all_gather(full, 'zl', axis=1, tiled=True)]
    psum x1 -> x0, waiting for transfers between devices: 44.6 us -> none  [local(): lax.psum(weight_part.astype(jnp.bfloat16), 'dp').astype(jnp.float32)]
    all_to_all x0 -> x5, starting transfers between devices: none -> 41.6 us  [exchange(): return lax.all_to_all(x, axes, 0, 0, tiled=True)]
    reduce_scatter x1 -> x0, waiting for transfers between devices: 30.3 us -> none  [local(): lax.psum_scatter(latent_part.astype(jnp.bfloat16), 'tensor', scatter_dime...]
    dot_general x14 -> x2, matrix products: 22.3 us -> 0.55 us  [the longest x1 0.31 us: dot_nt(): lax.dot_general(a, b, (((1,), (1,)), ((), ())), preferred_element_type=F32)]
  transfers between devices with their start and end apart: 6 -> 9, of which waited for: 6 -> 7; matrix products, arithmetic and copies ran while one was open for 4% -> 3% of each run, Pallas kernels for 0% -> 2%
where the time goes in v1:
time: 220 us; the launch traced here: 219 us
  waiting for transfers between devices  97.4 us (44%)
  starting transfers between devices  49.3 us (22%)
  blocking collectives  31.7 us (14%)
  between operations  14.3 us (6%)
  Pallas kernels  11.7 us (5%)
  local copies, waits for them, and re-layouts  9.65 us (4%)
  other arithmetic  4.65 us (2%)
    all_to_all x5, waiting for transfers between devices, exchange(): return lax.all_to_all(x, axes, 0, 0, tiled=True)  92.6 us
    all_to_all x5, starting transfers between devices, exchange(): return lax.all_to_all(x, axes, 0, 0, tiled=True)  41.6 us
    all_to_all x1, blocking collectives, exchange(): return lax.all_to_all(x, axes, 0, 0, tiled=True)  18.3 us
    all_gather x1, blocking collectives, local(): every = lax.all_gather(full, 'zl', axis=1, tiled=True)  13.4 us
    pallas_call x1, Pallas kernels, attend(): pl.pallas_call(kernel, grid_spec=pltpu.PrefetchScalarGridSpec(num_scalar_...  6.71 us
    pallas_call x1, Pallas kernels, project(): pl.pallas_call(project_kernel, grid=(2 * half,), in_specs=[pl.BlockSpec((...  4.97 us
  transfers between devices with their start and end apart: 9, of which 7 were waited for; matrix products, arithmetic and copies ran while one was open for 3% of the time, Pallas kernels for 2%

profile of v1, /device:TPU:1, one launch (start us, length us, event | category | flops | bytes accessed | tf_op | source)
XLA Modules:
  0.0 219.2 jit_solution(12651966328315568970)
XLA Ops:
  7.2 0.9 reshape.261
  8.1 0.9 reshape.262
  8.9 0.8 convert_multiply_fusion
  9.9 0.7 reduce-precision_convert_fusion
  10.9 0.9 broadcast_in_dim.14
  11.8 16.7 %all-to-all-start = ((bf16[32,80,128]{2,1,0:T(8,128)(2,1)}), bf16[32,80,128]{2,1,0:T(8,128)(2,1)S(1)}, u32[]{:S(2)}, u32[]{:S(2)}) async-start(bf16[32,80,128]{2,1,0:T(8,128)(2,1)} %bitcast.7), calls=%async_computation | async-start | bytes 1310720 | tf_op jit(solution)/shard_map/all_to_all | solution.py:160
  29.3 2.1 collective-permute-start
  31.5 36.6 %all-to-all-done = bf16[32,80,128]{2,1,0:T(8,128)(2,1)S(1)} async-done(((bf16[32,80,128]{2,1,0:T(8,128)(2,1)}), bf16[32,80,128]{2,1,0:T(8,128)(2,1)S(1)}, u32[]{:S(2)}, u32[]{:S(2)}) %all-to-all-start) | async-done | bytes 655392 | tf_op jit(solution)/shard_map/all_to_all | solution.py:160
  68.1 1.6 broadcast_in_dim.16
  69.8 4.3 %all-to-all-start.1 = ((bf16[4,2048,128]{2,1,0:T(8,128)(2,1)}), bf16[4,2048,128]{2,1,0:T(8,128)(2,1)S(1)}, u32[]{:S(2)}, u32[]{:S(2)}) async-start(bf16[4,2048,128]{2,1,0:T(8,128)(2,1)} %broadcast_in_dim.16), calls=%async_computation.1 | async-start | bytes 4194304 | tf_op jit(solution)/shard_map/all_to_all | solution.py:160
  74.4 24.8 %all-to-all-done.1.weight_ref = bf16[4,2048,128]{2,1,0:T(8,128)(2,1)S(1)} async-done(((bf16[4,2048,128]{2,1,0:T(8,128)(2,1)}), bf16[4,2048,128]{2,1,0:T(8,128)(2,1)S(1)}, u32[]{:S(2)}, u32[]{:S(2)}) %all-to-all-start.1) | async-done | bytes 2097184 | tf_op jit(solution)/shard_map/all_to_all | solution.py:160
  99.2 5.0 %shard_map.120.refs_1_ = bf16[1024,512]{1,0:T(8,128)(2,1)S(1)} custom-call(bf16[512,2048]{1,0:T(8,128)(2,1)} %bitcast.1.own_ref, bf16[512,2048]{1,0:T(8,128)(2,1)} %collective-permute-done.other_ref, bf16[4,2048,128]{2,1,0:T(8,128)(2,1)S(1)} %all-to-all-done.1.weight_ref), custom_call_target="tpu_custom_call" | custom-call | flops 2147483648 | bytes 8388608 | tf_op jit(solution)/shard_map/pallas_call | solution.py:48
  104.2 3.4 %all-gather.2.cloned.1.call-done.refs_2_.refs_3_ = bf16[1024,1024]{1,0:T(8,128)(2,1)} async-done(((bf16[32,1024]{1,0:T(8,128)(2,1)}), bf16[1024,1024]{1,0:T(8,128)(2,1)}) %all-gather.2.cloned.1.call-update) | async-done | bytes 2097168 | tf_op jit(solution)/shard_map/all_gather | solution.py:192
  107.6 1.6 copy-done
  109.2 6.7 %shard_map.121 = (bf16[512,512]{1,0:T(8,128)(2,1)S(1)}, bf16[512,512]{1,0:T(8,128)(2,1)S(1)}, bf16[4,256,256]{2,1,0:T(8,128)(2,1)S(1)}) custom-call(s32[1]{0:T(128)} %bitcast.refs_0_, bf16[1024,512]{1,0:T(8,128)(2,1)S(1)} %shard_map.120.refs_1_, bf16[1024,1024]{1,0:T(8,128)(2,1)S(1)} %copy-done, bf16[1024,1024]{1,0:T(8,128)(2,1)S(1)} %copy-done, ...), custom_call_target="tpu_custom_call" | custom-call | flops 2684354560 | bytes 6291456 | tf_op jit(solution)/shard_map/pallas_call | solution.py:123
  115.9 18.3 %all_to_all.30 = bf16[4,256,256]{2,1,0:T(8,128)(2,1)S(1)} all-to-all(bf16[4,256,256]{2,1,0:T(8,128)(2,1)S(1)} %get-tuple-element.9), channel_id=1, replica_groups=mesh['zh'=4,'zl'=4,'core'=2,'tensor'=4,'dp'=4] {'zl'}, dimensions={0} | all-to-all | bytes 1048576 | tf_op jit(solution)/shard_map/all_to_all | solution.py:160
  134.3 0.8 broadcast_in_dim.34
  135.1 6.4 %all-to-all-start.3 = ((bf16[4,256,256]{2,1,0:T(8,128)(2,1)}), bf16[4,256,256]{2,1,0:T(8,128)(2,1)S(1)}, u32[]{:S(2)}, u32[]{:S(2)}) async-start(bf16[4,256,256]{2,1,0:T(8,128)(2,1)} %broadcast_in_dim.34), calls=%async_computation.3 | async-start | bytes 1048576 | tf_op jit(solution)/shard_map/all_to_all | solution.py:160
  141.7 3.6 %collective-permute-start.1 = (bf16[512,512]{1,0:T(8,128)(2,1)S(1)}, bf16[512,512]{1,0:T(8,128)(2,1)S(1)}, u32[]{:S(2)}, u32[]{:S(2)}) collective-permute-start(bf16[512,512]{1,0:T(8,128)(2,1)S(1)} %get-tuple-element.8), channel_id=1, source_target_pairs={{0,16},{16,0},{1,17},{17,1},{2,18},{18,2},{3,19},{19,3},{4,20},{20... | collective-permute-start | bytes 1572872 | tf_op jit(solution)/shard_map/ppermute | solution.py:233
  145.3 1.9 collective-permute-start.2
  147.2 1.3 collective-permute-done.2
  148.7 1.2 maximum_select_fusion
  149.9 20.0 %all-to-all-done.3 = bf16[4,256,256]{2,1,0:T(8,128)(2,1)S(1)} async-done(((bf16[4,256,256]{2,1,0:T(8,128)(2,1)}), bf16[4,256,256]{2,1,0:T(8,128)(2,1)S(1)}, u32[]{:S(2)}, u32[]{:S(2)}) %all-to-all-start.3) | async-done | bytes 524320 | tf_op jit(solution)/shard_map/all_to_all | solution.py:160
  170.0 13.4 %all_gather.7 = bf16[256,1024]{1,0:T(8,128)(2,1)S(1)} all-gather(bf16[256,256]{1,0:T(8,128)(2,1)S(1)} %reduce_sum.56), channel_id=1, replica_groups=mesh['zh'=4,'zl'=4,'core'=2,'tensor'=4,'dp'=4] {'zl'}, dimensions={1}, use_global_device_ids=true | all-gather | bytes 655360 | tf_op jit(solution)/shard_map/all_gather | solution.py:244
  183.7 0.7 broadcast_in_dim.37
  184.4 9.5 %all-to-all-start.5 = ((bf16[8,64,256]{2,1,0:T(8,128)(2,1)}), bf16[8,64,256]{2,1,0:T(8,128)(2,1)S(1)}, u32[]{:S(2)}, u32[]{:S(2)}) async-start(bf16[8,64,256]{2,1,0:T(8,128)(2,1)} %bitcast.26), calls=%async_computation.5 | async-start | bytes 524288 | tf_op jit(solution)/shard_map/all_to_all | solution.py:160
  194.3 0.7 copy.59
  195.0 5.4 %all-to-all-done.5 = bf16[8,64,256]{2,1,0:T(8,128)(2,1)S(1)} async-done(((bf16[8,64,256]{2,1,0:T(8,128)(2,1)}), bf16[8,64,256]{2,1,0:T(8,128)(2,1)S(1)}, u32[]{:S(2)}, u32[]{:S(2)}) %all-to-all-start.5) | async-done | bytes 262176 | tf_op jit(solution)/shard_map/all_to_all | solution.py:160
  200.4 4.7 %all-to-all-start.4 = ((bf16[8,64,256]{2,1,0:T(8,128)(2,1)}), bf16[8,64,256]{2,1,0:T(8,128)(2,1)S(1)}, u32[]{:S(2)}, u32[]{:S(2)}) async-start(bf16[8,64,256]{2,1,0:T(8,128)(2,1)} %bitcast.21), calls=%async_computation.4 | async-start | bytes 524288 | tf_op jit(solution)/shard_map/all_to_all | solution.py:160
  205.2 0.7 copy.67
  205.9 5.8 %all-to-all-done.4 = bf16[8,64,256]{2,1,0:T(8,128)(2,1)S(1)} async-done(((bf16[8,64,256]{2,1,0:T(8,128)(2,1)}), bf16[8,64,256]{2,1,0:T(8,128)(2,1)S(1)}, u32[]{:S(2)}, u32[]{:S(2)}) %all-to-all-start.4) | async-done | bytes 262176 | tf_op jit(solution)/shard_map/all_to_all | solution.py:160
  211.7 0.7 reduce_sum.57
  (49 shorter events, 2.7 us)
Async XLA Ops:
  7.2 21.5 %copy-start.3 = (bf16[1,32,512]{2,1,0:T(8,128)(2,1)S(1)}, bf16[1,32,512]{2,1,0:T(8,128)(2,1)}, u32[]{:S(2)}) copy-start(bf16[1,32,512]{2,1,0:T(8,128)(2,1)} %param.14) | copy-start | bytes 98308
  7.2 21.5 %copy-start.5 = (bf16[1,32,512]{2,1,0:T(8,128)(2,1)S(1)}, bf16[1,32,512]{2,1,0:T(8,128)(2,1)}, u32[]{:S(2)}) copy-start(bf16[1,32,512]{2,1,0:T(8,128)(2,1)} %param.13) | copy-start | bytes 98308
  11.8 56.2 %all-to-all-start = ((bf16[32,80,128]{2,1,0:T(8,128)(2,1)}), bf16[32,80,128]{2,1,0:T(8,128)(2,1)S(1)}, u32[]{:S(2)}, u32[]{:S(2)}) async-start(bf16[32,80,128]{2,1,0:T(8,128)(2,1)} %bitcast.7), calls=%async_computation | async-start | bytes 1310720 | tf_op jit(solution)/shard_map/all_to_all | solution.py:160
  28.6 79.0 %all-gather.2.cloned.1.call-start = ((), (), s32[]{:S(2)}) async-start(), calls=%async_computation.6 | async-start | bytes 2162688 | tf_op jit(solution)/shard_map/all_gather | solution.py:192
  29.3 45.1 %collective-permute-start = (bf16[512,2048]{1,0:T(8,128)(2,1)}, bf16[512,2048]{1,0:T(8,128)(2,1)}, u32[]{:S(2)}, u32[]{:S(2)}) collective-permute-start(bf16[512,2048]{1,0:T(8,128)(2,1)} %bitcast.1.own_ref), channel_id=1, source_target_pairs={{0,16},{16,0},{1,17},{17,1},{2,18},{18,2},{3,19},{19,3},{4,20},{20... | collective-permute-start | bytes 6291464 | tf_op jit(solution)/shard_map/ppermute | solution.py:195
  69.8 29.5 %all-to-all-start.1 = ((bf16[4,2048,128]{2,1,0:T(8,128)(2,1)}), bf16[4,2048,128]{2,1,0:T(8,128)(2,1)S(1)}, u32[]{:S(2)}, u32[]{:S(2)}) async-start(bf16[4,2048,128]{2,1,0:T(8,128)(2,1)} %broadcast_in_dim.16), calls=%async_computation.1 | async-start | bytes 4194304 | tf_op jit(solution)/shard_map/all_to_all | solution.py:160
  107.6 1.6 copy-start
  115.9 25.6 %copy-start.4 = (bf16[64,512]{1,0:T(8,128)(2,1)S(1)}, bf16[64,512]{1,0:T(8,128)(2,1)}, u32[]{:S(2)}) copy-start(bf16[64,512]{1,0:T(8,128)(2,1)} %param.12) | copy-start | bytes 196612
  115.9 29.4 %copy-start.2 = (bf16[1,1024,64]{1,2,0:T(8,128)(2,1)S(1)}, bf16[1,1024,64]{1,2,0:T(8,128)(2,1)}, u32[]{:S(2)}) copy-start(bf16[1,1024,64]{1,2,0:T(8,128)(2,1)} %param.17) | copy-start | bytes 393220
  135.1 34.8 %all-to-all-start.3 = ((bf16[4,256,256]{2,1,0:T(8,128)(2,1)}), bf16[4,256,256]{2,1,0:T(8,128)(2,1)S(1)}, u32[]{:S(2)}, u32[]{:S(2)}) async-start(bf16[4,256,256]{2,1,0:T(8,128)(2,1)} %broadcast_in_dim.34), calls=%async_computation.3 | async-start | bytes 1048576 | tf_op jit(solution)/shard_map/all_to_all | solution.py:160
  141.7 7.0 %collective-permute-start.1 = (bf16[512,512]{1,0:T(8,128)(2,1)S(1)}, bf16[512,512]{1,0:T(8,128)(2,1)S(1)}, u32[]{:S(2)}, u32[]{:S(2)}) collective-permute-start(bf16[512,512]{1,0:T(8,128)(2,1)S(1)} %get-tuple-element.8), channel_id=1, source_target_pairs={{0,16},{16,0},{1,17},{17,1},{2,18},{18,2},{3,19},{19,3},{4,20},{20... | collective-permute-start | bytes 1572872 | tf_op jit(solution)/shard_map/ppermute | solution.py:233
  145.3 3.3 %collective-permute-start.2 = (bf16[64,1280]{1,0:T(8,128)(2,1)S(1)}, bf16[64,1280]{1,0:T(8,128)(2,1)S(1)}, u32[]{:S(2)}, u32[]{:S(2)}) collective-permute-start(bf16[64,1280]{1,0:T(8,128)(2,1)S(1)} %pad_maximum_fusion), channel_id=1, source_target_pairs={{0,16},{16,0},{1,17},{17,1},{2,18},{18,2},{3,19},{19,3},{4,20},{20... | collective-permute-start | bytes 491528 | tf_op jit(solution)/shard_map/ppermute | solution.py:200
  148.6 1.3 copy-start.1
  169.9 24.0 %slice-start = ((bf16[64,1280]{1,0:T(8,128)(2,1)}), bf16[64,256]{1,0:T(8,128)(2,1)S(1)}, s32[]{:S(2)}) async-start(bf16[64,1280]{1,0:T(8,128)(2,1)} %copy-done.1), calls=%async_computation.7 | async-start | bytes 65536 | tf_op jit(solution)/shard_map/slice | solution.py:201
  184.4 16.1 %all-to-all-start.5 = ((bf16[8,64,256]{2,1,0:T(8,128)(2,1)}), bf16[8,64,256]{2,1,0:T(8,128)(2,1)S(1)}, u32[]{:S(2)}, u32[]{:S(2)}) async-start(bf16[8,64,256]{2,1,0:T(8,128)(2,1)} %bitcast.26), calls=%async_computation.5 | async-start | bytes 524288 | tf_op jit(solution)/shard_map/all_to_all | solution.py:160
  200.4 11.3 %all-to-all-start.4 = ((bf16[8,64,256]{2,1,0:T(8,128)(2,1)}), bf16[8,64,256]{2,1,0:T(8,128)(2,1)S(1)}, u32[]{:S(2)}, u32[]{:S(2)}) async-start(bf16[8,64,256]{2,1,0:T(8,128)(2,1)} %bitcast.21), calls=%async_computation.4 | async-start | bytes 524288 | tf_op jit(solution)/shard_map/all_to_all | solution.py:160
Sparse Core Ops, SparseCore 0:
  32.1 75.4 all-gather.1

commit v2 on v1

--- a/solution.py
+++ b/solution.py
@@ -21,45 +21,55 @@
     return lax.dot_general(a, b, (((1,), (1,)), ((), ())), preferred_element_type=F32)
 
 
-def project_kernel(own_ref, other_ref, weight_ref, out_ref):
+def project_kernel(batch_ref, own_ref, other_ref, *refs):
+    slabs, out_ref, weight = refs[:-2], refs[-2], refs[-1]
     step = pl.program_id(0)
     half = pl.num_programs(0) // 2
-    size = weight_ref.shape[2]
-
-    def run(rows):
-        for pair in range(2):
-            weight = jnp.concatenate([weight_ref[2 * pair], weight_ref[2 * pair + 1]], axis=1)
-            out_ref[:, 2 * pair * size : 2 * (pair + 1) * size] = dot(rows, weight).astype(BF)
+    near, far, rows, size = slabs[0].shape
+
+    @pl.when(step == 0)
+    def _():
+        for shift, slab in enumerate(slabs):
+            source = lax.rem(batch_ref[0] + len(slabs) - shift, len(slabs))
+            cols = pl.ds(pl.multiple_of(source * size, size), size)
+            for zl in range(near):
+                for zh in range(far):
+                    first = (zh * near + zl) * rows
+                    weight[first : first + rows, cols] = slab[zl, zh]
 
     @pl.when(step < half)
     def _():
-        run(own_ref[...])
+        out_ref[...] = dot(own_ref[...], weight[...]).astype(BF)
 
     @pl.when(step >= half)
     def _():
-        run(other_ref[...])
-
-
-def project(own, other, weight):
+        out_ref[...] = dot(other_ref[...], weight[...]).astype(BF)
+
+
+def project(batch, own, other, slabs):
     rows, width = own.shape
-    slabs, _, size = weight.shape
+    size = slabs[0].shape[-1]
+    columns = len(slabs) * size
     block = 256
     half = rows // block
+    whole = pl.BlockSpec(slabs[0].shape, lambda t, b: (0, 0, 0, 0))
     return pl.pallas_call(
         project_kernel,
-        grid=(2 * half,),
-        in_specs=[
-            pl.BlockSpec((block, width), lambda t: (jnp.minimum(t, half - 1), 0)),
-            pl.BlockSpec((block, width), lambda t: (jnp.maximum(t - half, 0), 0)),
-            pl.BlockSpec((slabs, width, size), lambda t: (0, 0, 0)),
-        ],
-        out_specs=pl.BlockSpec((block, slabs * size), lambda t: (t, 0)),
-        out_shape=jax.ShapeDtypeStruct((2 * rows, slabs * size), BF),
-        compiler_params=pltpu.CompilerParams(vmem_limit_bytes=40 * 2**20),
-        cost_estimate=pl.CostEstimate(
-            flops=4 * rows * width * slabs * size, bytes_accessed=8 * 2**20, transcendentals=0
-        ),
-    )(own, other, weight)
+        grid_spec=pltpu.PrefetchScalarGridSpec(
+            num_scalar_prefetch=1,
+            grid=(2 * half,),
+            in_specs=[
+                pl.BlockSpec((block, width), lambda t, b: (jnp.minimum(t, half - 1), 0)),
+                pl.BlockSpec((block, width), lambda t, b: (jnp.maximum(t - half, 0), 0)),
+            ]
+            + [whole] * len(slabs),
+            out_specs=pl.BlockSpec((block, columns), lambda t, b: (t, 0)),
+            scratch_shapes=[pltpu.VMEM((width, columns), BF)],
+        ),
+        out_shape=jax.ShapeDtypeStruct((2 * rows, columns), BF),
+        compiler_params=pltpu.CompilerParams(vmem_limit_bytes=56 * 2**20),
+        cost_estimate=pl.CostEstimate(flops=0, bytes_accessed=2**20, transcendentals=0),
+    )(batch, own, other, *slabs)
 
 
 def attend_kernel(
@@ -147,7 +157,7 @@
             jax.ShapeDtypeStruct((tokens // 2, columns), BF),
             jax.ShapeDtypeStruct((groups, 2 * size, latents // groups), BF),
         ],
-        compiler_params=pltpu.CompilerParams(vmem_limit_bytes=48 * 2**20),
+        compiler_params=pltpu.CompilerParams(vmem_limit_bytes=56 * 2**20),
         cost_estimate=pl.CostEstimate(
             flops=20 * tokens * latents * size,
             bytes_accessed=6 * 2**20,
@@ -214,18 +224,28 @@
     packed = jnp.transpose(jnp.stack([high, low]), (3, 1, 0, 4, 2))
     packed = packed.reshape(2, 2, 2 * (heads // 2) * rows)
     packed = jnp.pad(packed, ((0, 0), (0, 14), (0, 0)))
-    slabs = jnp.concatenate([halves(key_weight), halves(value_weight)], axis=2)
-    slab = lax.dynamic_slice_in_dim(slabs, batch * size, size, 2)
+    source = jnp.where(batch < batches // 2, key_weight, value_weight)
+    column = lax.rem(batch, batches // 2) * size
+    slab = jnp.stack(
+        [lax.dynamic_slice_in_dim(source, c * (columns // 2) + column, size, 1) for c in range(2)]
+    )
     block = jnp.concatenate([slab, packed], axis=1)
-    block = jnp.broadcast_to(block[None], (ranks // 2,) + block.shape).reshape((ranks,) + block.shape[1:])
-    landed = exchange(block, SEQ)
+    far = lax.axis_size("zh")
+    near = lax.axis_size("zl")
+    block = jnp.broadcast_to(block[None], (far,) + block.shape).reshape((-1,) + block.shape[1:])
+    landed = lax.all_gather(exchange(block, ("zh", "core")), "zl", axis=0, tiled=True)
     depth = key_weight.shape[0]
-    weight = spread(landed[:, :depth].reshape(depth * ranks, size), "dp")
-    stats_all = landed[:, depth : depth + 2].astype(F32).reshape(ranks, 2, 2, heads // 2, rows)
-    stats_all = jnp.transpose(stats_all[:, :, 0] + stats_all[:, :, 1], (2, 1, 0, 3))
-    stats_all = stats_all.reshape(heads, latents)
-
-    kv = project(tokens_in, other_tokens, weight)
+    first_slab = landed[:, :depth].reshape(near, far, 2 * depth, size)
+    arrived = [first_slab] + [
+        lax.ppermute(first_slab, "dp", [(i, (i + d) % batches) for i in range(batches)])
+        for d in range(1, batches)
+    ]
+    stats_all = landed[:, depth : depth + 2].astype(F32)
+    stats_all = stats_all.reshape(near, far, 2, 2, 2, heads // 2, rows)
+    stats_all = stats_all[:, :, :, :, 0] + stats_all[:, :, :, :, 1]
+    stats_all = jnp.transpose(stats_all, (4, 3, 1, 0, 2, 5)).reshape(heads, latents)
+
+    kv = project(batch.reshape(1).astype(jnp.int32), tokens_in, other_tokens, arrived)
     groups = lax.axis_size("zl")
     own_grads, other_grads, part = attend(
         jnp.reshape(core, (1,)).astype(jnp.int32), kv, gathered, stats_all, groups, token_count * ranks

time: 220 us -> 212 us (0.964)
  waiting for transfers between devices: 97.4 us -> 49.1 us
  blocking collectives: 31.7 us -> 74.1 us
  Pallas kernels: 11.7 us -> 15.8 us
  starting transfers between devices: 49.3 us -> 45.3 us
  local copies, waits for them, and re-layouts: 9.65 us -> 5.81 us
    all_to_all x5 -> x3, waiting for transfers between devices: 92.6 us -> 30.7 us  [exchange(): return lax.all_to_all(x, axes, 0, 0, tiled=True)]
    all_to_all x1 -> x2, blocking collectives: 18.3 us -> 40.9 us  [exchange(): return lax.all_to_all(x, axes, 0, 0, tiled=True)]
    all_to_all x5 -> x3, starting transfers between devices: 41.6 us -> 19.8 us  [exchange(): return lax.all_to_all(x, axes, 0, 0, tiled=True)]
    all_gather x0 -> x1, blocking collectives: none -> 20.4 us  [local(): lax.all_gather(exchange(block, ('zh', 'core')), 'zl', axis=0, tiled=True)]
    ppermute x0 -> x3, waiting for transfers between devices: none -> 17 us  [local(): lax.ppermute(first_slab, 'dp', [(i, (i + d) % batches) for i in range(bat...]
    ppermute x0 -> x3, starting transfers between devices: none -> 11 us  [local(): lax.ppermute(first_slab, 'dp', [(i, (i + d) % batches) for i in range(bat...]
    ppermute x1, starting transfers between devices: 2.15 us -> 8.79 us  [local(): other_tokens = lax.ppermute(tokens_in, 'core', SWAP)]
    all_gather x1, waiting for transfers between devices: 3.36 us -> 0.01 us  [local(): lax.all_gather(jnp.concatenate([queries[0], out_grad[0]], axis=1), SEQ, a...]
  transfers between devices with their start and end apart: 9 -> 10, of which waited for: 7 -> 7; matrix products, arithmetic and copies ran while one was open for 3% -> 3% of each run, Pallas kernels for 2% -> 3%
where the time goes in v2:
time: 212 us; the launch traced here: 211 us
  blocking collectives  74.1 us (35%)
  waiting for transfers between devices  49.1 us (23%)
  starting transfers between devices  45.3 us (21%)
  Pallas kernels  15.8 us (7%)
  between operations  14.4 us (7%)
  other arithmetic  6.17 us (3%)
  local copies, waits for them, and re-layouts  5.81 us (3%)
    all_to_all x2, blocking collectives, exchange(): return lax.all_to_all(x, axes, 0, 0, tiled=True)  40.9 us
    all_to_all x3, waiting for transfers between devices, exchange(): return lax.all_to_all(x, axes, 0, 0, tiled=True)  30.7 us
    all_gather x1, blocking collectives, local(): lax.all_gather(exchange(block, ('zh', 'core')), 'zl', axis=0, tiled=True)  20.4 us
    all_to_all x3, starting transfers between devices, exchange(): return lax.all_to_all(x, axes, 0, 0, tiled=True)  19.8 us
    ppermute x3, waiting for transfers between devices, local(): lax.ppermute(first_slab, 'dp', [(i, (i + d) % batches) for i in range(bat...  17 us
    all_gather x1, blocking collectives, local(): every = lax.all_gather(full, 'zl', axis=1, tiled=True)  12.8 us
    ppermute x3, starting transfers between devices, local(): lax.ppermute(first_slab, 'dp', [(i, (i + d) % batches) for i in range(bat...  11 us
    pallas_call x1, Pallas kernels, attend(): pl.pallas_call(kernel, grid_spec=pltpu.PrefetchScalarGridSpec(num_scalar_...  9 us
  transfers between devices with their start and end apart: 10, of which 7 were waited for; matrix products, arithmetic and copies ran while one was open for 3% of the time, Pallas kernels for 3%

profile of v2, /device:TPU:1, one launch (start us, length us, event | category | flops | bytes accessed | tf_op | source)
XLA Modules:
  0.0 211.2 jit_solution(10332408607278864057)
XLA Ops:
  7.2 1.4 pad_maximum_fusion.1
  8.6 8.8 %collective-permute-start = (bf16[512,2048]{1,0:T(8,128)(2,1)}, bf16[512,2048]{1,0:T(8,128)(2,1)S(1)}, u32[]{:S(2)}, u32[]{:S(2)}) collective-permute-start(bf16[512,2048]{1,0:T(8,128)(2,1)} %bitcast.56), channel_id=1, source_target_pairs={{0,16},{16,0},{1,17},{17,1},{2,18},{18,2},{3,19},{19,3},{4,20},{20... | collective-permute-start | bytes 6291464 | tf_op jit(solution)/shard_map/ppermute | solution.py:205
  17.4 0.8 convert_multiply_fusion
  18.5 0.7 reduce-precision_convert_fusion
  19.3 0.9 broadcast_select_fusion.2
  20.2 22.9 %all_to_all.25 = bf16[8,80,128]{2,1,0:T(8,128)(2,1)S(1)} all-to-all(bf16[8,80,128]{2,1,0:T(8,128)(2,1)S(1)} %bitcast.62), channel_id=1, replica_groups=mesh['zh'=4,'zl'=4,'core'=2,'tensor'=4,'dp'=4] {'zh','core'}, dimensions={0} | all-to-all | bytes 327680 | tf_op jit(solution)/shard_map/all_to_all | solution.py:170
  43.1 20.4 %all_gather.9 = bf16[32,80,128]{2,1,0:T(8,128)(2,1)S(1)} all-gather(bf16[8,80,128]{2,1,0:T(8,128)(2,1)S(1)} %all_to_all.25), channel_id=1, replica_groups=mesh['zh'=4,'zl'=4,'core'=2,'tensor'=4,'dp'=4] {'zl'}, dimensions={0}, use_global_device_ids=true | all-gather | bytes 819200 | tf_op jit(solution)/shard_map/all_gather | solution.py:236
  63.5 3.5 %collective-permute-start.1 = (bf16[4,4,128,128]{3,2,1,0:T(8,128)(2,1)S(1)}, bf16[4,4,128,128]{3,2,1,0:T(8,128)(2,1)}, u32[]{:S(2)}, u32[]{:S(2)}) collective-permute-start(bf16[4,4,128,128]{3,2,1,0:T(8,128)(2,1)S(1)} %bitcast.58), channel_id=1, source_target_pairs={{0,1},{1,2},{2,3},{3,0},{4,5},{5,6},{6,7},{7,4},{8,9},{9,10},{10,1... | collective-permute-start | bytes 1572872 | tf_op jit(solution)/shard_map/ppermute | solution.py:240
  67.1 4.3 %collective-permute-start.2 = (bf16[4,4,128,128]{3,2,1,0:T(8,128)(2,1)S(1)}, bf16[4,4,128,128]{3,2,1,0:T(8,128)(2,1)}, u32[]{:S(2)}, u32[]{:S(2)}) collective-permute-start(bf16[4,4,128,128]{3,2,1,0:T(8,128)(2,1)S(1)} %bitcast.59), channel_id=1, source_target_pairs={{0,2},{1,3},{2,0},{3,1},{4,6},{5,7},{6,4},{7,5},{8,10},{9,11},{10,... | collective-permute-start | bytes 1572872 | tf_op jit(solution)/shard_map/ppermute | solution.py:240
  71.4 3.2 %collective-permute-start.3 = (bf16[4,4,128,128]{3,2,1,0:T(8,128)(2,1)S(1)}, bf16[4,4,128,128]{3,2,1,0:T(8,128)(2,1)}, u32[]{:S(2)}, u32[]{:S(2)}) collective-permute-start(bf16[4,4,128,128]{3,2,1,0:T(8,128)(2,1)S(1)} %bitcast.60), channel_id=1, source_target_pairs={{0,3},{1,0},{2,1},{3,2},{4,7},{5,4},{6,5},{7,6},{8,11},{9,8},{10,9... | collective-permute-start | bytes 1572872 | tf_op jit(solution)/shard_map/ppermute | solution.py:240
  74.9 0.7 reshape.266.refs_4_
  75.6 1.4 collective-permute-done.1.refs_1_
  77.0 12.4 %collective-permute-done.2.refs_2_ = bf16[4,4,128,128]{3,2,1,0:T(8,128)(2,1)} collective-permute-done((bf16[4,4,128,128]{3,2,1,0:T(8,128)(2,1)S(1)}, bf16[4,4,128,128]{3,2,1,0:T(8,128)(2,1)}, u32[]{:S(2)}, u32[]{:S(2)}) %collective-permute-start.2) | collective-permute-done | bytes 524320 | tf_op jit(solution)/shard_map/ppermute | solution.py:240
  89.4 3.3 %collective-permute-done.3.refs_3_ = bf16[4,4,128,128]{3,2,1,0:T(8,128)(2,1)} collective-permute-done((bf16[4,4,128,128]{3,2,1,0:T(8,128)(2,1)S(1)}, bf16[4,4,128,128]{3,2,1,0:T(8,128)(2,1)}, u32[]{:S(2)}, u32[]{:S(2)}) %collective-permute-start.3) | collective-permute-done | bytes 524320 | tf_op jit(solution)/shard_map/ppermute | solution.py:240
  92.6 1.3 copy-done
  94.0 6.8 %shard_map.120.refs_1_ = bf16[1024,512]{1,0:T(8,128)(2,1)} custom-call(s32[1]{0:T(128)} %bitcast.1.batch_ref, bf16[512,2048]{1,0:T(8,128)(2,1)} %bitcast.57, bf16[512,2048]{1,0:T(8,128)(2,1)} %copy-done, bf16[4,4,128,128]{3,2,1,0:T(8,128)(2,1)} %bitcast.61, bf16[4,4,128,128]{3,2,1,0:T(8,128)(2,1)} %collective-permute-done.1.refs_1_, ...), custom_call_target="tpu_custom_call" | custom-call | bytes 1048576 | tf_op jit(solution)/shard_map/pallas_call | solution.py:56
  100.7 9.0 %shard_map.121 = (bf16[512,512]{1,0:T(8,128)(2,1)}, bf16[512,512]{1,0:T(8,128)(2,1)}, bf16[4,256,256]{2,1,0:T(8,128)(2,1)}) custom-call(s32[1]{0:T(128)} %bitcast.refs_0_, bf16[1024,512]{1,0:T(8,128)(2,1)} %shard_map.120.refs_1_, bf16[1024,1024]{1,0:T(8,128)(2,1)} %all-gather.2.cloned.1.call-done.refs_2_.refs_3_, ...), custom_call_target="tpu_custom_call" | custom-call | flops 2684354560 | bytes 6291456 | tf_op jit(solution)/shard_map/pallas_call | solution.py:133
  109.8 18.0 %all_to_all.26 = bf16[4,256,256]{2,1,0:T(8,128)(2,1)S(1)} all-to-all(bf16[4,256,256]{2,1,0:T(8,128)(2,1)} %get-tuple-element.9), channel_id=1, replica_groups=mesh['zh'=4,'zl'=4,'core'=2,'tensor'=4,'dp'=4] {'zl'}, dimensions={0} | all-to-all | bytes 1048576 | tf_op jit(solution)/shard_map/all_to_all | solution.py:170
  127.9 0.8 broadcast_in_dim.11
  128.7 3.5 %all-to-all-start.2 = ((bf16[4,256,256]{2,1,0:T(8,128)(2,1)}), bf16[4,256,256]{2,1,0:T(8,128)(2,1)S(1)}, u32[]{:S(2)}, u32[]{:S(2)}) async-start(bf16[4,256,256]{2,1,0:T(8,128)(2,1)} %broadcast_in_dim.11), calls=%async_computation.2 | async-start | bytes 1048576 | tf_op jit(solution)/shard_map/all_to_all | solution.py:170
  132.4 3.7 %collective-permute-start.4 = (bf16[512,512]{1,0:T(8,128)(2,1)S(1)}, bf16[512,512]{1,0:T(8,128)(2,1)S(1)}, u32[]{:S(2)}, u32[]{:S(2)}) collective-permute-start(bf16[512,512]{1,0:T(8,128)(2,1)S(1)} %copy-done.6), channel_id=1, source_target_pairs={{0,16},{16,0},{1,17},{17,1},{2,18},{18,2},{3,19},{19,3},{4,20},{20... | collective-permute-start | bytes 1572872 | tf_op jit(solution)/shard_map/ppermute | solution.py:253
  136.2 1.9 collective-permute-start.5
  138.1 1.3 collective-permute-done.5
  139.6 1.2 maximum_select_fusion
  140.8 19.4 %all-to-all-done.2 = bf16[4,256,256]{2,1,0:T(8,128)(2,1)S(1)} async-done(((bf16[4,256,256]{2,1,0:T(8,128)(2,1)}), bf16[4,256,256]{2,1,0:T(8,128)(2,1)S(1)}, u32[]{:S(2)}, u32[]{:S(2)}) %all-to-all-start.2) | async-done | bytes 524320 | tf_op jit(solution)/shard_map/all_to_all | solution.py:170
  160.3 12.8 %all_gather.11 = bf16[256,1024]{1,0:T(8,128)(2,1)S(1)} all-gather(bf16[256,256]{1,0:T(8,128)(2,1)S(1)} %reduce_sum.56), channel_id=1, replica_groups=mesh['zh'=4,'zl'=4,'core'=2,'tensor'=4,'dp'=4] {'zl'}, dimensions={1}, use_global_device_ids=true | all-gather | bytes 655360 | tf_op jit(solution)/shard_map/all_gather | solution.py:264
  173.5 0.7 broadcast_in_dim.28
  174.2 9.4 %all-to-all-start.4 = ((bf16[8,64,256]{2,1,0:T(8,128)(2,1)}), bf16[8,64,256]{2,1,0:T(8,128)(2,1)S(1)}, u32[]{:S(2)}, u32[]{:S(2)}) async-start(bf16[8,64,256]{2,1,0:T(8,128)(2,1)} %bitcast.27), calls=%async_computation.4 | async-start | bytes 524288 | tf_op jit(solution)/shard_map/all_to_all | solution.py:170
  184.0 0.7 copy.48
  184.8 5.4 %all-to-all-done.4 = bf16[8,64,256]{2,1,0:T(8,128)(2,1)S(1)} async-done(((bf16[8,64,256]{2,1,0:T(8,128)(2,1)}), bf16[8,64,256]{2,1,0:T(8,128)(2,1)S(1)}, u32[]{:S(2)}, u32[]{:S(2)}) %all-to-all-start.4) | async-done | bytes 262176 | tf_op jit(solution)/shard_map/all_to_all | solution.py:170
  190.2 6.9 %all-to-all-start.3 = ((bf16[8,64,256]{2,1,0:T(8,128)(2,1)}), bf16[8,64,256]{2,1,0:T(8,128)(2,1)S(1)}, u32[]{:S(2)}, u32[]{:S(2)}) async-start(bf16[8,64,256]{2,1,0:T(8,128)(2,1)} %bitcast.22), calls=%async_computation.3 | async-start | bytes 524288 | tf_op jit(solution)/shard_map/all_to_all | solution.py:170
  197.8 5.8 %all-to-all-done.3 = bf16[8,64,256]{2,1,0:T(8,128)(2,1)S(1)} async-done(((bf16[8,64,256]{2,1,0:T(8,128)(2,1)}), bf16[8,64,256]{2,1,0:T(8,128)(2,1)S(1)}, u32[]{:S(2)}, u32[]{:S(2)}) %all-to-all-start.3) | async-done | bytes 262176 | tf_op jit(solution)/shard_map/all_to_all | solution.py:170
  (52 shorter events, 3.3 us)
Async XLA Ops:
  7.2 93.6 %all-gather.2.cloned.1.call-start = ((), (), s32[]{:S(2)}) async-start(), calls=%async_computation.5 | async-start | bytes 2162688 | tf_op jit(solution)/shard_map/all_gather | solution.py:202
  8.6 84.0 %collective-permute-start = (bf16[512,2048]{1,0:T(8,128)(2,1)}, bf16[512,2048]{1,0:T(8,128)(2,1)S(1)}, u32[]{:S(2)}, u32[]{:S(2)}) collective-permute-start(bf16[512,2048]{1,0:T(8,128)(2,1)} %bitcast.56), channel_id=1, source_target_pairs={{0,16},{16,0},{1,17},{17,1},{2,18},{18,2},{3,19},{19,3},{4,20},{20... | collective-permute-start | bytes 6291464 | tf_op jit(solution)/shard_map/ppermute | solution.py:205
  63.5 29.1 %copy-start.1 = (bf16[32,64,128]{2,1,0:T(8,128)(2,1)}, bf16[32,64,128]{2,1,0:T(8,128)(2,1)S(1)}, u32[]{:S(2)}) copy-start(bf16[32,64,128]{2,1,0:T(8,128)(2,1)S(1)} %slice.50) | copy-start | bytes 1572868
  63.5 13.5 %collective-permute-start.1 = (bf16[4,4,128,128]{3,2,1,0:T(8,128)(2,1)S(1)}, bf16[4,4,128,128]{3,2,1,0:T(8,128)(2,1)}, u32[]{:S(2)}, u32[]{:S(2)}) collective-permute-start(bf16[4,4,128,128]{3,2,1,0:T(8,128)(2,1)S(1)} %bitcast.58), channel_id=1, source_target_pairs={{0,1},{1,2},{2,3},{3,0},{4,5},{5,6},{6,7},{7,4},{8,9},{9,10},{10,1... | collective-permute-start | bytes 1572872 | tf_op jit(solution)/shard_map/ppermute | solution.py:240
  67.1 22.3 %collective-permute-start.2 = (bf16[4,4,128,128]{3,2,1,0:T(8,128)(2,1)S(1)}, bf16[4,4,128,128]{3,2,1,0:T(8,128)(2,1)}, u32[]{:S(2)}, u32[]{:S(2)}) collective-permute-start(bf16[4,4,128,128]{3,2,1,0:T(8,128)(2,1)S(1)} %bitcast.59), channel_id=1, source_target_pairs={{0,2},{1,3},{2,0},{3,1},{4,6},{5,7},{6,4},{7,5},{8,10},{9,11},{10,... | collective-permute-start | bytes 1572872 | tf_op jit(solution)/shard_map/ppermute | solution.py:240
  71.4 21.3 %collective-permute-start.3 = (bf16[4,4,128,128]{3,2,1,0:T(8,128)(2,1)S(1)}, bf16[4,4,128,128]{3,2,1,0:T(8,128)(2,1)}, u32[]{:S(2)}, u32[]{:S(2)}) collective-permute-start(bf16[4,4,128,128]{3,2,1,0:T(8,128)(2,1)S(1)} %bitcast.60), channel_id=1, source_target_pairs={{0,3},{1,0},{2,1},{3,2},{4,7},{5,4},{6,5},{7,6},{8,11},{9,8},{10,9... | collective-permute-start | bytes 1572872 | tf_op jit(solution)/shard_map/ppermute | solution.py:240
  92.6 1.3 copy-start
  109.8 22.5 %copy-start.5 = (bf16[64,512]{1,0:T(8,128)(2,1)S(1)}, bf16[64,512]{1,0:T(8,128)(2,1)}, u32[]{:S(2)}) copy-start(bf16[64,512]{1,0:T(8,128)(2,1)} %param.12) | copy-start | bytes 196612
  109.8 22.7 %copy-start.6 = (bf16[512,512]{1,0:T(8,128)(2,1)S(1)}, bf16[512,512]{1,0:T(8,128)(2,1)}, u32[]{:S(2)}) copy-start(bf16[512,512]{1,0:T(8,128)(2,1)} %get-tuple-element.8) | copy-start | bytes 1572868
  109.8 26.4 %copy-start.4 = (bf16[1,1024,64]{1,2,0:T(8,128)(2,1)S(1)}, bf16[1,1024,64]{1,2,0:T(8,128)(2,1)}, u32[]{:S(2)}) copy-start(bf16[1,1024,64]{1,2,0:T(8,128)(2,1)} %param.17) | copy-start | bytes 393220
  109.8 29.7 %copy-start.2 = (bf16[512,512]{1,0:T(8,128)(2,1)S(1)}, bf16[512,512]{1,0:T(8,128)(2,1)}, u32[]{:S(2)}) copy-start(bf16[512,512]{1,0:T(8,128)(2,1)} %get-tuple-element.7) | copy-start | bytes 1572868
  128.7 31.5 %all-to-all-start.2 = ((bf16[4,256,256]{2,1,0:T(8,128)(2,1)}), bf16[4,256,256]{2,1,0:T(8,128)(2,1)S(1)}, u32[]{:S(2)}, u32[]{:S(2)}) async-start(bf16[4,256,256]{2,1,0:T(8,128)(2,1)} %broadcast_in_dim.11), calls=%async_computation.2 | async-start | bytes 1048576 | tf_op jit(solution)/shard_map/all_to_all | solution.py:170
  132.4 7.1 %collective-permute-start.4 = (bf16[512,512]{1,0:T(8,128)(2,1)S(1)}, bf16[512,512]{1,0:T(8,128)(2,1)S(1)}, u32[]{:S(2)}, u32[]{:S(2)}) collective-permute-start(bf16[512,512]{1,0:T(8,128)(2,1)S(1)} %copy-done.6), channel_id=1, source_target_pairs={{0,16},{16,0},{1,17},{17,1},{2,18},{18,2},{3,19},{19,3},{4,20},{20... | collective-permute-start | bytes 1572872 | tf_op jit(solution)/shard_map/ppermute | solution.py:253
  136.2 3.3 %collective-permute-start.5 = (bf16[64,1280]{1,0:T(8,128)(2,1)S(1)}, bf16[64,1280]{1,0:T(8,128)(2,1)S(1)}, u32[]{:S(2)}, u32[]{:S(2)}) collective-permute-start(bf16[64,1280]{1,0:T(8,128)(2,1)S(1)} %pad_maximum_fusion), channel_id=1, source_target_pairs={{0,16},{16,0},{1,17},{17,1},{2,18},{18,2},{3,19},{19,3},{4,20},{20... | collective-permute-start | bytes 491528 | tf_op jit(solution)/shard_map/ppermute | solution.py:210
  139.5 1.4 copy-start.3
  160.3 23.3 %slice-start = ((bf16[64,1280]{1,0:T(8,128)(2,1)}), bf16[64,256]{1,0:T(8,128)(2,1)S(1)}, s32[]{:S(2)}) async-start(bf16[64,1280]{1,0:T(8,128)(2,1)} %copy-done.3), calls=%async_computation.6 | async-start | bytes 65536 | tf_op jit(solution)/shard_map/slice | solution.py:211
  174.2 16.0 %all-to-all-start.4 = ((bf16[8,64,256]{2,1,0:T(8,128)(2,1)}), bf16[8,64,256]{2,1,0:T(8,128)(2,1)S(1)}, u32[]{:S(2)}, u32[]{:S(2)}) async-start(bf16[8,64,256]{2,1,0:T(8,128)(2,1)} %bitcast.27), calls=%async_computation.4 | async-start | bytes 524288 | tf_op jit(solution)/shard_map/all_to_all | solution.py:170
  190.2 13.5 %all-to-all-start.3 = ((bf16[8,64,256]{2,1,0:T(8,128)(2,1)}), bf16[8,64,256]{2,1,0:T(8,128)(2,1)S(1)}, u32[]{:S(2)}, u32[]{:S(2)}) async-start(bf16[8,64,256]{2,1,0:T(8,128)(2,1)} %bitcast.22), calls=%async_computation.3 | async-start | bytes 524288 | tf_op jit(solution)/shard_map/all_to_all | solution.py:170
Sparse Core Ops, SparseCore 0:
  10.7 80.1 all-gather.1

commit v3 on v2

--- a/solution.py
+++ b/solution.py
@@ -21,21 +21,22 @@
     return lax.dot_general(a, b, (((1,), (1,)), ((), ())), preferred_element_type=F32)
 
 
-def project_kernel(batch_ref, own_ref, other_ref, *refs):
-    slabs, out_ref, weight = refs[:-2], refs[-2], refs[-1]
+def project_kernel(own_ref, other_ref, slab_ref, out_ref, weight):
     step = pl.program_id(0)
     half = pl.num_programs(0) // 2
-    near, far, rows, size = slabs[0].shape
+    near, slabs, far, cores, _, size = slab_ref.shape
+    rows = weight.shape[0] // (near * far * cores)
 
     @pl.when(step == 0)
     def _():
-        for shift, slab in enumerate(slabs):
-            source = lax.rem(batch_ref[0] + len(slabs) - shift, len(slabs))
-            cols = pl.ds(pl.multiple_of(source * size, size), size)
+        for slab in range(slabs):
             for zl in range(near):
                 for zh in range(far):
-                    first = (zh * near + zl) * rows
-                    weight[first : first + rows, cols] = slab[zl, zh]
+                    for core in range(cores):
+                        first = ((zh * near + zl) * cores + core) * rows
+                        weight[first : first + rows, slab * size : (slab + 1) * size] = slab_ref[
+                            zl, slab, zh, core, :rows
+                        ]
 
     @pl.when(step < half)
     def _():
@@ -46,36 +47,32 @@
         out_ref[...] = dot(other_ref[...], weight[...]).astype(BF)
 
 
-def project(batch, own, other, slabs):
+def project(own, other, slabs):
     rows, width = own.shape
-    size = slabs[0].shape[-1]
-    columns = len(slabs) * size
+    columns = slabs.shape[1] * slabs.shape[5]
     block = 256
     half = rows // block
-    whole = pl.BlockSpec(slabs[0].shape, lambda t, b: (0, 0, 0, 0))
     return pl.pallas_call(
         project_kernel,
-        grid_spec=pltpu.PrefetchScalarGridSpec(
-            num_scalar_prefetch=1,
-            grid=(2 * half,),
-            in_specs=[
-                pl.BlockSpec((block, width), lambda t, b: (jnp.minimum(t, half - 1), 0)),
-                pl.BlockSpec((block, width), lambda t, b: (jnp.maximum(t - half, 0), 0)),
-            ]
-            + [whole] * len(slabs),
-            out_specs=pl.BlockSpec((block, columns), lambda t, b: (t, 0)),
-            scratch_shapes=[pltpu.VMEM((width, columns), BF)],
-        ),
+        grid=(2 * half,),
+        in_specs=[
+            pl.BlockSpec((block, width), lambda t: (jnp.minimum(t, half - 1), 0)),
+            pl.BlockSpec((block, width), lambda t: (jnp.maximum(t - half, 0), 0)),
+            pl.BlockSpec(slabs.shape, lambda t: (0, 0, 0, 0, 0, 0)),
+        ],
+        out_specs=pl.BlockSpec((block, columns), lambda t: (t, 0)),
         out_shape=jax.ShapeDtypeStruct((2 * rows, columns), BF),
-        compiler_params=pltpu.CompilerParams(vmem_limit_bytes=56 * 2**20),
+        scratch_shapes=[pltpu.VMEM((width, columns), BF)],
+        compiler_params=pltpu.CompilerParams(vmem_limit_bytes=32 * 2**20),
         cost_estimate=pl.CostEstimate(flops=0, bytes_accessed=2**20, transcendentals=0),
-    )(batch, own, other, *slabs)
+    )(own, other, slabs)
 
 
 def attend_kernel(
-    core_ref, kv_ref, query_ref, grad_ref, stat_ref, own_ref, other_ref, part_ref, qt, gt, total,
-    *, size, scaling, latent_factor, prefix_factor,
+    place_ref, kv_ref, query_ref, grad_ref, stat_ref, own_ref, other_ref, *refs,
+    size, scaling, latent_factor, prefix_factor,
 ):
+    part_refs, (qt, gt, total) = refs[:-3], refs[-3:]
     step = pl.program_id(0)
     last = pl.num_programs(0) - 1
     half = pl.num_programs(0) // 2
@@ -110,14 +107,14 @@
 
     @pl.when(step == last)
     def _():
-        count, _, width = part_ref.shape
-        for i in range(count):
-            part_ref[i] = (
-                total[:, i * width : (i + 1) * width] * (scaling * prefix_factor)
-            ).astype(BF)
-
-
-def attend(core, kv, gathered, stats, groups, prefix_count):
+        for ahead, part_ref in enumerate(part_refs):
+            rows = part_ref.shape[0]
+            block = lax.rem(place_ref[1] + ahead, len(part_refs))
+            part = total[pl.ds(pl.multiple_of(block * rows, rows), rows), :]
+            part_ref[...] = (part * (scaling * prefix_factor)).astype(BF)
+
+
+def attend(place, kv, gathered, stats, near, prefix_count):
     tokens, columns = kv.shape
     latents = gathered.shape[0]
     size = columns // 4
@@ -144,8 +141,8 @@
             out_specs=[
                 pl.BlockSpec((block, columns), lambda t, c: (jnp.minimum(t, half - 1), 0)),
                 pl.BlockSpec((block, columns), lambda t, c: (jnp.maximum(t - half, 0), 0)),
-                pl.BlockSpec((groups, 2 * size, latents // groups), lambda t, c: (0, 0, 0)),
-            ],
+            ]
+            + [pl.BlockSpec((2 * size // near, latents), lambda t, c: (0, 0))] * near,
             scratch_shapes=[
                 pltpu.VMEM((2 * size, latents), BF),
                 pltpu.VMEM((2 * size, latents), BF),
@@ -155,24 +152,53 @@
         out_shape=[
             jax.ShapeDtypeStruct((tokens // 2, columns), BF),
             jax.ShapeDtypeStruct((tokens // 2, columns), BF),
-            jax.ShapeDtypeStruct((groups, 2 * size, latents // groups), BF),
-        ],
-        compiler_params=pltpu.CompilerParams(vmem_limit_bytes=56 * 2**20),
+        ]
+        + [jax.ShapeDtypeStruct((2 * size // near, latents), BF)] * near,
+        compiler_params=pltpu.CompilerParams(vmem_limit_bytes=32 * 2**20),
         cost_estimate=pl.CostEstimate(
             flops=20 * tokens * latents * size,
             bytes_accessed=6 * 2**20,
             transcendentals=2 * tokens * latents,
         ),
-    )(core, kv, gathered, gathered, stats)
+    )(place, kv, gathered, gathered, stats)
+
+
+def tail_kernel(place_ref, query_ref, latent_ref, *refs):
+    blocks, (latent_out, weight_out, every) = refs[:-3], refs[-3:]
+    for ahead, block_ref in enumerate(blocks):
+        rows = block_ref.shape[0]
+        block = lax.rem(place_ref[1] + ahead, len(blocks))
+        every[pl.ds(pl.multiple_of(block * rows, rows), rows), :] = block_ref[...]
+    count, rows, width = latent_out.shape
+    latent = dot(query_ref[...], every[...]).astype(BF)
+    weight = dot_nt(latent_ref[...], every[...]).astype(BF)
+    for i in range(count):
+        core, group = divmod(i, count // 2)
+        latent_out[i] = latent[core * rows : (core + 1) * rows, group * width : (group + 1) * width]
+        weight_out[i] = weight[core * rows : (core + 1) * rows, :]
+
+
+def tail(place, query, latent, blocks, tensors, batches):
+    both, half = query.shape
+    rows = both // 2
+    latents = latent.shape[1]
+    return pl.pallas_call(
+        tail_kernel,
+        in_specs=[pl.BlockSpec(memory_space=pltpu.SMEM)]
+        + [pl.BlockSpec(memory_space=pltpu.VMEM)] * (2 + len(blocks)),
+        out_specs=[pl.BlockSpec(memory_space=pltpu.VMEM)] * 2,
+        out_shape=[
+            jax.ShapeDtypeStruct((2 * tensors, rows, latents // tensors), BF),
+            jax.ShapeDtypeStruct((2 * batches, rows, half), BF),
+        ],
+        scratch_shapes=[pltpu.VMEM((half, latents), BF)],
+        compiler_params=pltpu.CompilerParams(vmem_limit_bytes=32 * 2**20),
+        cost_estimate=pl.CostEstimate(flops=0, bytes_accessed=2**20, transcendentals=0),
+    )(place, query, latent, *blocks)
 
 
 def exchange(x, axes):
     return lax.all_to_all(x, axes, 0, 0, tiled=True)
-
-
-def spread(x, axes):
-    count = lax.axis_size(axes)
-    return exchange(jnp.broadcast_to(x[None], (count,) + x.shape), axes)
 
 
 def halves(x):
@@ -233,22 +259,28 @@
     far = lax.axis_size("zh")
     near = lax.axis_size("zl")
     block = jnp.broadcast_to(block[None], (far,) + block.shape).reshape((-1,) + block.shape[1:])
-    landed = lax.all_gather(exchange(block, ("zh", "core")), "zl", axis=0, tiled=True)
     depth = key_weight.shape[0]
-    first_slab = landed[:, :depth].reshape(near, far, 2 * depth, size)
-    arrived = [first_slab] + [
-        lax.ppermute(first_slab, "dp", [(i, (i + d) % batches) for i in range(batches)])
-        for d in range(1, batches)
-    ]
-    stats_all = landed[:, depth : depth + 2].astype(F32)
-    stats_all = stats_all.reshape(near, far, 2, 2, 2, heads // 2, rows)
+
+    def gather_slabs(carried):
+        landed = exchange(block, ("zh", "core"))
+        wide = jnp.broadcast_to(landed, (near * batches,) + landed.shape)
+        return carried[0] + 1, exchange(wide.reshape((-1,) + landed.shape[1:]), ("zl", "dp"))
+
+    _, spread_out = lax.while_loop(
+        lambda carried: carried[0] < 1,
+        gather_slabs,
+        (jnp.minimum(batch, 0), jnp.zeros((near * batches * block.shape[0],) + block.shape[1:], BF)),
+    )
+    spread_out = spread_out.reshape(near, batches, far, 2, depth + 16, size)
+    stats_all = lax.dynamic_index_in_dim(spread_out, batch, 1, False)[:, :, :, depth : depth + 2]
+    stats_all = stats_all.astype(F32).reshape(near, far, 2, 2, 2, heads // 2, rows)
     stats_all = stats_all[:, :, :, :, 0] + stats_all[:, :, :, :, 1]
     stats_all = jnp.transpose(stats_all, (4, 3, 1, 0, 2, 5)).reshape(heads, latents)
 
-    kv = project(batch.reshape(1).astype(jnp.int32), tokens_in, other_tokens, arrived)
-    groups = lax.axis_size("zl")
-    own_grads, other_grads, part = attend(
-        jnp.reshape(core, (1,)).astype(jnp.int32), kv, gathered, stats_all, groups, token_count * ranks
+    kv = project(tokens_in, other_tokens, spread_out)
+    place = jnp.stack([core, lax.axis_index("zl")]).astype(jnp.int32)
+    own_grads, other_grads, *parts = attend(
+        place, kv, gathered, stats_all, near, token_count * ranks
     )
     theirs = lax.ppermute(other_grads, "core", SWAP)
     half = columns // 2
@@ -259,20 +291,23 @@
             first, jnp.concatenate([mine, other], 1), jnp.concatenate([other, mine], 1)
         )[None]
 
-    near = jnp.sum(exchange(part, "zl").astype(F32), axis=0).astype(BF)
-    full = jnp.sum(spread(near, "zh").astype(F32), axis=0).astype(BF)
-    every = lax.all_gather(full, "zl", axis=1, tiled=True)
-
-    latent_part = dot(query_both, every).astype(BF)
-    latent_part = latent_part.reshape(2, columns // 8, lax.axis_size("tensor"), -1)
-    latent_part = jnp.transpose(latent_part, (0, 2, 1, 3)).reshape(-1, columns // 8, latents // 4)
+    def move(x, distance):
+        return lax.ppermute(x, ("zh", "zl"), [(i, (i + distance) % 16) for i in range(16)])
+
+    def total(*terms):
+        return sum(term.astype(F32) for term in terms).astype(BF)
+
+    window = total(parts[0], move(parts[1], 1), move(parts[2], 2), move(parts[3], -1))
+    full = total(window, move(window, 4), move(window, 8), move(window, -4))
+    blocks = [full, move(full, -1), move(full, 2), move(full, 1)]
+    latent_part, weight_part = tail(
+        place, query_both, latent_both, blocks, lax.axis_size("tensor"), batches
+    )
+
     latent_sum = jnp.sum(exchange(latent_part, ("core", "tensor")).astype(F32), axis=0)
     latent_grad = latent_sum.astype(BF).T[None]
 
-    weight_part = dot_nt(latent_both, every).astype(BF)
-    weight_part = weight_part.reshape(2, 1, columns // 8, half)
-    weight_part = jnp.broadcast_to(weight_part, (2, batches, columns // 8, half))
-    weight_sum = exchange(weight_part.reshape(-1, columns // 8, half), ("core", "dp"))
+    weight_sum = exchange(weight_part, ("core", "dp"))
     weight_sum = jnp.sum(weight_sum.reshape(2, batches, columns // 8, half).astype(F32), axis=1)
     weight_factor = 1.0 / math.sqrt(latents * batches)
     weight_grad = jnp.transpose(weight_sum, (1, 0, 2)).reshape(columns // 8, columns) * weight_factor

time: 212 us -> 237 us (1.12)
  blocking collectives: 74.1 us -> 0 us
  waiting for transfers between devices: 49.1 us -> 98.9 us
  starting transfers between devices: 45.3 us -> 91.3 us
  local copies, waits for them, and re-layouts: 5.81 us -> 9.44 us
    all_to_all x3 -> x4, waiting for transfers between devices: 30.7 us -> 77.6 us  [exchange(): return lax.all_to_all(x, axes, 0, 0, tiled=True)]
    all_to_all x2 -> x0, blocking collectives: 40.9 us -> none  [exchange(): return lax.all_to_all(x, axes, 0, 0, tiled=True)]
    ppermute x3 -> x9, starting transfers between devices: 11 us -> 45.6 us  [move(): lax.ppermute(x, ('zh', 'zl'), [(i, (i + distance) % 16) for i in range(16)])]
    all_gather x2 -> x0, blocking collectives: 33.2 us -> none  [the longest x1 20.4 us: local(): lax.all_gather(exchange(block, ('zh', 'core')), 'zl', axis=0, tiled=True)]
    all_to_all x3 -> x4, starting transfers between devices: 19.8 us -> 29.6 us  [exchange(): return lax.all_to_all(x, axes, 0, 0, tiled=True)]
    ppermute x3 -> x9, waiting for transfers between devices: 17 us -> 21.3 us  [move(): lax.ppermute(x, ('zh', 'zl'), [(i, (i + distance) % 16) for i in range(16)])]
    pallas_call x1 -> x2, Pallas kernels: 6.78 us -> 7.56 us  [the longest x1 5.87 us: project(): pl.pallas_call(project_kernel, grid=(2 * half,), in_specs=[pl.BlockSpec((...]
  transfers between devices with their start and end apart: 10 -> 17, of which waited for: 7 -> 9; matrix products, arithmetic and copies ran while one was open for 3% -> 5% of each run, Pallas kernels for 3% -> 6%
where the time goes in v3:
time: 237 us; the launch traced here: 236 us
  waiting for transfers between devices  98.9 us (42%)
  starting transfers between devices  91.3 us (39%)
  Pallas kernels  15 us (6%)
  between operations  14.4 us (6%)
  local copies, waits for them, and re-layouts  9.44 us (4%)
  other arithmetic  7.08 us (3%)
    all_to_all x4, waiting for transfers between devices, exchange(): return lax.all_to_all(x, axes, 0, 0, tiled=True)  77.6 us
    ppermute x9, starting transfers between devices, move(): lax.ppermute(x, ('zh', 'zl'), [(i, (i + distance) % 16) for i in range(16)])  45.6 us
    all_to_all x4, starting transfers between devices, exchange(): return lax.all_to_all(x, axes, 0, 0, tiled=True)  29.6 us
    ppermute x9, waiting for transfers between devices, move(): lax.ppermute(x, ('zh', 'zl'), [(i, (i + distance) % 16) for i in range(16)])  21.3 us
    ppermute x1, starting transfers between devices, local(): other_tokens = lax.ppermute(tokens_in, 'core', SWAP)  8.79 us
    pallas_call x1, Pallas kernels, attend(): pl.pallas_call(kernel, grid_spec=pltpu.PrefetchScalarGridSpec(num_scalar_...  7.39 us
    pallas_call x1, Pallas kernels, project(): pl.pallas_call(project_kernel, grid=(2 * half,), in_specs=[pl.BlockSpec((...  5.87 us
    ppermute x1, starting transfers between devices, local(): theirs = lax.ppermute(other_grads, 'core', SWAP)  5.28 us
  transfers between devices with their start and end apart: 17, of which 9 were waited for; matrix products, arithmetic and copies ran while one was open for 5% of the time, Pallas kernels for 6%

profile of v3, /device:TPU:1, one launch (start us, length us, event | category | flops | bytes accessed | tf_op | source)
XLA Modules:
  0.0 236.1 jit_solution(17255358469599517836)
XLA Ops:
  7.2 1.4 pad_maximum_fusion.1
  8.6 8.8 %collective-permute-start = (bf16[512,2048]{1,0:T(8,128)(2,1)}, bf16[512,2048]{1,0:T(8,128)(2,1)}, u32[]{:S(2)}, u32[]{:S(2)}) collective-permute-start(bf16[512,2048]{1,0:T(8,128)(2,1)} %bitcast.56), channel_id=1, source_target_pairs={{0,16},{16,0},{1,17},{17,1},{2,18},{18,2},{3,19},{19,3},{4,20},{20... | collective-permute-start | bytes 6291464 | tf_op jit(solution)/shard_map/ppermute | solution.py:231
  20.9 9.8 %all-to-all-start.1 = ((bf16[8,80,128]{2,1,0:T(8,128)(2,1)}), bf16[8,80,128]{2,1,0:T(8,128)(2,1)S(1)}, u32[]{:S(2)}, u32[]{:S(2)}) async-start(bf16[8,80,128]{2,1,0:T(8,128)(2,1)} %bitcast.9), calls=%async_computation.1 | async-start | bytes 327680 | tf_op jit(solution)/shard_map/while/body/all_to_all | solution.py:201
  32.5 1.9 collective-permute-start.2
  34.5 10.3 %all-to-all-done.1 = bf16[8,80,128]{2,1,0:T(8,128)(2,1)S(1)} async-done(((bf16[8,80,128]{2,1,0:T(8,128)(2,1)}), bf16[8,80,128]{2,1,0:T(8,128)(2,1)S(1)}, u32[]{:S(2)}, u32[]{:S(2)}) %all-to-all-start.1) | async-done | bytes 163872 | tf_op jit(solution)/shard_map/while/body/all_to_all | solution.py:201
  44.8 1.9 broadcast_in_dim.19
  46.7 68.3 %while.12 = (s32[]{:T(128)}, bf16[128,80,128]{2,1,0:T(8,128)(2,1)}, bf16[8,80,128]{2,1,0:T(8,128)(2,1)S(1)}, s32[]{:T(128)}) while((s32[]{:T(128)}, bf16[128,80,128]{2,1,0:T(8,128)(2,1)}, bf16[8,80,128]{2,1,0:T(8,128)(2,1)S(1)}, s32[]{:T(128)}) %tuple.35), condition=%wide.region_2.3_spmd, body=%wide.region_1.2_spmd.sunk | while | flops 2 | bytes 10649685 | solution.py:269
  46.7 2.0 broadcast_in_dim.23
  48.7 10.1 %all-to-all-start = ((bf16[128,80,128]{2,1,0:T(8,128)(2,1)}), bf16[128,80,128]{2,1,0:T(8,128)(2,1)}, u32[]{:S(2)}, u32[]{:S(2)}) async-start(bf16[128,80,128]{2,1,0:T(8,128)(2,1)} %bitcast.58), calls=%async_computation | async-start | bytes 5242880 | tf_op jit(solution)/shard_map/while/body/all_to_all | solution.py:201
  58.8 56.2 %all-to-all-done = bf16[128,80,128]{2,1,0:T(8,128)(2,1)} async-done(((bf16[128,80,128]{2,1,0:T(8,128)(2,1)}), bf16[128,80,128]{2,1,0:T(8,128)(2,1)}, u32[]{:S(2)}, u32[]{:S(2)}) %all-to-all-start) | async-done | bytes 2621472 | tf_op jit(solution)/shard_map/while/body/all_to_all | solution.py:201
  116.5 5.9 %shard_map.120.refs_1_ = bf16[1024,512]{1,0:T(8,128)(2,1)S(1)} custom-call(bf16[512,2048]{1,0:T(8,128)(2,1)S(1)} %bitcast.57, bf16[512,2048]{1,0:T(8,128)(2,1)} %collective-permute-done.other_ref, bf16[4,4,4,2,80,128]{5,4,3,2,1,0:T(8,128)(2,1)} %bitcast.10.slab_ref), custom_call_target="tpu_custom_call" | custom-call | bytes 1048576 | tf_op jit(solution)/shard_map/pallas_call | solution.py:55
  122.4 1.6 copy-done.1
  124.0 7.4 %shard_map.121 = (bf16[512,512]{1,0:T(8,128)(2,1)S(1)}, bf16[512,512]{1,0:T(8,128)(2,1)S(1)}, bf16[64,1024]{1,0:T(8,128)(2,1)S(1)}, bf16[64,1024]{1,0:T(8,128)(2...) custom-call(s32[2]{0:T(128)S(1)} %pad_add_fusion.refs_0_.place_ref, ...), custom_call_target="tpu_custom_call" | custom-call | flops 2684354560 | bytes 6291456 | tf_op jit(solution)/shard_map/pallas_call | solution.py:130
  131.4 9.3 %collective-permute-start.3 = (bf16[64,1024]{1,0:T(8,128)(2,1)S(1)}, bf16[64,1024]{1,0:T(8,128)(2,1)S(1)}, u32[]{:S(2)}, u32[]{:S(2)}) collective-permute-start(bf16[64,1024]{1,0:T(8,128)(2,1)S(1)} %get-tuple-element.52), channel_id=1, source_target_pairs={{0,32},{32,64},{64,96},{96,128},{128,160},{160,192},{192,224},{224... | collective-permute-start | bytes 393224 | tf_op jit(solution)/shard_map/ppermute | solution.py:295
  140.7 5.3 %collective-permute-start.4 = (bf16[64,1024]{1,0:T(8,128)(2,1)S(1)}, bf16[64,1024]{1,0:T(8,128)(2,1)S(1)}, u32[]{:S(2)}, u32[]{:S(2)}) collective-permute-start(bf16[64,1024]{1,0:T(8,128)(2,1)S(1)} %get-tuple-element.53), channel_id=1, source_target_pairs={{0,64},{32,96},{64,128},{96,160},{128,192},{160,224},{192,256},{22... | collective-permute-start | bytes 393224 | tf_op jit(solution)/shard_map/ppermute | solution.py:295
  146.0 4.6 %collective-permute-start.5 = (bf16[64,1024]{1,0:T(8,128)(2,1)S(1)}, bf16[64,1024]{1,0:T(8,128)(2,1)S(1)}, u32[]{:S(2)}, u32[]{:S(2)}) collective-permute-start(bf16[64,1024]{1,0:T(8,128)(2,1)S(1)} %get-tuple-element.54), channel_id=1, source_target_pairs={{0,480},{32,0},{64,32},{96,64},{128,96},{160,128},{192,160},{224,1... | collective-permute-start | bytes 393224 | tf_op jit(solution)/shard_map/ppermute | solution.py:295
  150.6 1.9 collective-permute-done.5
  152.6 3.3 %collective-permute-start.6 = (bf16[64,1024]{1,0:T(8,128)(2,1)S(1)}, bf16[64,1024]{1,0:T(8,128)(2,1)S(1)}, u32[]{:S(2)}, u32[]{:S(2)}) collective-permute-start(bf16[64,1024]{1,0:T(8,128)(2,1)S(1)} %add_convert_fusion.1), channel_id=1, source_target_pairs={{0,128},{32,160},{64,192},{96,224},{128,256},{160,288},{192,320},{... | collective-permute-start | bytes 393224 | tf_op jit(solution)/shard_map/ppermute | solution.py:295
  155.9 6.1 %collective-permute-start.7 = (bf16[64,1024]{1,0:T(8,128)(2,1)S(1)}, bf16[64,1024]{1,0:T(8,128)(2,1)S(1)}, u32[]{:S(2)}, u32[]{:S(2)}) collective-permute-start(bf16[64,1024]{1,0:T(8,128)(2,1)S(1)} %add_convert_fusion.1), channel_id=1, source_target_pairs={{0,256},{32,288},{64,320},{96,352},{128,384},{160,416},{192,448},{... | collective-permute-start | bytes 393224 | tf_op jit(solution)/shard_map/ppermute | solution.py:295
  162.0 2.9 %collective-permute-start.8 = (bf16[64,1024]{1,0:T(8,128)(2,1)S(1)}, bf16[64,1024]{1,0:T(8,128)(2,1)S(1)}, u32[]{:S(2)}, u32[]{:S(2)}) collective-permute-start(bf16[64,1024]{1,0:T(8,128)(2,1)S(1)} %add_convert_fusion.1), channel_id=1, source_target_pairs={{0,384},{32,416},{64,448},{96,480},{128,0},{160,32},{192,64},{224,... | collective-permute-start | bytes 393224 | tf_op jit(solution)/shard_map/ppermute | solution.py:295
  165.0 5.3 %collective-permute-start.1 = (bf16[512,512]{1,0:T(8,128)(2,1)S(1)}, bf16[512,512]{1,0:T(8,128)(2,1)S(1)}, u32[]{:S(2)}, u32[]{:S(2)}) collective-permute-start(bf16[512,512]{1,0:T(8,128)(2,1)S(1)} %get-tuple-element.50), channel_id=1, source_target_pairs={{0,16},{16,0},{1,17},{17,1},{2,18},{18,2},{3,19},{19,3},{4,20},{20... | collective-permute-start | bytes 1572872 | tf_op jit(solution)/shard_map/ppermute | solution.py:285
  170.3 11.4 %collective-permute-done.7 = bf16[64,1024]{1,0:T(8,128)(2,1)S(1)} collective-permute-done((bf16[64,1024]{1,0:T(8,128)(2,1)S(1)}, bf16[64,1024]{1,0:T(8,128)(2,1)S(1)}, u32[]{:S(2)}, u32[]{:S(2)}) %collective-permute-start.7) | collective-permute-done | bytes 131104 | tf_op jit(solution)/shard_map/ppermute | solution.py:295
  181.8 4.5 %collective-permute-done.8 = bf16[64,1024]{1,0:T(8,128)(2,1)S(1)} collective-permute-done((bf16[64,1024]{1,0:T(8,128)(2,1)S(1)}, bf16[64,1024]{1,0:T(8,128)(2,1)S(1)}, u32[]{:S(2)}, u32[]{:S(2)}) %collective-permute-start.8) | collective-permute-done | bytes 131104 | tf_op jit(solution)/shard_map/ppermute | solution.py:295
  186.3 7.6 %collective-permute-start.10 = (bf16[64,1024]{1,0:T(8,128)(2,1)S(1)}, bf16[64,1024]{1,0:T(8,128)(2,1)S(1)}, u32[]{:S(2)}, u32[]{:S(2)}) collective-permute-start(bf16[64,1024]{1,0:T(8,128)(2,1)S(1)} %add_convert_fusion.refs_0_), channel_id=1, source_target_pairs={{0,64},{32,96},{64,128},{96,160},{128,192},{160,224},{192,256},{22... | collective-permute-start | bytes 393224 | tf_op jit(solution)/shard_map/ppermute | solution.py:295
  193.9 1.9 collective-permute-start.11
  195.9 4.6 %collective-permute-start.9 = (bf16[64,1024]{1,0:T(8,128)(2,1)S(1)}, bf16[64,1024]{1,0:T(8,128)(2,1)S(1)}, u32[]{:S(2)}, u32[]{:S(2)}) collective-permute-start(bf16[64,1024]{1,0:T(8,128)(2,1)S(1)} %add_convert_fusion.refs_0_), channel_id=1, source_target_pairs={{0,480},{32,0},{64,32},{96,64},{128,96},{160,128},{192,160},{224,1... | collective-permute-start | bytes 393224 | tf_op jit(solution)/shard_map/ppermute | solution.py:295
  201.1 2.9 %collective-permute-done.11.refs_3_ = bf16[64,1024]{1,0:T(8,128)(2,1)S(1)} collective-permute-done((bf16[64,1024]{1,0:T(8,128)(2,1)S(1)}, bf16[64,1024]{1,0:T(8,128)(2,1)S(1)}, u32[]{:S(2)}, u32[]{:S(2)}) %collective-permute-start.11) | collective-permute-done | bytes 131104 | tf_op jit(solution)/shard_map/ppermute | solution.py:295
  204.1 1.7 shard_map.122
  205.7 5.0 %all-to-all-start.3 = ((bf16[8,64,256]{2,1,0:T(8,128)(2,1)}), bf16[8,64,256]{2,1,0:T(8,128)(2,1)S(1)}, u32[]{:S(2)}, u32[]{:S(2)}) async-start(bf16[8,64,256]{2,1,0:T(8,128)(2,1)} %get-tuple-element.56), calls=%async_computation.3 | async-start | bytes 524288 | tf_op jit(solution)/shard_map/all_to_all | solution.py:201
  212.1 5.3 %all-to-all-done.3 = bf16[8,64,256]{2,1,0:T(8,128)(2,1)S(1)} async-done(((bf16[8,64,256]{2,1,0:T(8,128)(2,1)}), bf16[8,64,256]{2,1,0:T(8,128)(2,1)S(1)}, u32[]{:S(2)}, u32[]{:S(2)}) %all-to-all-start.3) | async-done | bytes 262176 | tf_op jit(solution)/shard_map/all_to_all | solution.py:201
  217.3 4.7 %all-to-all-start.2 = ((bf16[8,64,256]{2,1,0:T(8,128)(2,1)}), bf16[8,64,256]{2,1,0:T(8,128)(2,1)S(1)}, u32[]{:S(2)}, u32[]{:S(2)}) async-start(bf16[8,64,256]{2,1,0:T(8,128)(2,1)} %get-tuple-element.55), calls=%async_computation.2 | async-start | bytes 524288 | tf_op jit(solution)/shard_map/all_to_all | solution.py:201
  222.7 5.8 %all-to-all-done.2 = bf16[8,64,256]{2,1,0:T(8,128)(2,1)S(1)} async-done(((bf16[8,64,256]{2,1,0:T(8,128)(2,1)}), bf16[8,64,256]{2,1,0:T(8,128)(2,1)S(1)}, u32[]{:S(2)}, u32[]{:S(2)}) %all-to-all-start.2) | async-done | bytes 262176 | tf_op jit(solution)/shard_map/all_to_all | solution.py:201
  (51 shorter events, 10.3 us)
Async XLA Ops:
  7.2 115.2 %all-gather.2.cloned.1.call-start = ((), (), s32[]{:S(2)}) async-start(), calls=%async_computation.4 | async-start | bytes 2162688 | tf_op jit(solution)/shard_map/all_gather | solution.py:228
  8.6 107.8 %collective-permute-start = (bf16[512,2048]{1,0:T(8,128)(2,1)}, bf16[512,2048]{1,0:T(8,128)(2,1)}, u32[]{:S(2)}, u32[]{:S(2)}) collective-permute-start(bf16[512,2048]{1,0:T(8,128)(2,1)} %bitcast.56), channel_id=1, source_target_pairs={{0,16},{16,0},{1,17},{17,1},{2,18},{18,2},{3,19},{19,3},{4,20},{20... | collective-permute-start | bytes 6291464 | tf_op jit(solution)/shard_map/ppermute | solution.py:231
  20.9 23.9 %all-to-all-start.1 = ((bf16[8,80,128]{2,1,0:T(8,128)(2,1)}), bf16[8,80,128]{2,1,0:T(8,128)(2,1)S(1)}, u32[]{:S(2)}, u32[]{:S(2)}) async-start(bf16[8,80,128]{2,1,0:T(8,128)(2,1)} %bitcast.9), calls=%async_computation.1 | async-start | bytes 327680 | tf_op jit(solution)/shard_map/while/body/all_to_all | solution.py:201
  32.5 118.1 %collective-permute-start.2 = (bf16[64,1280]{1,0:T(8,128)(2,1)S(1)}, bf16[64,1280]{1,0:T(8,128)(2,1)S(1)}, u32[]{:S(2)}, u32[]{:S(2)}) collective-permute-start(bf16[64,1280]{1,0:T(8,128)(2,1)S(1)} %pad_maximum_fusion), channel_id=1, source_target_pairs={{0,16},{16,0},{1,17},{17,1},{2,18},{18,2},{3,19},{19,3},{4,20},{20... | collective-permute-start | bytes 491528 | tf_op jit(solution)/shard_map/ppermute | solution.py:236
  46.7 69.8 %copy-start = (bf16[1,512,2048]{2,1,0:T(8,128)(2,1)S(1)}, bf16[1,512,2048]{2,1,0:T(8,128)(2,1)}, u32[]{:S(2)}) copy-start(bf16[1,512,2048]{2,1,0:T(8,128)(2,1)} %param.11) | copy-start | bytes 6291460
  48.7 66.3 %all-to-all-start = ((bf16[128,80,128]{2,1,0:T(8,128)(2,1)}), bf16[128,80,128]{2,1,0:T(8,128)(2,1)}, u32[]{:S(2)}, u32[]{:S(2)}) async-start(bf16[128,80,128]{2,1,0:T(8,128)(2,1)} %bitcast.58), calls=%async_computation | async-start | bytes 5242880 | tf_op jit(solution)/shard_map/while/body/all_to_all | solution.py:201
  122.4 1.6 copy-start.1
  124.0 40.9 %copy-start.2 = (bf16[1,1024,64]{1,2,0:T(8,128)(2,1)S(1)}, bf16[1,1024,64]{1,2,0:T(8,128)(2,1)}, u32[]{:S(2)}) copy-start(bf16[1,1024,64]{1,2,0:T(8,128)(2,1)} %param.19) | copy-start | bytes 393220
  131.4 19.2 %collective-permute-start.3 = (bf16[64,1024]{1,0:T(8,128)(2,1)S(1)}, bf16[64,1024]{1,0:T(8,128)(2,1)S(1)}, u32[]{:S(2)}, u32[]{:S(2)}) collective-permute-start(bf16[64,1024]{1,0:T(8,128)(2,1)S(1)} %get-tuple-element.52), channel_id=1, source_target_pairs={{0,32},{32,64},{64,96},{96,128},{128,160},{160,192},{192,224},{224... | collective-permute-start | bytes 393224 | tf_op jit(solution)/shard_map/ppermute | solution.py:295
  140.7 9.9 %collective-permute-start.4 = (bf16[64,1024]{1,0:T(8,128)(2,1)S(1)}, bf16[64,1024]{1,0:T(8,128)(2,1)S(1)}, u32[]{:S(2)}, u32[]{:S(2)}) collective-permute-start(bf16[64,1024]{1,0:T(8,128)(2,1)S(1)} %get-tuple-element.53), channel_id=1, source_target_pairs={{0,64},{32,96},{64,128},{96,160},{128,192},{160,224},{192,256},{22... | collective-permute-start | bytes 393224 | tf_op jit(solution)/shard_map/ppermute | solution.py:295
  146.0 6.5 %collective-permute-start.5 = (bf16[64,1024]{1,0:T(8,128)(2,1)S(1)}, bf16[64,1024]{1,0:T(8,128)(2,1)S(1)}, u32[]{:S(2)}, u32[]{:S(2)}) collective-permute-start(bf16[64,1024]{1,0:T(8,128)(2,1)S(1)} %get-tuple-element.54), channel_id=1, source_target_pairs={{0,480},{32,0},{64,32},{96,64},{128,96},{160,128},{192,160},{224,1... | collective-permute-start | bytes 393224 | tf_op jit(solution)/shard_map/ppermute | solution.py:295
  152.6 17.8 %collective-permute-start.6 = (bf16[64,1024]{1,0:T(8,128)(2,1)S(1)}, bf16[64,1024]{1,0:T(8,128)(2,1)S(1)}, u32[]{:S(2)}, u32[]{:S(2)}) collective-permute-start(bf16[64,1024]{1,0:T(8,128)(2,1)S(1)} %add_convert_fusion.1), channel_id=1, source_target_pairs={{0,128},{32,160},{64,192},{96,224},{128,256},{160,288},{192,320},{... | collective-permute-start | bytes 393224 | tf_op jit(solution)/shard_map/ppermute | solution.py:295
  155.9 25.8 %collective-permute-start.7 = (bf16[64,1024]{1,0:T(8,128)(2,1)S(1)}, bf16[64,1024]{1,0:T(8,128)(2,1)S(1)}, u32[]{:S(2)}, u32[]{:S(2)}) collective-permute-start(bf16[64,1024]{1,0:T(8,128)(2,1)S(1)} %add_convert_fusion.1), channel_id=1, source_target_pairs={{0,256},{32,288},{64,320},{96,352},{128,384},{160,416},{192,448},{... | collective-permute-start | bytes 393224 | tf_op jit(solution)/shard_map/ppermute | solution.py:295
  162.0 24.2 %collective-permute-start.8 = (bf16[64,1024]{1,0:T(8,128)(2,1)S(1)}, bf16[64,1024]{1,0:T(8,128)(2,1)S(1)}, u32[]{:S(2)}, u32[]{:S(2)}) collective-permute-start(bf16[64,1024]{1,0:T(8,128)(2,1)S(1)} %add_convert_fusion.1), channel_id=1, source_target_pairs={{0,384},{32,416},{64,448},{96,480},{128,0},{160,32},{192,64},{224,... | collective-permute-start | bytes 393224 | tf_op jit(solution)/shard_map/ppermute | solution.py:295
  165.0 45.8 %collective-permute-start.1 = (bf16[512,512]{1,0:T(8,128)(2,1)S(1)}, bf16[512,512]{1,0:T(8,128)(2,1)S(1)}, u32[]{:S(2)}, u32[]{:S(2)}) collective-permute-start(bf16[512,512]{1,0:T(8,128)(2,1)S(1)} %get-tuple-element.50), channel_id=1, source_target_pairs={{0,16},{16,0},{1,17},{17,1},{2,18},{18,2},{3,19},{19,3},{4,20},{20... | collective-permute-start | bytes 1572872 | tf_op jit(solution)/shard_map/ppermute | solution.py:285
  186.3 14.8 %collective-permute-start.10 = (bf16[64,1024]{1,0:T(8,128)(2,1)S(1)}, bf16[64,1024]{1,0:T(8,128)(2,1)S(1)}, u32[]{:S(2)}, u32[]{:S(2)}) collective-permute-start(bf16[64,1024]{1,0:T(8,128)(2,1)S(1)} %add_convert_fusion.refs_0_), channel_id=1, source_target_pairs={{0,64},{32,96},{64,128},{96,160},{128,192},{160,224},{192,256},{22... | collective-permute-start | bytes 393224 | tf_op jit(solution)/shard_map/ppermute | solution.py:295
  193.9 10.1 %collective-permute-start.11 = (bf16[64,1024]{1,0:T(8,128)(2,1)S(1)}, bf16[64,1024]{1,0:T(8,128)(2,1)S(1)}, u32[]{:S(2)}, u32[]{:S(2)}) collective-permute-start(bf16[64,1024]{1,0:T(8,128)(2,1)S(1)} %add_convert_fusion.refs_0_), channel_id=1, source_target_pairs={{0,32},{32,64},{64,96},{96,128},{128,160},{160,192},{192,224},{224... | collective-permute-start | bytes 393224 | tf_op jit(solution)/shard_map/ppermute | solution.py:295
  195.9 8.2 %collective-permute-start.9 = (bf16[64,1024]{1,0:T(8,128)(2,1)S(1)}, bf16[64,1024]{1,0:T(8,128)(2,1)S(1)}, u32[]{:S(2)}, u32[]{:S(2)}) collective-permute-start(bf16[64,1024]{1,0:T(8,128)(2,1)S(1)} %add_convert_fusion.refs_0_), channel_id=1, source_target_pairs={{0,480},{32,0},{64,32},{96,64},{128,96},{160,128},{192,160},{224,1... | collective-permute-start | bytes 393224 | tf_op jit(solution)/shard_map/ppermute | solution.py:295
  205.7 11.6 %all-to-all-start.3 = ((bf16[8,64,256]{2,1,0:T(8,128)(2,1)}), bf16[8,64,256]{2,1,0:T(8,128)(2,1)S(1)}, u32[]{:S(2)}, u32[]{:S(2)}) async-start(bf16[8,64,256]{2,1,0:T(8,128)(2,1)} %get-tuple-element.56), calls=%async_computation.3 | async-start | bytes 524288 | tf_op jit(solution)/shard_map/all_to_all | solution.py:201
  217.3 11.2 %all-to-all-start.2 = ((bf16[8,64,256]{2,1,0:T(8,128)(2,1)}), bf16[8,64,256]{2,1,0:T(8,128)(2,1)S(1)}, u32[]{:S(2)}, u32[]{:S(2)}) async-start(bf16[8,64,256]{2,1,0:T(8,128)(2,1)} %get-tuple-element.55), calls=%async_computation.2 | async-start | bytes 524288 | tf_op jit(solution)/shard_map/all_to_all | solution.py:201
Sparse Core Ops, SparseCore 0:
  10.7 107.3 all-gather.1

commit v4 on v2

v4 whole, which is shorter than its diff:
```python
import functools
import math

import jax
import jax.numpy as jnp
from jax import lax
from jax.experimental import pallas as pl
from jax.experimental.pallas import tpu as pltpu
from jax.sharding import Mesh, PartitionSpec as P

BF = jnp.bfloat16
F32 = jnp.float32
SEQ = ("zh", "zl", "core")
SWAP = [(0, 1), (1, 0)]


def dot(a, b):
    return jnp.dot(a, b, preferred_element_type=F32)


def dot_nt(a, b):
    return lax.dot_general(a, b, (((1,), (1,)), ((), ())), preferred_element_type=F32)


def pack_kernel(place_ref, key_ref, value_ref, query_ref, grad_ref, out_ref, lse_ref, block_ref):
    batch = place_ref[2]
    depth, columns = key_ref.shape
    rows = query_ref.shape[0]
    count, _, size = block_ref.shape
    heads = columns // size
    half = columns // 2
    product = grad_ref[...].astype(F32) * out_ref[...].astype(F32)
    lane = lax.broadcasted_iota(jnp.int32, (rows, size), 1)
    delta = jnp.zeros((rows, size), F32)
    for head in range(heads):
        one = jnp.sum(product[:, head * size : (head + 1) * size], axis=1, keepdims=True)
        delta = jnp.where(lane == head, one, delta)
    lse, delta = lse_ref[...], delta.T[:heads]
    zeros = jnp.zeros((16, size), BF)
    for core in range(2):
        column = pl.multiple_of(core * half + lax.rem(batch, 2) * size, size)
        mine = slice(core * heads // 2, (core + 1) * heads // 2)
        exact = jnp.concatenate([lse[mine], delta[mine]], axis=0)
        high = exact.astype(BF).astype(F32)
        stats = jnp.concatenate([high, exact - high], axis=0).astype(BF)
        for block in range(core, count, 2):

            @pl.when(batch < 2)
            def _():
                block_ref[block, :depth] = key_ref[:, pl.ds(column, size)]

            @pl.when(batch >= 2)
            def _():
                block_ref[block, :depth] = value_ref[:, pl.ds(column, size)]

            first = depth
            for ref in (query_ref, grad_ref):
                for lo in range(core * half, (core + 1) * half, size):
                    block_ref[block, first : first + rows] = ref[:, lo : lo + size]
                    first += rows
            block_ref[block, first:] = zeros
            block_ref[block, first : first + 2 * heads, :rows] = stats


def pack(place, key_weight, value_weight, query, grad, out, lse, count):
    depth, columns = key_weight.shape
    size = columns // lse.shape[0]
    return pl.pallas_call(
        pack_kernel,
        grid=(1,),
        in_specs=[pl.BlockSpec(memory_space=pltpu.SMEM)]
        + [
            pl.BlockSpec(x.shape, lambda i: (0, 0))
            for x in (key_weight, value_weight, query, grad, out, lse)
        ],
        out_specs=pl.BlockSpec((count, depth + 4 * query.shape[0] + 16, size), lambda i: (0, 0, 0)),
        out_shape=jax.ShapeDtypeStruct((count, depth + 4 * query.shape[0] + 16, size), BF),
        compiler_params=pltpu.CompilerParams(vmem_limit_bytes=32 * 2**20),
        cost_estimate=pl.CostEstimate(flops=0, bytes_accessed=2**19, transcendentals=0),
    )(place, key_weight, value_weight, query, grad, out, lse)


def project_kernel(place_ref, own_ref, other_ref, *refs):
    slabs, out_ref, weight = refs[:-2], refs[-2], refs[-1]
    step = pl.program_id(0)
    half = pl.num_programs(0) // 2
    near, far, rows, size = slabs[0].shape

    @pl.when(step == 0)
    def _():
        for shift, slab in enumerate(slabs):
            source = lax.rem(place_ref[2] + len(slabs) - shift, len(slabs))
            cols = pl.ds(pl.multiple_of(source * size, size), size)
            for zl in range(near):
                for zh in range(far):
                    first = (zh * near + zl) * rows
                    weight[first : first + rows, cols] = slab[zl, zh]

    @pl.when(step < half)
    def _():
        out_ref[...] = dot(own_ref[...], weight[...]).astype(BF)

    @pl.when(step >= half)
    def _():
        out_ref[...] = dot(other_ref[...], weight[...]).astype(BF)


def project(place, own, other, slabs):
    rows, width = own.shape
    size = slabs[0].shape[-1]
    columns = len(slabs) * size
    block = 256
    half = rows // block
    whole = pl.BlockSpec(slabs[0].shape, lambda t, b: (0, 0, 0, 0))
    return pl.pallas_call(
        project_kernel,
        grid_spec=pltpu.PrefetchScalarGridSpec(
            num_scalar_prefetch=1,
            grid=(2 * half,),
            in_specs=[
                pl.BlockSpec((block, width), lambda t, b: (jnp.minimum(t, half - 1), 0)),
                pl.BlockSpec((block, width), lambda t, b: (jnp.maximum(t - half, 0), 0)),
            ]
            + [whole] * len(slabs),
            out_specs=pl.BlockSpec((block, columns), lambda t, b: (t, 0)),
            scratch_shapes=[pltpu.VMEM((width, columns), BF)],
        ),
        out_shape=jax.ShapeDtypeStruct((2 * rows, columns), BF),
        compiler_params=pltpu.CompilerParams(vmem_limit_bytes=32 * 2**20),
        cost_estimate=pl.CostEstimate(flops=0, bytes_accessed=2**20, transcendentals=0),
    )(place, own, other, *slabs)


def attend_kernel(
    kv_ref, rows_ref, stat_ref, own_ref, other_ref, part_ref, query, grad, qt, gt, total,
    size, scaling, latent_factor, prefix_factor,
):
    step = pl.program_id(0)
    last = pl.num_programs(0) - 1
    half = pl.num_programs(0) // 2
    near, far, cores, _, _ = rows_ref.shape
    rows = query.shape[0] // (near * far * cores)

    @pl.when(step == 0)
    def _():
        for zl in range(near):
            for zh in range(far):
                for core in range(cores):
                    first = ((zh * near + zl) * cores + core) * rows
                    for part in range(4):
                        to = (query, grad)[part // 2]
                        lo = part % 2 * size
                        to[first : first + rows, lo : lo + size] = rows_ref[
                            zl, zh, core, part * rows : (part + 1) * rows
                        ]
        qt[...] = query[...].T
        gt[...] = grad[...].T
        total[...] = jnp.zeros_like(total)

    key_out, value_out = [], []
    for head in range(2):
        cols = slice(head * size, (head + 1) * size)
        keys = kv_ref[:, cols]
        values = kv_ref[:, (2 + head) * size : (3 + head) * size]
        scores = dot(keys, qt[cols, :]) * scaling
        weights = jnp.exp(scores - stat_ref[head : head + 1, :])
        probs = dot(values, gt[cols, :])
        score_grad = (weights * (probs - stat_ref[2 + head : 3 + head, :])).astype(BF)
        value_out.append(dot(weights.astype(BF), grad[:, cols]) * latent_factor)
        key_out.append(dot(score_grad, query[:, cols]) * (scaling * latent_factor))
        total[cols, :] += dot(keys.T, score_grad)
    result = jnp.concatenate(key_out + value_out, axis=1).astype(BF)

    @pl.when(step < half)
    def _():
        own_ref[...] = result

    @pl.when(step >= half)
    def _():
        other_ref[...] = result

    @pl.when(step == last)
    def _():
        part_ref[...] = (total[...] * (scaling * prefix_factor)).astype(BF)


def attend(kv, gathered, stats, prefix_count):
    tokens, columns = kv.shape
    latents = stats.shape[1]
    size = columns // 4
    block = 256
    half = tokens // block // 2
    kernel = functools.partial(
        attend_kernel,
        size=size,
        scaling=1.0 / math.sqrt(size),
        latent_factor=1.0 / math.sqrt(latents),
        prefix_factor=1.0 / math.sqrt(prefix_count),
    )
    return pl.pallas_call(
        kernel,
        grid=(tokens // block,),
        in_specs=[
            pl.BlockSpec((block, columns), lambda t: (t, 0)),
            pl.BlockSpec(gathered.shape, lambda t: (0, 0, 0, 0, 0)),
            pl.BlockSpec(stats.shape, lambda t: (0, 0)),
        ],
        out_specs=[
            pl.BlockSpec((block, columns), lambda t: (jnp.minimum(t, half - 1), 0)),
            pl.BlockSpec((block, columns), lambda t: (jnp.maximum(t - half, 0), 0)),
            pl.BlockSpec((2 * size, latents), lambda t: (0, 0)),
        ],
        out_shape=[
            jax.ShapeDtypeStruct((tokens // 2, columns), BF),
            jax.ShapeDtypeStruct((tokens // 2, columns), BF),
            jax.ShapeDtypeStruct((2 * size, latents), BF),
        ],
        scratch_shapes=[
            pltpu.VMEM((latents, 2 * size), BF),
            pltpu.VMEM((latents, 2 * size), BF),
            pltpu.VMEM((2 * size, latents), BF),
            pltpu.VMEM((2 * size, latents), BF),
            pltpu.VMEM((2 * size, latents), F32),
        ],
        compiler_params=pltpu.CompilerParams(vmem_limit_bytes=32 * 2**20),
        cost_estimate=pl.CostEstimate(
            flops=20 * tokens * latents * size,
            bytes_accessed=6 * 2**20,
            transcendentals=2 * tokens * latents,
        ),
    )(kv, gathered, stats)


def tail_kernel(query_ref, latent_ref, every_ref, latent_out, weight_out):
    count, rows, width = latent_out.shape
    latent = dot(query_ref[...], every_ref[...]).astype(BF)
    weight = dot_nt(latent_ref[...], every_ref[...]).astype(BF)
    for i in range(count):
        core, group = divmod(i, count // 2)
        latent_out[i] = latent[core * rows : (core + 1) * rows, group * width : (group + 1) * width]
        weight_out[i] = weight[core * rows : (core + 1) * rows, :]


def tail(query, latent, every, tensors, batches):
    both, half = query.shape
    rows = both // 2
    latents = latent.shape[1]
    return pl.pallas_call(
        tail_kernel,
        in_specs=[pl.BlockSpec(memory_space=pltpu.VMEM)] * 3,
        out_specs=[pl.BlockSpec(memory_space=pltpu.VMEM)] * 2,
        out_shape=[
            jax.ShapeDtypeStruct((2 * tensors, rows, latents // tensors), BF),
            jax.ShapeDtypeStruct((2 * batches, rows, half), BF),
        ],
        compiler_params=pltpu.CompilerParams(vmem_limit_bytes=32 * 2**20),
        cost_estimate=pl.CostEstimate(flops=0, bytes_accessed=2**20, transcendentals=0),
    )(query, latent, every)


def exchange(x, axes):
    return lax.all_to_all(x, axes, 0, 0, tiled=True)


def spread(x, axes):
    count = lax.axis_size(axes)
    return exchange(jnp.broadcast_to(x[None], (count,) + x.shape), axes)


def halves(x):
    return jnp.transpose(x.reshape(x.shape[0], 2, x.shape[1] // 2), (1, 0, 2))


def local(
    prefix, key_weight, value_weight, query_weight, queries, out_grad, attn_out, shifted_lse, latent_in
):
    core = lax.axis_index("core")
    batch = lax.axis_index("dp")
    first = core == 0
    ranks = lax.axis_size(SEQ)
    batches = lax.axis_size("dp")
    tokens_in = prefix[0]
    token_count = tokens_in.shape[0]
    rows, columns = queries.shape[1:]
    heads = shifted_lse.shape[2]
    size = columns // heads
    latents = rows * ranks

    other_tokens = lax.ppermute(tokens_in, "core", SWAP)
    latent_own = latent_in[0].T
    query_halves = halves(query_weight)
    query_mine = jnp.where(first, query_halves[0], query_halves[1])
    query_theirs = jnp.where(first, query_halves[1], query_halves[0])
    swapped = lax.ppermute(jnp.concatenate([latent_own, query_theirs], axis=1), "core", SWAP)
    latent_other, query_other = swapped[:, :latents], swapped[:, latents:]

    def in_order(own, other):
        return jnp.where(first, jnp.concatenate([own, other], 0), jnp.concatenate([other, own], 0))

    latent_both = in_order(latent_own, latent_other)
    query_both = in_order(query_mine, query_other)

    far = lax.axis_size("zh")
    near = lax.axis_size("zl")
    depth = key_weight.shape[0]
    place = jnp.stack([core, lax.axis_index("zl"), batch]).astype(jnp.int32)
    blocks = pack(
        place, key_weight, value_weight, queries[0], out_grad[0], attn_out[0], shifted_lse[0].T, 2 * far
    )
    landed = exchange(blocks, ("zh", "core"))
    slab = lax.all_gather(landed[:, :depth], "zl", axis=0, tiled=True)
    gathered = spread(landed[:, depth:], "zl").reshape(near, far, 2, -1, size)
    slab = slab.reshape(near, far, 2 * depth, size)
    slabs = [slab] + [
        lax.ppermute(slab, "dp", [(i, (i + d) % batches) for i in range(batches)])
        for d in range(1, batches)
    ]
    stats = gathered[:, :, :, 4 * rows : 4 * rows + 2 * heads, :rows].astype(F32)
    stats = stats[:, :, :, :heads] + stats[:, :, :, heads:]
    stats = jnp.transpose(stats, (3, 1, 0, 2, 4)).reshape(heads, latents)

    kv = project(place, tokens_in, other_tokens, slabs)
    own_grads, other_grads, part = attend(kv, gathered, stats, token_count * ranks)
    theirs = lax.ppermute(other_grads, "core", SWAP)
    half = columns // 2

    def whole(lo):
        mine, other = own_grads[:, lo : lo + half], theirs[:, lo : lo + half]
        return jnp.where(
            first, jnp.concatenate([mine, other], 1), jnp.concatenate([other, mine], 1)
        )[None]

    share = exchange(part.reshape(far * near, -1, latents), ("zh", "zl"))
    share = jnp.sum(share.astype(F32), axis=0).astype(BF)
    every = lax.all_gather(share, ("zh", "zl"), axis=0, tiled=True)
    latent_part, weight_part = tail(
        query_both, latent_both, every, lax.axis_size("tensor"), batches
    )

    latent_sum = jnp.sum(exchange(latent_part, ("core", "tensor")).astype(F32), axis=0)
    latent_grad = latent_sum.astype(BF).T[None]

    weight_sum = exchange(weight_part, ("core", "dp"))
    weight_sum = jnp.sum(weight_sum.reshape(2, batches, columns // 8, half).astype(F32), axis=1)
    weight_factor = 1.0 / math.sqrt(latents * batches)
    weight_grad = jnp.transpose(weight_sum, (1, 0, 2)).reshape(columns // 8, columns) * weight_factor
    return (whole(0), whole(half), latent_grad, weight_grad)


def solution(mesh):
    fine = Mesh(
        mesh.devices.reshape(4, 4, 2, *mesh.devices.shape[1:]), SEQ + tuple(mesh.axis_names[1:])
    )
    return jax.shard_map(
        local,
        mesh=fine,
        in_specs=(
            P("dp", SEQ, None),
            P(SEQ, "tensor"),
            P(SEQ, "tensor"),
            P(SEQ, "tensor"),
            P("dp", SEQ, "tensor"),
            P("dp", SEQ, "tensor"),
            P("dp", SEQ, "tensor"),
            P("dp", SEQ, "tensor"),
            P("dp", None, SEQ),
        ),
        out_specs=(
            P("dp", SEQ, "tensor"),
            P("dp", SEQ, "tensor"),
            P("dp", "tensor", SEQ),
            P(SEQ, "tensor"),
        ),
        check_vma=False,
    )
```

time: 212 us -> 228 us (1.075)
  blocking collectives: 74.1 us -> 99.1 us
  between operations: 14.4 us -> 0.85 us
  starting transfers between devices: 45.3 us -> 56.8 us
  local copies, waits for them, and re-layouts: 5.81 us -> 11.5 us
  waiting for transfers between devices: 49.1 us -> 43.7 us
  other arithmetic: 6.17 us -> 2.22 us
  Pallas kernels: 15.8 us -> 13.2 us
    all_gather x2, blocking collectives: 33.2 us -> 60.1 us  [the longest x1 31.1 us: local(): slab = lax.all_gather(landed[:, :depth], 'zl', axis=0, tiled=True)]
    all_to_all x3 -> x4, starting transfers between devices: 19.8 us -> 35.6 us  [exchange(): return lax.all_to_all(x, axes, 0, 0, tiled=True)]
    all_to_all x3 -> x4, waiting for transfers between devices: 30.7 us -> 24.9 us  [exchange(): return lax.all_to_all(x, axes, 0, 0, tiled=True)]
    unnamed x16 -> x22, local copies, waits for them, and re-layouts: 1.37 us -> 6.83 us
    ppermute x1, starting transfers between devices: 8.79 us -> 3.55 us  [local(): other_tokens = lax.ppermute(tokens_in, 'core', SWAP)]
    pallas_call x1, Pallas kernels: 6.78 us -> 3.87 us  [project(): pl.pallas_call(project_kernel, grid_spec=pltpu.PrefetchScalarGridSpec(num...]
    ppermute x1, starting transfers between devices: 1.92 us -> 4.67 us  [local(): lax.ppermute(jnp.concatenate([latent_own, query_theirs], axis=1), 'core',...]
    slice x2, local copies, waits for them, and re-layouts: 0.07 us -> 2.56 us  [the longest x1 1.57 us: local(): slab = lax.all_gather(landed[:, :depth], 'zl', axis=0, tiled=True)]
  transfers between devices with their start and end apart: 10 -> 10, of which waited for: 7 -> 7; matrix products, arithmetic and copies ran while one was open for 3% -> 2% of each run, Pallas kernels for 3% -> 2%
where the time goes in v4:
time: 228 us; the launch traced here: 227 us
  blocking collectives  99.1 us (43%)
  starting transfers between devices  56.8 us (25%)
  waiting for transfers between devices  43.7 us (19%)
  Pallas kernels  13.2 us (6%)
  local copies, waits for them, and re-layouts  11.5 us (5%)
    all_to_all x1, blocking collectives, exchange(): return lax.all_to_all(x, axes, 0, 0, tiled=True)  39 us
    all_to_all x4, starting transfers between devices, exchange(): return lax.all_to_all(x, axes, 0, 0, tiled=True)  35.6 us
    all_gather x1, blocking collectives, local(): slab = lax.all_gather(landed[:, :depth], 'zl', axis=0, tiled=True)  31.1 us
    all_gather x1, blocking collectives, local(): every = lax.all_gather(share, ('zh', 'zl'), axis=0, tiled=True)  29 us
    all_to_all x4, waiting for transfers between devices, exchange(): return lax.all_to_all(x, axes, 0, 0, tiled=True)  24.9 us
    ppermute x3, waiting for transfers between devices, local(): lax.ppermute(slab, 'dp', [(i, (i + d) % batches) for i in range(batches)])  17.8 us
    ppermute x3, starting transfers between devices, local(): lax.ppermute(slab, 'dp', [(i, (i + d) % batches) for i in range(batches)])  10.7 us
    pallas_call x1, Pallas kernels, attend(): pl.pallas_call(kernel, grid=(tokens // block,), in_specs=[pl.BlockSpec((b...  7.38 us
  transfers between devices with their start and end apart: 10, of which 7 were waited for; matrix products, arithmetic and copies ran while one was open for 2% of the time, Pallas kernels for 2%

profile of v4, /device:TPU:1, one launch (start us, length us, event | category | flops | bytes accessed | tf_op | source)
XLA Modules:
  0.0 227.3 jit_solution(16674619305589740037)
XLA Ops:
  0.7 0.8 copy-done.3
  1.6 0.8 copy-done.4
  5.4 0.8 shard_map.120
  6.2 39.0 %all_to_all.25 = bf16[8,208,128]{2,1,0:T(8,128)(2,1)} all-to-all(bf16[8,208,128]{2,1,0:T(8,128)(2,1)S(1)} %shard_map.120), channel_id=1, replica_groups=mesh['zh'=4,'zl'=4,'core'=2,'tensor'=4,'dp'=4] {'zh','core'}, dimensions={0} | all-to-all | bytes 851968 | tf_op jit(solution)/shard_map/all_to_all | solution.py:262
  45.1 1.0 slice.55
  46.1 1.2 broadcast_in_dim.4
  47.3 8.2 %all-to-all-start.1 = ((bf16[4,8,144,128]{3,2,1,0:T(8,128)(2,1)}), bf16[4,8,144,128]{3,2,1,0:T(8,128)(2,1)S(1)}, u32[]{:S(2)}, u32[]{:S(2)}) async-start(bf16[4,8,144,128]{3,2,1,0:T(8,128)(2,1)} %broadcast_in_dim.4), calls=%async_computation.1 | async-start | bytes 2359296 | tf_op jit(solution)/shard_map/all_to_all | solution.py:262
  55.5 3.6 %collective-permute-start = (bf16[512,2048]{1,0:T(8,128)(2,1)S(1)}, bf16[512,2048]{1,0:T(8,128)(2,1)S(1)}, u32[]{:S(2)}, u32[]{:S(2)}) collective-permute-start(bf16[512,2048]{1,0:T(8,128)(2,1)S(1)} %bitcast.47), channel_id=1, source_target_pairs={{0,16},{16,0},{1,17},{17,1},{2,18},{18,2},{3,19},{19,3},{4,20},{20... | collective-permute-start | bytes 6291464 | tf_op jit(solution)/shard_map/ppermute | solution.py:289
  59.1 1.6 slice.54
  60.6 31.1 %all_gather.6 = bf16[32,64,128]{2,1,0:T(8,128)(2,1)S(1)} all-gather(bf16[8,64,128]{2,1,0:T(8,128)(2,1)} %slice.54), channel_id=1, replica_groups=mesh['zh'=4,'zl'=4,'core'=2,'tensor'=4,'dp'=4] {'zl'}, dimensions={0}, use_global_device_ids=true | all-gather | bytes 655360 | tf_op jit(solution)/shard_map/all_gather | solution.py:311
  91.7 3.2 %collective-permute-start.1 = (bf16[4,4,128,128]{3,2,1,0:T(8,128)(2,1)S(1)}, bf16[4,4,128,128]{3,2,1,0:T(8,128)(2,1)S(1)}, u32[]{:S(2)}, u32[]{:S(2)}) collective-permute-start(bf16[4,4,128,128]{3,2,1,0:T(8,128)(2,1)S(1)} %bitcast.49), channel_id=1, source_target_pairs={{0,1},{1,2},{2,3},{3,0},{4,5},{5,6},{6,7},{7,4},{8,9},{9,10},{10,1... | collective-permute-start | bytes 1572872 | tf_op jit(solution)/shard_map/ppermute | solution.py:315
  94.9 4.5 %collective-permute-start.2 = (bf16[4,4,128,128]{3,2,1,0:T(8,128)(2,1)S(1)}, bf16[4,4,128,128]{3,2,1,0:T(8,128)(2,1)S(1)}, u32[]{:S(2)}, u32[]{:S(2)}) collective-permute-start(bf16[4,4,128,128]{3,2,1,0:T(8,128)(2,1)S(1)} %bitcast.50), channel_id=1, source_target_pairs={{0,2},{1,3},{2,0},{3,1},{4,6},{5,7},{6,4},{7,5},{8,10},{9,11},{10,... | collective-permute-start | bytes 1572872 | tf_op jit(solution)/shard_map/ppermute | solution.py:315
  99.5 3.0 %collective-permute-start.3 = (bf16[4,4,128,128]{3,2,1,0:T(8,128)(2,1)S(1)}, bf16[4,4,128,128]{3,2,1,0:T(8,128)(2,1)S(1)}, u32[]{:S(2)}, u32[]{:S(2)}) collective-permute-start(bf16[4,4,128,128]{3,2,1,0:T(8,128)(2,1)S(1)} %bitcast.51), channel_id=1, source_target_pairs={{0,3},{1,0},{2,1},{3,2},{4,7},{5,4},{6,5},{7,6},{8,11},{9,8},{10,9... | collective-permute-start | bytes 1572872 | tf_op jit(solution)/shard_map/ppermute | solution.py:315
  102.5 1.9 collective-permute-done.1.refs_1_
  104.4 12.3 %collective-permute-done.2.refs_2_ = bf16[4,4,128,128]{3,2,1,0:T(8,128)(2,1)S(1)} collective-permute-done((bf16[4,4,128,128]{3,2,1,0:T(8,128)(2,1)S(1)}, bf16[4,4,128,128]{3,2,1,0:T(8,128)(2,1)S(1)}, u32[]{:S(2)}, u32[]{:S(2)}) %collective-permute-start.2) | collective-permute-done | bytes 524320 | tf_op jit(solution)/shard_map/ppermute | solution.py:315
  116.7 3.6 %collective-permute-done.3.refs_3_ = bf16[4,4,128,128]{3,2,1,0:T(8,128)(2,1)S(1)} collective-permute-done((bf16[4,4,128,128]{3,2,1,0:T(8,128)(2,1)S(1)}, bf16[4,4,128,128]{3,2,1,0:T(8,128)(2,1)S(1)}, u32[]{:S(2)}, u32[]{:S(2)}) %collective-permute-start.3) | collective-permute-done | bytes 524320 | tf_op jit(solution)/shard_map/ppermute | solution.py:315
  120.3 3.9 %shard_map.121.kv_ref = bf16[1024,512]{1,0:T(8,128)(2,1)S(1)} custom-call(s32[3]{0:T(128)S(1)} %pad_add_fusion.place_ref, bf16[512,2048]{1,0:T(8,128)(2,1)S(1)} %bitcast.48, bf16[512,2048]{1,0:T(8,128)(2,1)S(1)} %collective-permute-done.other_ref, bf16[4,4,128,128]{3,2,1,0:T(8,128)(2,1)S(1)} %bitcast.52, ...), custom_call_target="tpu_custom_call" | custom-call | bytes 1048576 | tf_op jit(solution)/shard_map/pallas_call | solution.py:115
  124.2 1.0 copy-done.1
  125.3 1.2 copy-done.2
  126.6 7.4 %shard_map.122 = (bf16[512,512]{1,0:T(8,128)(2,1)S(1)}, bf16[512,512]{1,0:T(8,128)(2,1)S(1)}, bf16[256,1024]{1,0:T(8,128)(2,1)}) custom-call(bf16[1024,512]{1,0:T(8,128)(2,1)S(1)} %copy-done.2, bf16[4,4,2,144,128]{4,3,2,1,0:T(8,128)(2,1)S(1)} %bitcast.54, f32[4,1024]{1,0:T(4,128)S(1)} %reshape.146.stat_ref), custom_call_target="tpu_custom_call" | custom-call | flops 2684354560 | bytes 6291456 | tf_op jit(solution)/shard_map/pallas_call | solution.py:200
  133.9 4.5 %all-to-all-start.2 = ((bf16[16,16,1024]{2,1,0:T(8,128)(2,1)}), bf16[16,16,1024]{2,1,0:T(8,128)(2,1)S(1)}, u32[]{:S(2)}, u32[]{:S(2)}) async-start(bf16[16,16,1024]{2,1,0:T(8,128)(2,1)} %bitcast.22), calls=%async_computation.2 | async-start | bytes 1048576 | tf_op jit(solution)/shard_map/all_to_all | solution.py:262
  138.5 4.7 %collective-permute-start.5 = (bf16[64,1280]{1,0:T(8,128)(2,1)S(1)}, bf16[64,1280]{1,0:T(8,128)(2,1)S(1)}, u32[]{:S(2)}, u32[]{:S(2)}) collective-permute-start(bf16[64,1280]{1,0:T(8,128)(2,1)S(1)} %pad_maximum_fusion), channel_id=1, source_target_pairs={{0,16},{16,0},{1,17},{17,1},{2,18},{18,2},{3,19},{19,3},{4,20},{20... | collective-permute-start | bytes 491528 | tf_op jit(solution)/shard_map/ppermute | solution.py:294
  143.2 1.0 collective-permute-done.5
  144.3 2.3 %collective-permute-start.4 = (bf16[512,512]{1,0:T(8,128)(2,1)S(1)}, bf16[512,512]{1,0:T(8,128)(2,1)S(1)}, u32[]{:S(2)}, u32[]{:S(2)}) collective-permute-start(bf16[512,512]{1,0:T(8,128)(2,1)S(1)} %get-tuple-element.10), channel_id=1, source_target_pairs={{0,16},{16,0},{1,17},{17,1},{2,18},{18,2},{3,19},{19,3},{4,20},{20... | collective-permute-start | bytes 1572872 | tf_op jit(solution)/shard_map/ppermute | solution.py:324
  146.6 13.8 %all-to-all-done.2 = bf16[16,16,1024]{2,1,0:T(8,128)(2,1)S(1)} async-done(((bf16[16,16,1024]{2,1,0:T(8,128)(2,1)}), bf16[16,16,1024]{2,1,0:T(8,128)(2,1)S(1)}, u32[]{:S(2)}, u32[]{:S(2)}) %all-to-all-start.2) | async-done | bytes 524320 | tf_op jit(solution)/shard_map/all_to_all | solution.py:262
  160.5 29.0 %all_gather.7.every_ref = bf16[256,1024]{1,0:T(8,128)(2,1)S(1)} all-gather(bf16[16,1024]{1,0:T(8,128)(2,1)S(1)} %reduce_sum.33), channel_id=1, replica_groups=mesh['zh'=4,'zl'=4,'core'=2,'tensor'=4,'dp'=4] {'zh','zl'}, dimensions={0}, use_global_device_ids=true | all-gather | bytes 557056 | tf_op jit(solution)/shard_map/all_gather | solution.py:335
  189.5 1.1 shard_map.123
  190.6 18.3 %all-to-all-start.4 = ((bf16[8,64,256]{2,1,0:T(8,128)(2,1)}), bf16[8,64,256]{2,1,0:T(8,128)(2,1)S(1)}, u32[]{:S(2)}, u32[]{:S(2)}) async-start(bf16[8,64,256]{2,1,0:T(8,128)(2,1)} %get-tuple-element.13), calls=%async_computation.4 | async-start | bytes 524288 | tf_op jit(solution)/shard_map/all_to_all | solution.py:262
  209.0 1.2 maximum_select_fusion
  210.2 5.3 %all-to-all-done.4 = bf16[8,64,256]{2,1,0:T(8,128)(2,1)S(1)} async-done(((bf16[8,64,256]{2,1,0:T(8,128)(2,1)}), bf16[8,64,256]{2,1,0:T(8,128)(2,1)S(1)}, u32[]{:S(2)}, u32[]{:S(2)}) %all-to-all-start.4) | async-done | bytes 262176 | tf_op jit(solution)/shard_map/all_to_all | solution.py:262
  215.5 4.6 %all-to-all-start.3 = ((bf16[8,64,256]{2,1,0:T(8,128)(2,1)}), bf16[8,64,256]{2,1,0:T(8,128)(2,1)S(1)}, u32[]{:S(2)}, u32[]{:S(2)}) async-start(bf16[8,64,256]{2,1,0:T(8,128)(2,1)} %get-tuple-element.12), calls=%async_computation.3 | async-start | bytes 524288 | tf_op jit(solution)/shard_map/all_to_all | solution.py:262
  220.8 5.8 %all-to-all-done.3 = bf16[8,64,256]{2,1,0:T(8,128)(2,1)S(1)} async-done(((bf16[8,64,256]{2,1,0:T(8,128)(2,1)}), bf16[8,64,256]{2,1,0:T(8,128)(2,1)S(1)}, u32[]{:S(2)}, u32[]{:S(2)}) %all-to-all-start.3) | async-done | bytes 262176 | tf_op jit(solution)/shard_map/all_to_all | solution.py:262
  (40 shorter events, 4.9 us)
Async XLA Ops:
  0.7 0.8 copy-start.3
  1.6 0.8 copy-start.4
  2.4 0.8 copy-start.5
  3.2 0.8 copy-start.6
  3.9 0.8 copy-start.7
  4.7 0.7 copy-start.8
  47.3 8.2 %copy-start = (bf16[1,512,2048]{2,1,0:T(8,128)(2,1)S(1)}, bf16[1,512,2048]{2,1,0:T(8,128)(2,1)}, u32[]{:S(2)}) copy-start(bf16[1,512,2048]{2,1,0:T(8,128)(2,1)} %param.9) | copy-start | bytes 6291460
  47.3 77.8 %all-to-all-start.1 = ((bf16[4,8,144,128]{3,2,1,0:T(8,128)(2,1)}), bf16[4,8,144,128]{3,2,1,0:T(8,128)(2,1)S(1)}, u32[]{:S(2)}, u32[]{:S(2)}) async-start(bf16[4,8,144,128]{3,2,1,0:T(8,128)(2,1)} %broadcast_in_dim.4), calls=%async_computation.1 | async-start | bytes 2359296 | tf_op jit(solution)/shard_map/all_to_all | solution.py:262
  55.5 64.8 %collective-permute-start = (bf16[512,2048]{1,0:T(8,128)(2,1)S(1)}, bf16[512,2048]{1,0:T(8,128)(2,1)S(1)}, u32[]{:S(2)}, u32[]{:S(2)}) collective-permute-start(bf16[512,2048]{1,0:T(8,128)(2,1)S(1)} %bitcast.47), channel_id=1, source_target_pairs={{0,16},{16,0},{1,17},{17,1},{2,18},{18,2},{3,19},{19,3},{4,20},{20... | collective-permute-start | bytes 6291464 | tf_op jit(solution)/shard_map/ppermute | solution.py:289
  91.7 12.6 %collective-permute-start.1 = (bf16[4,4,128,128]{3,2,1,0:T(8,128)(2,1)S(1)}, bf16[4,4,128,128]{3,2,1,0:T(8,128)(2,1)S(1)}, u32[]{:S(2)}, u32[]{:S(2)}) collective-permute-start(bf16[4,4,128,128]{3,2,1,0:T(8,128)(2,1)S(1)} %bitcast.49), channel_id=1, source_target_pairs={{0,1},{1,2},{2,3},{3,0},{4,5},{5,6},{6,7},{7,4},{8,9},{9,10},{10,1... | collective-permute-start | bytes 1572872 | tf_op jit(solution)/shard_map/ppermute | solution.py:315
  94.9 21.8 %collective-permute-start.2 = (bf16[4,4,128,128]{3,2,1,0:T(8,128)(2,1)S(1)}, bf16[4,4,128,128]{3,2,1,0:T(8,128)(2,1)S(1)}, u32[]{:S(2)}, u32[]{:S(2)}) collective-permute-start(bf16[4,4,128,128]{3,2,1,0:T(8,128)(2,1)S(1)} %bitcast.50), channel_id=1, source_target_pairs={{0,2},{1,3},{2,0},{3,1},{4,6},{5,7},{6,4},{7,5},{8,10},{9,11},{10,... | collective-permute-start | bytes 1572872 | tf_op jit(solution)/shard_map/ppermute | solution.py:315
  99.5 20.8 %collective-permute-start.3 = (bf16[4,4,128,128]{3,2,1,0:T(8,128)(2,1)S(1)}, bf16[4,4,128,128]{3,2,1,0:T(8,128)(2,1)S(1)}, u32[]{:S(2)}, u32[]{:S(2)}) collective-permute-start(bf16[4,4,128,128]{3,2,1,0:T(8,128)(2,1)S(1)} %bitcast.51), channel_id=1, source_target_pairs={{0,3},{1,0},{2,1},{3,2},{4,7},{5,4},{6,5},{7,6},{8,11},{9,8},{10,9... | collective-permute-start | bytes 1572872 | tf_op jit(solution)/shard_map/ppermute | solution.py:315
  124.2 1.0 copy-start.1
  125.3 1.2 copy-start.2
  126.6 11.9 %copy-start.10 = (bf16[64,512]{1,0:T(8,128)(2,1)S(1)}, bf16[64,512]{1,0:T(8,128)(2,1)}, u32[]{:S(2)}) copy-start(bf16[64,512]{1,0:T(8,128)(2,1)} %param.12) | copy-start | bytes 196612
  133.9 4.5 %copy-start.9 = (bf16[1,1024,64]{1,2,0:T(8,128)(2,1)S(1)}, bf16[1,1024,64]{1,2,0:T(8,128)(2,1)}, u32[]{:S(2)}) copy-start(bf16[1,1024,64]{1,2,0:T(8,128)(2,1)} %param.17) | copy-start | bytes 393220
  133.9 26.5 %all-to-all-start.2 = ((bf16[16,16,1024]{2,1,0:T(8,128)(2,1)}), bf16[16,16,1024]{2,1,0:T(8,128)(2,1)S(1)}, u32[]{:S(2)}, u32[]{:S(2)}) async-start(bf16[16,16,1024]{2,1,0:T(8,128)(2,1)} %bitcast.22), calls=%async_computation.2 | async-start | bytes 1048576 | tf_op jit(solution)/shard_map/all_to_all | solution.py:262
  138.5 5.7 %collective-permute-start.5 = (bf16[64,1280]{1,0:T(8,128)(2,1)S(1)}, bf16[64,1280]{1,0:T(8,128)(2,1)S(1)}, u32[]{:S(2)}, u32[]{:S(2)}) collective-permute-start(bf16[64,1280]{1,0:T(8,128)(2,1)S(1)} %pad_maximum_fusion), channel_id=1, source_target_pairs={{0,16},{16,0},{1,17},{17,1},{2,18},{18,2},{3,19},{19,3},{4,20},{20... | collective-permute-start | bytes 491528 | tf_op jit(solution)/shard_map/ppermute | solution.py:294
  144.3 64.6 %collective-permute-start.4 = (bf16[512,512]{1,0:T(8,128)(2,1)S(1)}, bf16[512,512]{1,0:T(8,128)(2,1)S(1)}, u32[]{:S(2)}, u32[]{:S(2)}) collective-permute-start(bf16[512,512]{1,0:T(8,128)(2,1)S(1)} %get-tuple-element.10), channel_id=1, source_target_pairs={{0,16},{16,0},{1,17},{17,1},{2,18},{18,2},{3,19},{19,3},{4,20},{20... | collective-permute-start | bytes 1572872 | tf_op jit(solution)/shard_map/ppermute | solution.py:324
  190.6 24.8 %all-to-all-start.4 = ((bf16[8,64,256]{2,1,0:T(8,128)(2,1)}), bf16[8,64,256]{2,1,0:T(8,128)(2,1)S(1)}, u32[]{:S(2)}, u32[]{:S(2)}) async-start(bf16[8,64,256]{2,1,0:T(8,128)(2,1)} %get-tuple-element.13), calls=%async_computation.4 | async-start | bytes 524288 | tf_op jit(solution)/shard_map/all_to_all | solution.py:262
  215.5 11.2 %all-to-all-start.3 = ((bf16[8,64,256]{2,1,0:T(8,128)(2,1)}), bf16[8,64,256]{2,1,0:T(8,128)(2,1)S(1)}, u32[]{:S(2)}, u32[]{:S(2)}) async-start(bf16[8,64,256]{2,1,0:T(8,128)(2,1)} %get-tuple-element.12), calls=%async_computation.3 | async-start | bytes 524288 | tf_op jit(solution)/shard_map/all_to_all | solution.py:262

commit v5 on v4

--- a/solution.py
+++ b/solution.py
@@ -22,7 +22,17 @@
     return lax.dot_general(a, b, (((1,), (1,)), ((), ())), preferred_element_type=F32)
 
 
-def pack_kernel(place_ref, key_ref, value_ref, query_ref, grad_ref, out_ref, lse_ref, block_ref):
+def pack_kernel(place_ref, *refs):
+    sources, block_ref, landing, arrived = refs[:6], refs[6], refs[7:13], refs[13]
+    copies = [
+        pltpu.make_async_copy(source, target, arrived.at[i])
+        for i, (source, target) in enumerate(zip(sources, landing))
+    ]
+    for copy in copies:
+        copy.start()
+    for copy in copies:
+        copy.wait()
+    key_ref, value_ref, query_ref, grad_ref, out_ref, lse_ref = landing
     batch = place_ref[2]
     depth, columns = key_ref.shape
     rows = query_ref.shape[0]
@@ -65,19 +75,40 @@
 def pack(place, key_weight, value_weight, query, grad, out, lse, count):
     depth, columns = key_weight.shape
     size = columns // lse.shape[0]
+    sources = (key_weight, value_weight, query, grad, out, lse)
     return pl.pallas_call(
         pack_kernel,
-        grid=(1,),
         in_specs=[pl.BlockSpec(memory_space=pltpu.SMEM)]
-        + [
-            pl.BlockSpec(x.shape, lambda i: (0, 0))
-            for x in (key_weight, value_weight, query, grad, out, lse)
-        ],
-        out_specs=pl.BlockSpec((count, depth + 4 * query.shape[0] + 16, size), lambda i: (0, 0, 0)),
+        + [pl.BlockSpec(memory_space=pltpu.HBM)] * len(sources),
+        out_specs=pl.BlockSpec(memory_space=pltpu.VMEM),
         out_shape=jax.ShapeDtypeStruct((count, depth + 4 * query.shape[0] + 16, size), BF),
-        compiler_params=pltpu.CompilerParams(vmem_limit_bytes=32 * 2**20),
+        scratch_shapes=[pltpu.VMEM(x.shape, x.dtype) for x in sources]
+        + [pltpu.SemaphoreType.DMA((len(sources),))],
+        compiler_params=pltpu.CompilerParams(vmem_limit_bytes=60 * 2**20),
         cost_estimate=pl.CostEstimate(flops=0, bytes_accessed=2**19, transcendentals=0),
-    )(place, key_weight, value_weight, query, grad, out, lse)
+    )(place, *sources)
+
+
+def unpack_kernel(landed_ref, weight_ref, rows_ref):
+    depth = weight_ref.shape[1]
+    weight_ref[...] = landed_ref[:, :depth]
+    for i in range(rows_ref.shape[0]):
+        rows_ref[i] = landed_ref[:, depth:]
+
+
+def unpack(landed, depth, copies):
+    blocks, rows, size = landed.shape
+    return pl.pallas_call(
+        unpack_kernel,
+        in_specs=[pl.BlockSpec(memory_space=pltpu.VMEM)],
+        out_specs=[pl.BlockSpec(memory_space=pltpu.VMEM)] * 2,
+        out_shape=[
+            jax.ShapeDtypeStruct((blocks, depth, size), BF),
+            jax.ShapeDtypeStruct((copies, blocks, rows - depth, size), BF),
+        ],
+        compiler_params=pltpu.CompilerParams(vmem_limit_bytes=60 * 2**20),
+        cost_estimate=pl.CostEstimate(flops=0, bytes_accessed=2**20, transcendentals=0),
+    )(landed)
 
 
 def project_kernel(place_ref, own_ref, other_ref, *refs):
@@ -126,7 +157,7 @@
             scratch_shapes=[pltpu.VMEM((width, columns), BF)],
         ),
         out_shape=jax.ShapeDtypeStruct((2 * rows, columns), BF),
-        compiler_params=pltpu.CompilerParams(vmem_limit_bytes=32 * 2**20),
+        compiler_params=pltpu.CompilerParams(vmem_limit_bytes=60 * 2**20),
         cost_estimate=pl.CostEstimate(flops=0, bytes_accessed=2**20, transcendentals=0),
     )(place, own, other, *slabs)
 
@@ -222,7 +253,7 @@
             pltpu.VMEM((2 * size, latents), BF),
             pltpu.VMEM((2 * size, latents), F32),
         ],
-        compiler_params=pltpu.CompilerParams(vmem_limit_bytes=32 * 2**20),
+        compiler_params=pltpu.CompilerParams(vmem_limit_bytes=56 * 2**20),
         cost_estimate=pl.CostEstimate(
             flops=20 * tokens * latents * size,
             bytes_accessed=6 * 2**20,
@@ -231,40 +262,47 @@
     )(kv, gathered, stats)
 
 
-def tail_kernel(query_ref, latent_ref, every_ref, latent_out, weight_out):
+def tail_kernel(place_ref, query_ref, latent_ref, every_ref, latent_out, mine_out, theirs_out):
+    core = place_ref[0]
     count, rows, width = latent_out.shape
+    weight = dot_nt(latent_ref[...], every_ref[...]).astype(BF)
+    for one, out in enumerate((mine_out, theirs_out)):
+
+        @pl.when(core == 0)
+        def _():
+            out[...] = weight[one * rows : (one + 1) * rows]
+
+        @pl.when(core == 1)
+        def _():
+            out[...] = weight[(1 - one) * rows : (2 - one) * rows]
+
     latent = dot(query_ref[...], every_ref[...]).astype(BF)
-    weight = dot_nt(latent_ref[...], every_ref[...]).astype(BF)
     for i in range(count):
-        core, group = divmod(i, count // 2)
-        latent_out[i] = latent[core * rows : (core + 1) * rows, group * width : (group + 1) * width]
-        weight_out[i] = weight[core * rows : (core + 1) * rows, :]
-
-
-def tail(query, latent, every, tensors, batches):
+        half, group = divmod(i, count // 2)
+        latent_out[i] = latent[half * rows : (half + 1) * rows, group * width : (group + 1) * width]
+
+
+def tail(place, query, latent, every, tensors):
     both, half = query.shape
     rows = both // 2
     latents = latent.shape[1]
     return pl.pallas_call(
         tail_kernel,
-        in_specs=[pl.BlockSpec(memory_space=pltpu.VMEM)] * 3,
-        out_specs=[pl.BlockSpec(memory_space=pltpu.VMEM)] * 2,
+        in_specs=[pl.BlockSpec(memory_space=pltpu.SMEM)]
+        + [pl.BlockSpec(memory_space=pltpu.VMEM)] * 3,
+        out_specs=[pl.BlockSpec(memory_space=pltpu.VMEM)] * 3,
         out_shape=[
             jax.ShapeDtypeStruct((2 * tensors, rows, latents // tensors), BF),
-            jax.ShapeDtypeStruct((2 * batches, rows, half), BF),
+            jax.ShapeDtypeStruct((rows, half), BF),
+            jax.ShapeDtypeStruct((rows, half), BF),
         ],
         compiler_params=pltpu.CompilerParams(vmem_limit_bytes=32 * 2**20),
         cost_estimate=pl.CostEstimate(flops=0, bytes_accessed=2**20, transcendentals=0),
-    )(query, latent, every)
+    )(place, query, latent, every)
 
 
 def exchange(x, axes):
     return lax.all_to_all(x, axes, 0, 0, tiled=True)
-
-
-def spread(x, axes):
-    count = lax.axis_size(axes)
-    return exchange(jnp.broadcast_to(x[None], (count,) + x.shape), axes)
 
 
 def halves(x):
@@ -308,8 +346,10 @@
         place, key_weight, value_weight, queries[0], out_grad[0], attn_out[0], shifted_lse[0].T, 2 * far
     )
     landed = exchange(blocks, ("zh", "core"))
-    slab = lax.all_gather(landed[:, :depth], "zl", axis=0, tiled=True)
-    gathered = spread(landed[:, depth:], "zl").reshape(near, far, 2, -1, size)
+    weight_rows, other_rows = unpack(landed, depth, near)
+    slab = lax.all_gather(weight_rows, "zl", axis=0, tiled=True)
+    slab, other_rows = lax.optimization_barrier((slab, other_rows))
+    gathered = exchange(other_rows, "zl").reshape(near, far, 2, -1, size)
     slab = slab.reshape(near, far, 2 * depth, size)
     slabs = [slab] + [
         lax.ppermute(slab, "dp", [(i, (i + d) % batches) for i in range(batches)])
@@ -333,17 +373,21 @@
     share = exchange(part.reshape(far * near, -1, latents), ("zh", "zl"))
     share = jnp.sum(share.astype(F32), axis=0).astype(BF)
     every = lax.all_gather(share, ("zh", "zl"), axis=0, tiled=True)
-    latent_part, weight_part = tail(
-        query_both, latent_both, every, lax.axis_size("tensor"), batches
+    latent_part, weight_mine, weight_theirs = tail(
+        place, query_both, latent_both, every, lax.axis_size("tensor")
     )
 
     latent_sum = jnp.sum(exchange(latent_part, ("core", "tensor")).astype(F32), axis=0)
     latent_grad = latent_sum.astype(BF).T[None]
 
-    weight_sum = exchange(weight_part, ("core", "dp"))
-    weight_sum = jnp.sum(weight_sum.reshape(2, batches, columns // 8, half).astype(F32), axis=1)
-    weight_factor = 1.0 / math.sqrt(latents * batches)
-    weight_grad = jnp.transpose(weight_sum, (1, 0, 2)).reshape(columns // 8, columns) * weight_factor
+    weight_other = lax.ppermute(weight_theirs, "core", SWAP)
+    weight_rows = jnp.where(
+        first,
+        jnp.concatenate([weight_mine, weight_other], 1),
+        jnp.concatenate([weight_other, weight_mine], 1),
+    )
+    weight_sum = jnp.sum(lax.all_gather(weight_rows, "dp").astype(F32), axis=0)
+    weight_grad = weight_sum * (1.0 / math.sqrt(latents * batches))
     return (whole(0), whole(half), latent_grad, weight_grad)
 
 

time: 228 us -> 217 us (0.952)
  Pallas kernels: 13.2 us -> 23.3 us
  local copies, waits for them, and re-layouts: 11.5 us -> 1.7 us
  waiting for transfers between devices: 43.7 us -> 36.8 us
  starting transfers between devices: 56.8 us -> 51.2 us
  blocking collectives: 99.1 us -> 96.4 us
    all_to_all x4 -> x3, starting transfers between devices: 35.6 us -> 16 us  [exchange(): return lax.all_to_all(x, axes, 0, 0, tiled=True)]
    ppermute x0 -> x1, starting transfers between devices: none -> 14.3 us  [local(): weight_other = lax.ppermute(weight_theirs, 'core', SWAP)]
    all_to_all x4 -> x3, waiting for transfers between devices: 24.9 us -> 15.6 us  [exchange(): return lax.all_to_all(x, axes, 0, 0, tiled=True)]
    unnamed x22 -> x20, local copies, waits for them, and re-layouts: 6.83 us -> 0.84 us
    pallas_call x2 -> x3, Pallas kernels: 1.91 us -> 6.74 us  [the longest x1 2.61 us: pack(): pl.pallas_call(pack_kernel, in_specs=[pl.BlockSpec(memory_space=pltpu.SME...]
    pallas_call x1, Pallas kernels: 3.87 us -> 7.45 us  [project(): pl.pallas_call(project_kernel, grid_spec=pltpu.PrefetchScalarGridSpec(num...]
    slice x2 -> x0, local copies, waits for them, and re-layouts: 2.56 us -> none  [the longest x1 1.57 us: local(): slab = lax.all_gather(landed[:, :depth], 'zl', axis=0, tiled=True)]
    all_gather x1 -> x2, blocking collectives: 31.1 us -> 29.2 us  [the longest x1 18.6 us: local(): slab = lax.all_gather(weight_rows, 'zl', axis=0, tiled=True)]
  transfers between devices with their start and end apart: 10 -> 10, of which waited for: 7 -> 5; matrix products, arithmetic and copies ran while one was open for 2% -> 1% of each run, Pallas kernels for 2% -> 3%
where the time goes in v5:
time: 217 us; the launch traced here: 215 us
  blocking collectives  96.4 us (44%)
  starting transfers between devices  51.2 us (24%)
  waiting for transfers between devices  36.8 us (17%)
  Pallas kernels  23.3 us (11%)
  other arithmetic  4.28 us (2%)
    all_to_all x1, blocking collectives, exchange(): return lax.all_to_all(x, axes, 0, 0, tiled=True)  39.2 us
    all_gather x1, blocking collectives, local(): every = lax.all_gather(share, ('zh', 'zl'), axis=0, tiled=True)  28.1 us
    ppermute x3, waiting for transfers between devices, local(): lax.ppermute(slab, 'dp', [(i, (i + d) % batches) for i in range(batches)])  19.5 us
    all_gather x1, blocking collectives, local(): slab = lax.all_gather(weight_rows, 'zl', axis=0, tiled=True)  18.6 us
    all_to_all x3, starting transfers between devices, exchange(): return lax.all_to_all(x, axes, 0, 0, tiled=True)  16 us
    all_to_all x3, waiting for transfers between devices, exchange(): return lax.all_to_all(x, axes, 0, 0, tiled=True)  15.6 us
    ppermute x1, starting transfers between devices, local(): weight_other = lax.ppermute(weight_theirs, 'core', SWAP)  14.3 us
    ppermute x3, starting transfers between devices, local(): lax.ppermute(slab, 'dp', [(i, (i + d) % batches) for i in range(batches)])  10.7 us
  transfers between devices with their start and end apart: 10, of which 5 were waited for; matrix products, arithmetic and copies ran while one was open for 1% of the time, Pallas kernels for 3%

profile of v5, /device:TPU:1, one launch (start us, length us, event | category | flops | bytes accessed | tf_op | source)
XLA Modules:
  0.0 214.6 jit_solution(11257739960460289358)
XLA Ops:
  0.6 0.7 pad_add_fusion.place_ref
  1.3 2.6 %shard_map.120 = bf16[8,208,128]{2,1,0:T(8,128)(2,1)} custom-call(s32[3]{0:T(128)} %pad_add_fusion.place_ref, bf16[64,512]{1,0:T(8,128)(2,1)} %refs_0_.1, bf16[64,512]{1,0:T(8,128)(2,1)} %refs_1_.1, bf16[32,512]{1,0:T(8,128)(2,1)} %bitcast.54, bf16[32,512]{1,0:T(8,128)(2,1)} %bitcast.55, bf16[32,512]{1,0:T(8,128)(2,1)} %bitcast.56, f32[4,32]{1,0:T(4,128)} %bitcast.59), custom_call_target="tpu_custom_call" | custom-call | bytes 524288 | tf_op jit(solution)/shard_map/pallas_call | solution.py:79
  3.9 39.2 %all_to_all.20.landed_ref = bf16[8,208,128]{2,1,0:T(8,128)(2,1)} all-to-all(bf16[8,208,128]{2,1,0:T(8,128)(2,1)} %shard_map.120), channel_id=1, replica_groups=mesh['zh'=4,'zl'=4,'core'=2,'tensor'=4,'dp'=4] {'zh','core'}, dimensions={0} | all-to-all | bytes 851968 | tf_op jit(solution)/shard_map/all_to_all | solution.py:305
  43.1 2.2 %shard_map.121 = (bf16[8,64,128]{2,1,0:T(8,128)(2,1)}, bf16[4,8,144,128]{3,2,1,0:T(8,128)(2,1)}) custom-call(bf16[8,208,128]{2,1,0:T(8,128)(2,1)} %all_to_all.20.landed_ref), custom_call_target="tpu_custom_call" | custom-call | bytes 1048576 | tf_op jit(solution)/shard_map/pallas_call | solution.py:101
  45.3 18.6 %all_gather.10 = bf16[32,64,128]{2,1,0:T(8,128)(2,1)S(1)} all-gather(bf16[8,64,128]{2,1,0:T(8,128)(2,1)} %get-tuple-element.14), channel_id=1, replica_groups=mesh['zh'=4,'zl'=4,'core'=2,'tensor'=4,'dp'=4] {'zl'}, dimensions={0}, use_global_device_ids=true | all-gather | bytes 655360 | tf_op jit(solution)/shard_map/all_gather | solution.py:350
  63.9 4.5 %all-to-all-start.1 = ((bf16[4,8,144,128]{3,2,1,0:T(8,128)(2,1)}), bf16[4,8,144,128]{3,2,1,0:T(8,128)(2,1)}, u32[]{:S(2)}, u32[]{:S(2)}) async-start(bf16[4,8,144,128]{3,2,1,0:T(8,128)(2,1)} %get-tuple-element.17), calls=%async_computation.1 | async-start | bytes 2359296 | tf_op jit(solution)/shard_map/all_to_all | solution.py:305
  68.5 5.0 %collective-permute-start = (bf16[512,2048]{1,0:T(8,128)(2,1)S(1)}, bf16[512,2048]{1,0:T(8,128)(2,1)}, u32[]{:S(2)}, u32[]{:S(2)}) collective-permute-start(bf16[512,2048]{1,0:T(8,128)(2,1)S(1)} %bitcast.44), channel_id=1, source_target_pairs={{0,16},{16,0},{1,17},{17,1},{2,18},{18,2},{3,19},{19,3},{4,20},{20... | collective-permute-start | bytes 6291464 | tf_op jit(solution)/shard_map/ppermute | solution.py:327
  73.5 3.2 %collective-permute-start.1 = (bf16[4,4,128,128]{3,2,1,0:T(8,128)(2,1)S(1)}, bf16[4,4,128,128]{3,2,1,0:T(8,128)(2,1)S(1)}, u32[]{:S(2)}, u32[]{:S(2)}) collective-permute-start(bf16[4,4,128,128]{3,2,1,0:T(8,128)(2,1)S(1)} %bitcast.45), channel_id=1, source_target_pairs={{0,1},{1,2},{2,3},{3,0},{4,5},{5,6},{6,7},{7,4},{8,9},{9,10},{10,1... | collective-permute-start | bytes 1572872 | tf_op jit(solution)/shard_map/ppermute | solution.py:355
  76.7 4.5 %collective-permute-start.2 = (bf16[4,4,128,128]{3,2,1,0:T(8,128)(2,1)S(1)}, bf16[4,4,128,128]{3,2,1,0:T(8,128)(2,1)S(1)}, u32[]{:S(2)}, u32[]{:S(2)}) collective-permute-start(bf16[4,4,128,128]{3,2,1,0:T(8,128)(2,1)S(1)} %bitcast.46), channel_id=1, source_target_pairs={{0,2},{1,3},{2,0},{3,1},{4,6},{5,7},{6,4},{7,5},{8,10},{9,11},{10,... | collective-permute-start | bytes 1572872 | tf_op jit(solution)/shard_map/ppermute | solution.py:355
  81.3 3.0 %collective-permute-start.3 = (bf16[4,4,128,128]{3,2,1,0:T(8,128)(2,1)S(1)}, bf16[4,4,128,128]{3,2,1,0:T(8,128)(2,1)S(1)}, u32[]{:S(2)}, u32[]{:S(2)}) collective-permute-start(bf16[4,4,128,128]{3,2,1,0:T(8,128)(2,1)S(1)} %bitcast.47), channel_id=1, source_target_pairs={{0,3},{1,0},{2,1},{3,2},{4,7},{5,4},{6,5},{7,6},{8,11},{9,8},{10,9... | collective-permute-start | bytes 1572872 | tf_op jit(solution)/shard_map/ppermute | solution.py:355
  84.3 6.1 %collective-permute-done.1.refs_1_ = bf16[4,4,128,128]{3,2,1,0:T(8,128)(2,1)S(1)} collective-permute-done((bf16[4,4,128,128]{3,2,1,0:T(8,128)(2,1)S(1)}, bf16[4,4,128,128]{3,2,1,0:T(8,128)(2,1)S(1)}, u32[]{:S(2)}, u32[]{:S(2)}) %collective-permute-start.1) | collective-permute-done | bytes 524320 | tf_op jit(solution)/shard_map/ppermute | solution.py:355
  90.3 12.3 %collective-permute-done.2.refs_2_ = bf16[4,4,128,128]{3,2,1,0:T(8,128)(2,1)S(1)} collective-permute-done((bf16[4,4,128,128]{3,2,1,0:T(8,128)(2,1)S(1)}, bf16[4,4,128,128]{3,2,1,0:T(8,128)(2,1)S(1)}, u32[]{:S(2)}, u32[]{:S(2)}) %collective-permute-start.2) | collective-permute-done | bytes 524320 | tf_op jit(solution)/shard_map/ppermute | solution.py:355
  102.6 1.1 collective-permute-done.3.refs_3_
  103.8 0.8 copy-done.7
  104.6 7.5 %shard_map.122.kv_ref = bf16[1024,512]{1,0:T(8,128)(2,1)} custom-call(s32[3]{0:T(128)} %pad_add_fusion.place_ref, bf16[512,2048]{1,0:T(8,128)(2,1)} %bitcast.43, bf16[512,2048]{1,0:T(8,128)(2,1)} %collective-permute-done.other_ref, bf16[4,4,128,128]{3,2,1,0:T(8,128)(2,1)} %bitcast.48, bf16[4,4,128,128]{3,2,1,0:T(8,128)(2,1)} %copy-done.5, ...), custom_call_target="tpu_custom_call" | custom-call | bytes 1048576 | tf_op jit(solution)/shard_map/pallas_call | solution.py:146
  112.0 0.9 slice_convert_fusion
  113.0 0.7 reshape.194.stat_ref
  113.7 9.1 %shard_map.123 = (bf16[512,512]{1,0:T(8,128)(2,1)}, bf16[512,512]{1,0:T(8,128)(2,1)}, bf16[256,1024]{1,0:T(8,128)(2,1)}) custom-call(bf16[1024,512]{1,0:T(8,128)(2,1)} %shard_map.122.kv_ref, bf16[4,4,2,144,128]{4,3,2,1,0:T(8,128)(2,1)} %bitcast.10.rows_ref, f32[4,1024]{1,0:T(4,128)} %reshape.194.stat_ref), custom_call_target="tpu_custom_call" | custom-call | flops 2684354560 | bytes 6291456 | tf_op jit(solution)/shard_map/pallas_call | solution.py:231
  122.8 7.1 %all-to-all-start.2 = ((bf16[16,16,1024]{2,1,0:T(8,128)(2,1)}), bf16[16,16,1024]{2,1,0:T(8,128)(2,1)S(1)}, u32[]{:S(2)}, u32[]{:S(2)}) async-start(bf16[16,16,1024]{2,1,0:T(8,128)(2,1)} %bitcast.51), calls=%async_computation.2 | async-start | bytes 1048576 | tf_op jit(solution)/shard_map/all_to_all | solution.py:305
  130.0 3.2 %collective-permute-start.5 = (bf16[64,1280]{1,0:T(8,128)(2,1)S(1)}, bf16[64,1280]{1,0:T(8,128)(2,1)S(1)}, u32[]{:S(2)}, u32[]{:S(2)}) collective-permute-start(bf16[64,1280]{1,0:T(8,128)(2,1)S(1)} %pad_maximum_fusion), channel_id=1, source_target_pairs={{0,16},{16,0},{1,17},{17,1},{2,18},{18,2},{3,19},{19,3},{4,20},{20... | collective-permute-start | bytes 491528 | tf_op jit(solution)/shard_map/ppermute | solution.py:332
  133.2 1.9 collective-permute-start.4
  135.3 1.7 collective-permute-done.4
  137.1 15.6 %all-to-all-done.2 = bf16[16,16,1024]{2,1,0:T(8,128)(2,1)S(1)} async-done(((bf16[16,16,1024]{2,1,0:T(8,128)(2,1)}), bf16[16,16,1024]{2,1,0:T(8,128)(2,1)S(1)}, u32[]{:S(2)}, u32[]{:S(2)}) %all-to-all-start.2) | async-done | bytes 524320 | tf_op jit(solution)/shard_map/all_to_all | solution.py:305
  152.7 0.1 reduce_sum.33
  152.8 28.1 %all_gather.11.every_ref = bf16[256,1024]{1,0:T(8,128)(2,1)S(1)} all-gather(bf16[16,1024]{1,0:T(8,128)(2,1)S(1)} %reduce_sum.33), channel_id=1, replica_groups=mesh['zh'=4,'zl'=4,'core'=2,'tensor'=4,'dp'=4] {'zh','zl'}, dimensions={0}, use_global_device_ids=true | all-gather | bytes 557056 | tf_op jit(solution)/shard_map/all_gather | solution.py:375
  180.9 1.9 shard_map.124
  182.8 14.3 %collective-permute-start.6 = (bf16[64,256]{1,0:T(8,128)(2,1)S(1)}, bf16[64,256]{1,0:T(8,128)(2,1)S(1)}, u32[]{:S(2)}, u32[]{:S(2)}) collective-permute-start(bf16[64,256]{1,0:T(8,128)(2,1)S(1)} %get-tuple-element.23), channel_id=1, source_target_pairs={{0,16},{16,0},{1,17},{17,1},{2,18},{18,2},{3,19},{19,3},{4,20},{20... | collective-permute-start | bytes 98312 | tf_op jit(solution)/shard_map/ppermute | solution.py:383
  197.0 1.2 maximum_select_fusion
  198.2 4.4 %all-to-all-start.3 = ((bf16[8,64,256]{2,1,0:T(8,128)(2,1)}), bf16[8,64,256]{2,1,0:T(8,128)(2,1)S(1)}, u32[]{:S(2)}, u32[]{:S(2)}) async-start(bf16[8,64,256]{2,1,0:T(8,128)(2,1)} %get-tuple-element.21), calls=%async_computation.3 | async-start | bytes 524288 | tf_op jit(solution)/shard_map/all_to_all | solution.py:305
  202.7 10.6 %all_gather.12 = bf16[4,64,512]{2,1,0:T(8,128)(2,1)S(1)} all-gather(bf16[1,64,512]{2,1,0:T(8,128)(2,1)S(1)} %maximum_select_fusion.4), channel_id=1, replica_groups=mesh['zh'=4,'zl'=4,'core'=2,'tensor'=4,'dp'=4] {'dp'}, dimensions={0}, use_global_device_ids=true | all-gather | bytes 327680 | tf_op jit(solution)/shard_map/all_gather | solution.py:389
  213.3 0.7 broadcast_multiply_fusion
  213.9 0.7 reduce_sum.34
  (37 shorter events, 0.3 us)
Async XLA Ops:
  63.9 17.4 %copy-start.2 = (bf16[32,64,128]{2,1,0:T(8,128)(2,1)}, bf16[32,64,128]{2,1,0:T(8,128)(2,1)S(1)}, u32[]{:S(2)}) copy-start(bf16[32,64,128]{2,1,0:T(8,128)(2,1)S(1)} %all_gather.10) | copy-start | bytes 1572868
  63.9 4.5 %copy-start.1 = (bf16[1,512,2048]{2,1,0:T(8,128)(2,1)S(1)}, bf16[1,512,2048]{2,1,0:T(8,128)(2,1)}, u32[]{:S(2)}) copy-start(bf16[1,512,2048]{2,1,0:T(8,128)(2,1)} %param.9) | copy-start | bytes 6291460
  63.9 48.1 %all-to-all-start.1 = ((bf16[4,8,144,128]{3,2,1,0:T(8,128)(2,1)}), bf16[4,8,144,128]{3,2,1,0:T(8,128)(2,1)}, u32[]{:S(2)}, u32[]{:S(2)}) async-start(bf16[4,8,144,128]{3,2,1,0:T(8,128)(2,1)} %get-tuple-element.17), calls=%async_computation.1 | async-start | bytes 2359296 | tf_op jit(solution)/shard_map/all_to_all | solution.py:305
  68.5 36.1 %collective-permute-start = (bf16[512,2048]{1,0:T(8,128)(2,1)S(1)}, bf16[512,2048]{1,0:T(8,128)(2,1)}, u32[]{:S(2)}, u32[]{:S(2)}) collective-permute-start(bf16[512,2048]{1,0:T(8,128)(2,1)S(1)} %bitcast.44), channel_id=1, source_target_pairs={{0,16},{16,0},{1,17},{17,1},{2,18},{18,2},{3,19},{19,3},{4,20},{20... | collective-permute-start | bytes 6291464 | tf_op jit(solution)/shard_map/ppermute | solution.py:327
  73.5 16.8 %collective-permute-start.1 = (bf16[4,4,128,128]{3,2,1,0:T(8,128)(2,1)S(1)}, bf16[4,4,128,128]{3,2,1,0:T(8,128)(2,1)S(1)}, u32[]{:S(2)}, u32[]{:S(2)}) collective-permute-start(bf16[4,4,128,128]{3,2,1,0:T(8,128)(2,1)S(1)} %bitcast.45), channel_id=1, source_target_pairs={{0,1},{1,2},{2,3},{3,0},{4,5},{5,6},{6,7},{7,4},{8,9},{9,10},{10,1... | collective-permute-start | bytes 1572872 | tf_op jit(solution)/shard_map/ppermute | solution.py:355
  76.7 25.9 %collective-permute-start.2 = (bf16[4,4,128,128]{3,2,1,0:T(8,128)(2,1)S(1)}, bf16[4,4,128,128]{3,2,1,0:T(8,128)(2,1)S(1)}, u32[]{:S(2)}, u32[]{:S(2)}) collective-permute-start(bf16[4,4,128,128]{3,2,1,0:T(8,128)(2,1)S(1)} %bitcast.46), channel_id=1, source_target_pairs={{0,2},{1,3},{2,0},{3,1},{4,6},{5,7},{6,4},{7,5},{8,10},{9,11},{10,... | collective-permute-start | bytes 1572872 | tf_op jit(solution)/shard_map/ppermute | solution.py:355
  81.3 22.5 %collective-permute-start.3 = (bf16[4,4,128,128]{3,2,1,0:T(8,128)(2,1)S(1)}, bf16[4,4,128,128]{3,2,1,0:T(8,128)(2,1)S(1)}, u32[]{:S(2)}, u32[]{:S(2)}) collective-permute-start(bf16[4,4,128,128]{3,2,1,0:T(8,128)(2,1)S(1)} %bitcast.47), channel_id=1, source_target_pairs={{0,3},{1,0},{2,1},{3,2},{4,7},{5,4},{6,5},{7,6},{8,11},{9,8},{10,9... | collective-permute-start | bytes 1572872 | tf_op jit(solution)/shard_map/ppermute | solution.py:355
  90.3 14.3 %copy-start.5 = (bf16[4,4,128,128]{3,2,1,0:T(8,128)(2,1)}, bf16[4,4,128,128]{3,2,1,0:T(8,128)(2,1)S(1)}, u32[]{:S(2)}) copy-start(bf16[4,4,128,128]{3,2,1,0:T(8,128)(2,1)S(1)} %collective-permute-done.1.refs_1_) | copy-start | bytes 1572868
  102.6 1.9 copy-start.6
  103.8 0.8 copy-start.7
  113.7 16.2 %copy-start.8 = (bf16[64,512]{1,0:T(8,128)(2,1)S(1)}, bf16[64,512]{1,0:T(8,128)(2,1)}, u32[]{:S(2)}) copy-start(bf16[64,512]{1,0:T(8,128)(2,1)} %param.12) | copy-start | bytes 196612
  122.8 7.2 %copy-start.3 = (bf16[1,1024,64]{1,2,0:T(8,128)(2,1)S(1)}, bf16[1,1024,64]{1,2,0:T(8,128)(2,1)}, u32[]{:S(2)}) copy-start(bf16[1,1024,64]{1,2,0:T(8,128)(2,1)} %param.17) | copy-start | bytes 393220
  122.8 10.4 %copy-start.9 = (bf16[512,512]{1,0:T(8,128)(2,1)S(1)}, bf16[512,512]{1,0:T(8,128)(2,1)}, u32[]{:S(2)}) copy-start(bf16[512,512]{1,0:T(8,128)(2,1)} %get-tuple-element.19) | copy-start | bytes 1572868
  122.8 12.5 %copy-start.4 = (bf16[512,512]{1,0:T(8,128)(2,1)S(1)}, bf16[512,512]{1,0:T(8,128)(2,1)}, u32[]{:S(2)}) copy-start(bf16[512,512]{1,0:T(8,128)(2,1)} %get-tuple-element.18) | copy-start | bytes 1572868
  122.8 29.9 %all-to-all-start.2 = ((bf16[16,16,1024]{2,1,0:T(8,128)(2,1)}), bf16[16,16,1024]{2,1,0:T(8,128)(2,1)S(1)}, u32[]{:S(2)}, u32[]{:S(2)}) async-start(bf16[16,16,1024]{2,1,0:T(8,128)(2,1)} %bitcast.51), calls=%async_computation.2 | async-start | bytes 1048576 | tf_op jit(solution)/shard_map/all_to_all | solution.py:305
  130.0 5.2 %collective-permute-start.5 = (bf16[64,1280]{1,0:T(8,128)(2,1)S(1)}, bf16[64,1280]{1,0:T(8,128)(2,1)S(1)}, u32[]{:S(2)}, u32[]{:S(2)}) collective-permute-start(bf16[64,1280]{1,0:T(8,128)(2,1)S(1)} %pad_maximum_fusion), channel_id=1, source_target_pairs={{0,16},{16,0},{1,17},{17,1},{2,18},{18,2},{3,19},{19,3},{4,20},{20... | collective-permute-start | bytes 491528 | tf_op jit(solution)/shard_map/ppermute | solution.py:332
  133.2 3.8 %collective-permute-start.4 = (bf16[512,512]{1,0:T(8,128)(2,1)S(1)}, bf16[512,512]{1,0:T(8,128)(2,1)S(1)}, u32[]{:S(2)}, u32[]{:S(2)}) collective-permute-start(bf16[512,512]{1,0:T(8,128)(2,1)S(1)} %copy-done.9), channel_id=1, source_target_pairs={{0,16},{16,0},{1,17},{17,1},{2,18},{18,2},{3,19},{19,3},{4,20},{20... | collective-permute-start | bytes 1572872 | tf_op jit(solution)/shard_map/ppermute | solution.py:364
  135.3 45.5 %copy-start = (s32[3]{0:T(128)S(1)}, s32[3]{0:T(128)}, u32[]{:S(2)}) copy-start(s32[3]{0:T(128)} %pad_add_fusion.place_ref) | copy-start | bytes 40
  182.8 19.9 %collective-permute-start.6 = (bf16[64,256]{1,0:T(8,128)(2,1)S(1)}, bf16[64,256]{1,0:T(8,128)(2,1)S(1)}, u32[]{:S(2)}, u32[]{:S(2)}) collective-permute-start(bf16[64,256]{1,0:T(8,128)(2,1)S(1)} %get-tuple-element.23), channel_id=1, source_target_pairs={{0,16},{16,0},{1,17},{17,1},{2,18},{18,2},{3,19},{19,3},{4,20},{20... | collective-permute-start | bytes 98312 | tf_op jit(solution)/shard_map/ppermute | solution.py:383
  198.2 15.7 %all-to-all-start.3 = ((bf16[8,64,256]{2,1,0:T(8,128)(2,1)}), bf16[8,64,256]{2,1,0:T(8,128)(2,1)S(1)}, u32[]{:S(2)}, u32[]{:S(2)}) async-start(bf16[8,64,256]{2,1,0:T(8,128)(2,1)} %get-tuple-element.21), calls=%async_computation.3 | async-start | bytes 524288 | tf_op jit(solution)/shard_map/all_to_all | solution.py:305

commit v6 on v4

v6 whole, which is shorter than its diff:
```python
import functools
import math

import jax
import jax.numpy as jnp
from jax import lax
from jax.experimental import pallas as pl
from jax.experimental.pallas import tpu as pltpu
from jax.sharding import Mesh, PartitionSpec as P

BF = jnp.bfloat16
F32 = jnp.float32
SEQ = ("zh", "zl", "core")
Z = ("zh", "zl")
SWAP = [(0, 1), (1, 0)]


def dot(a, b):
    return jnp.dot(a, b, preferred_element_type=F32)


def dot_nt(a, b):
    return lax.dot_general(a, b, (((1,), (1,)), ((), ())), preferred_element_type=F32)


def pack_kernel(place_ref, *refs):
    sources, block_ref, landing, arrived = refs[:6], refs[6], refs[7:13], refs[13]
    copies = [
        pltpu.make_async_copy(source, target, arrived.at[i])
        for i, (source, target) in enumerate(zip(sources, landing))
    ]
    for copy in copies:
        copy.start()
    for copy in copies:
        copy.wait()
    key_ref, value_ref, query_ref, grad_ref, out_ref, lse_ref = landing
    batch = place_ref[2]
    depth, columns = key_ref.shape
    rows = query_ref.shape[0]
    size = block_ref.shape[2]
    heads = columns // size
    half = columns // 2
    product = grad_ref[...].astype(F32) * out_ref[...].astype(F32)
    lane = lax.broadcasted_iota(jnp.int32, (rows, size), 1)
    delta = jnp.zeros((rows, size), F32)
    for head in range(heads):
        one = jnp.sum(product[:, head * size : (head + 1) * size], axis=1, keepdims=True)
        delta = jnp.where(lane == head, one, delta)
    lse, delta = lse_ref[...], delta.T[:heads]
    for core in range(2):
        column = pl.multiple_of(core * half + lax.rem(batch, 2) * size, size)
        mine = slice(core * heads // 2, (core + 1) * heads // 2)
        exact = jnp.concatenate([lse[mine], delta[mine]], axis=0)
        high = exact.astype(BF).astype(F32)
        stats = jnp.concatenate([high, exact - high], axis=0).astype(BF)

        @pl.when(batch < 2)
        def _():
            block_ref[core, :depth] = key_ref[:, pl.ds(column, size)]

        @pl.when(batch >= 2)
        def _():
            block_ref[core, :depth] = value_ref[:, pl.ds(column, size)]

        first = depth
        for ref in (query_ref, grad_ref):
            for lo in range(core * half, (core + 1) * half, size):
                block_ref[core, first : first + rows] = ref[:, lo : lo + size]
                first += rows
                if first == depth + rows:
                    block_ref[core, first : first + 16] = jnp.zeros((16, size), BF)
                    block_ref[core, first : first + 2 * heads, :rows] = stats
                    first += 16


def pack(place, key_weight, value_weight, query, grad, out, lse):
    depth, columns = key_weight.shape
    size = columns // lse.shape[0]
    sources = (key_weight, value_weight, query, grad, out, lse)
    return pl.pallas_call(
        pack_kernel,
        in_specs=[pl.BlockSpec(memory_space=pltpu.SMEM)]
        + [pl.BlockSpec(memory_space=pltpu.HBM)] * len(sources),
        out_specs=pl.BlockSpec(memory_space=pltpu.VMEM),
        out_shape=jax.ShapeDtypeStruct((2, depth + 16 + 4 * query.shape[0], size), BF),
        scratch_shapes=[pltpu.VMEM(x.shape, x.dtype) for x in sources]
        + [pltpu.SemaphoreType.DMA((len(sources),))],
        compiler_params=pltpu.CompilerParams(vmem_limit_bytes=60 * 2**20),
        cost_estimate=pl.CostEstimate(flops=0, bytes_accessed=2**19, transcendentals=0),
    )(place, *sources)


def project_kernel(own_ref, other_ref, slab_ref, out_ref, weight):
    step = pl.program_id(0)
    half = pl.num_programs(0) // 2
    slabs, _, size = slab_ref.shape

    @pl.when(step == 0)
    def _():
        for slab in range(slabs):
            weight[:, slab * size : (slab + 1) * size] = slab_ref[slab]

    @pl.when(step < half)
    def _():
        out_ref[...] = dot(own_ref[...], weight[...]).astype(BF)

    @pl.when(step >= half)
    def _():
        out_ref[...] = dot(other_ref[...], weight[...]).astype(BF)


def project(own, other, slabs):
    rows, width = own.shape
    columns = slabs.shape[0] * slabs.shape[2]
    block = 256
    half = rows // block
    return pl.pallas_call(
        project_kernel,
        grid=(2 * half,),
        in_specs=[
            pl.BlockSpec((block, width), lambda t: (jnp.minimum(t, half - 1), 0)),
            pl.BlockSpec((block, width), lambda t: (jnp.maximum(t - half, 0), 0)),
            pl.BlockSpec(slabs.shape, lambda t: (0, 0, 0)),
        ],
        out_specs=pl.BlockSpec((block, columns), lambda t: (t, 0)),
        out_shape=jax.ShapeDtypeStruct((2 * rows, columns), BF),
        scratch_shapes=[pltpu.VMEM((width, columns), BF)],
        compiler_params=pltpu.CompilerParams(vmem_limit_bytes=32 * 2**20),
        cost_estimate=pl.CostEstimate(flops=0, bytes_accessed=2**20, transcendentals=0),
    )(own, other, slabs)


def attend_kernel(
    kv_ref, head_ref, stat_ref, rest_ref, own_ref, other_ref, part_ref, query, grad, qt, gt, pieces, stats, total,
    size, scaling, latent_factor, prefix_factor,
):
    step = pl.program_id(0)
    last = pl.num_programs(0) - 1
    half = pl.num_programs(0) // 2
    ranks = head_ref.shape[0]
    rows = query.shape[0] // ranks

    @pl.when(step == 0)
    def _():
        for rank in range(ranks):
            here = slice(rank * rows, (rank + 1) * rows)
            query[here, :size] = head_ref[rank]
            query[here, size:] = rest_ref[rank, :rows]
            grad[here, :size] = rest_ref[rank, rows : 2 * rows]
            grad[here, size:] = rest_ref[rank, 2 * rows :]
            pieces[:, here] = stat_ref[rank].astype(F32)[:8, :rows]
        stats[...] = pieces[:4] + pieces[4:]
        qt[...] = query[...].T
        gt[...] = grad[...].T
        total[...] = jnp.zeros_like(total)

    key_out, value_out = [], []
    for head in range(2):
        cols = slice(head * size, (head + 1) * size)
        keys = kv_ref[:, cols]
        values = kv_ref[:, (2 + head) * size : (3 + head) * size]
        scores = dot(keys, qt[cols, :]) * scaling
        weights = jnp.exp(scores - stats[head : head + 1, :])
        probs = dot(values, gt[cols, :])
        score_grad = (weights * (probs - stats[2 + head : 3 + head, :])).astype(BF)
        value_out.append(dot(weights.astype(BF), grad[:, cols]) * latent_factor)
        key_out.append(dot(score_grad, query[:, cols]) * (scaling * latent_factor))
        total[cols, :] += dot(keys.T, score_grad)
    result = jnp.concatenate(key_out + value_out, axis=1).astype(BF)

    @pl.when(step < half)
    def _():
        own_ref[...] = result

    @pl.when(step >= half)
    def _():
        other_ref[...] = result

    @pl.when(step == last)
    def _():
        part_ref[...] = (total[...] * (scaling * prefix_factor)).astype(BF)


def attend(kv, first_rows, last_rows, latents, prefix_count):
    tokens, columns = kv.shape
    ranks = first_rows.shape[0]
    rows = latents // ranks
    depth = first_rows.shape[1] - 16 - rows
    size = columns // 4
    block = 256
    half = tokens // block // 2
    kernel = functools.partial(
        attend_kernel,
        size=size,
        scaling=1.0 / math.sqrt(size),
        latent_factor=1.0 / math.sqrt(latents),
        prefix_factor=1.0 / math.sqrt(prefix_count),
    )
    return pl.pallas_call(
        kernel,
        grid=(tokens // block,),
        in_specs=[
            pl.BlockSpec((block, columns), lambda t: (t, 0)),
            pl.BlockSpec((ranks, rows, size), lambda t: (0, depth // rows, 0)),
            pl.BlockSpec((ranks, 16, size), lambda t: (0, (depth + rows) // 16, 0)),
            pl.BlockSpec(last_rows.shape, lambda t: (0, 0, 0)),
        ],
        out_specs=[
            pl.BlockSpec((block, columns), lambda t: (jnp.minimum(t, half - 1), 0)),
            pl.BlockSpec((block, columns), lambda t: (jnp.maximum(t - half, 0), 0)),
            pl.BlockSpec((2 * size, latents), lambda t: (0, 0)),
        ],
        out_shape=[
            jax.ShapeDtypeStruct((tokens // 2, columns), BF),
            jax.ShapeDtypeStruct((tokens // 2, columns), BF),
            jax.ShapeDtypeStruct((2 * size, latents), BF),
        ],
        scratch_shapes=[
            pltpu.VMEM((latents, 2 * size), BF),
            pltpu.VMEM((latents, 2 * size), BF),
            pltpu.VMEM((2 * size, latents), BF),
            pltpu.VMEM((2 * size, latents), BF),
            pltpu.VMEM((8, latents), F32),
            pltpu.VMEM((4, latents), F32),
            pltpu.VMEM((2 * size, latents), F32),
        ],
        compiler_params=pltpu.CompilerParams(vmem_limit_bytes=56 * 2**20),
        cost_estimate=pl.CostEstimate(
            flops=20 * tokens * latents * size,
            bytes_accessed=6 * 2**20,
            transcendentals=2 * tokens * latents,
        ),
    )(kv, first_rows, first_rows, last_rows)


def tail_kernel(query_ref, latent_ref, every_ref, latent_out, weight_out):
    count, rows, width = latent_out.shape
    weight_out[...] = dot_nt(latent_ref[...], every_ref[...]).astype(BF)
    latent = dot(query_ref[...], every_ref[...]).astype(BF)
    for i in range(count):
        half, group = divmod(i, count // 2)
        latent_out[i] = latent[half * rows : (half + 1) * rows, group * width : (group + 1) * width]


def tail(query, latent, every, tensors):
    both, half = query.shape
    latents = latent.shape[1]
    return pl.pallas_call(
        tail_kernel,
        in_specs=[pl.BlockSpec(memory_space=pltpu.VMEM)] * 3,
        out_specs=[pl.BlockSpec(memory_space=pltpu.VMEM)] * 2,
        out_shape=[
            jax.ShapeDtypeStruct((2 * tensors, both // 2, latents // tensors), BF),
            jax.ShapeDtypeStruct((both, half), BF),
        ],
        compiler_params=pltpu.CompilerParams(vmem_limit_bytes=32 * 2**20),
        cost_estimate=pl.CostEstimate(flops=0, bytes_accessed=2**20, transcendentals=0),
    )(query, latent, every)


def total_kernel(place_ref, part_ref, out_ref, *, factor):
    rows = out_ref.shape[0]
    here = pl.ds(pl.multiple_of(place_ref[0] * rows, rows), rows)
    count, _, width = part_ref.shape
    for half in range(2):
        parts = [part_ref[i, here, :].astype(F32) for i in range(half * count // 2, (half + 1) * count // 2)]
        out_ref[:, half * width : (half + 1) * width] = sum(parts[1:], parts[0]) * factor


def total(place, parts, factor):
    _, rows, width = parts.shape
    return pl.pallas_call(
        functools.partial(total_kernel, factor=factor),
        in_specs=[pl.BlockSpec(memory_space=pltpu.SMEM), pl.BlockSpec(memory_space=pltpu.VMEM)],
        out_specs=pl.BlockSpec(memory_space=pltpu.VMEM),
        out_shape=jax.ShapeDtypeStruct((rows // 2, 2 * width), F32),
        compiler_params=pltpu.CompilerParams(vmem_limit_bytes=32 * 2**20),
        cost_estimate=pl.CostEstimate(flops=0, bytes_accessed=2**10, transcendentals=0),
    )(place, parts)


def exchange(x, axes):
    return lax.all_to_all(x, axes, 0, 0, tiled=True)


def halves(x):
    return jnp.transpose(x.reshape(x.shape[0], 2, x.shape[1] // 2), (1, 0, 2))


def local(
    prefix, key_weight, value_weight, query_weight, queries, out_grad, attn_out, shifted_lse, latent_in
):
    core = lax.axis_index("core")
    batch = lax.axis_index("dp")
    first = core == 0
    ranks = lax.axis_size(SEQ)
    batches = lax.axis_size("dp")
    tokens_in = prefix[0]
    token_count = tokens_in.shape[0]
    rows, columns = queries.shape[1:]
    heads = shifted_lse.shape[2]
    size = columns // heads
    latents = rows * ranks

    other_tokens = lax.ppermute(tokens_in, "core", SWAP)
    latent_own = latent_in[0].T
    query_halves = halves(query_weight)
    query_mine = jnp.where(first, query_halves[0], query_halves[1])
    query_theirs = jnp.where(first, query_halves[1], query_halves[0])
    swapped = lax.ppermute(jnp.concatenate([latent_own, query_theirs], axis=1), "core", SWAP)
    latent_other, query_other = swapped[:, :latents], swapped[:, latents:]

    def in_order(own, other):
        return jnp.where(first, jnp.concatenate([own, other], 0), jnp.concatenate([other, own], 0))

    latent_both = in_order(latent_own, latent_other)
    query_both = in_order(query_mine, query_other)

    depth = key_weight.shape[0]
    place = jnp.stack([core, lax.axis_index("zl"), batch]).astype(jnp.int32)
    blocks = exchange(
        pack(place, key_weight, value_weight, queries[0], out_grad[0], attn_out[0], shifted_lse[0].T), "core"
    )
    cut = depth + 16 + rows
    first_rows = lax.all_gather(blocks[:, :cut], Z, axis=0, tiled=True)
    slab = first_rows[:, :depth].reshape(-1, size)
    slabs = jnp.broadcast_to(slab[None], (batches,) + slab.shape)
    slabs, rest = lax.optimization_barrier((slabs, blocks[:, cut:]))
    slabs = exchange(slabs, "dp")
    last_rows = lax.all_gather(rest, Z, axis=0, tiled=True)

    kv = project(tokens_in, other_tokens, slabs)
    own_grads, other_grads, part = attend(kv, first_rows, last_rows, latents, token_count * ranks)
    theirs = lax.ppermute(other_grads, "core", SWAP)
    half = columns // 2

    def whole(lo):
        mine, other = own_grads[:, lo : lo + half], theirs[:, lo : lo + half]
        return jnp.where(
            first, jnp.concatenate([mine, other], 1), jnp.concatenate([other, mine], 1)
        )[None]

    share = exchange(part.reshape(lax.axis_size(Z), -1, latents), Z)
    share = jnp.sum(share.astype(F32), axis=0).astype(BF)
    every = lax.all_gather(share, Z, axis=0, tiled=True)
    latent_part, weight_part = tail(query_both, latent_both, every, lax.axis_size("tensor"))

    latent_sum = jnp.sum(exchange(latent_part, ("core", "tensor")).astype(F32), axis=0)
    latent_grad = latent_sum.astype(BF).T[None]

    weight_parts = lax.all_gather(weight_part, ("core", "dp"))
    weight_grad = total(place, weight_parts, 1.0 / math.sqrt(latents * batches))
    return (whole(0), whole(half), latent_grad, weight_grad)


def solution(mesh):
    fine = Mesh(
        mesh.devices.reshape(4, 4, 2, *mesh.devices.shape[1:]), SEQ + tuple(mesh.axis_names[1:])
    )
    return jax.shard_map(
        local,
        mesh=fine,
        in_specs=(
            P("dp", SEQ, None),
            P(SEQ, "tensor"),
            P(SEQ, "tensor"),
            P(SEQ, "tensor"),
            P("dp", SEQ, "tensor"),
            P("dp", SEQ, "tensor"),
            P("dp", SEQ, "tensor"),
            P("dp", SEQ, "tensor"),
            P("dp", None, SEQ),
        ),
        out_specs=(
            P("dp", SEQ, "tensor"),
            P("dp", SEQ, "tensor"),
            P("dp", "tensor", SEQ),
            P(SEQ, "tensor"),
        ),
        check_vma=False,
    )
```

time: 228 us -> 202 us (0.89)
  waiting for transfers between devices: 43.7 us -> 1.92 us
  blocking collectives: 99.1 us -> 112 us
  local copies, waits for them, and re-layouts: 11.5 us -> 4.33 us
  Pallas kernels: 13.2 us -> 19.2 us
  starting transfers between devices: 56.8 us -> 60.1 us
    all_gather x2 -> x4, blocking collectives: 60.1 us -> 107 us  [the longest x1 28.8 us: local(): first_rows = lax.all_gather(blocks[:, :cut], Z, axis=0, tiled=True)]
    all_to_all x1, blocking collectives: 39 us -> 4.45 us  [exchange(): return lax.all_to_all(x, axes, 0, 0, tiled=True)]
    all_to_all x4 -> x3, waiting for transfers between devices: 24.9 us -> 0.01 us  [exchange(): return lax.all_to_all(x, axes, 0, 0, tiled=True)]
    ppermute x3 -> x0, waiting for transfers between devices: 17.8 us -> none  [local(): lax.ppermute(slab, 'dp', [(i, (i + d) % batches) for i in range(batches)])]
    ppermute x1, starting transfers between devices: 4.67 us -> 15.6 us  [local(): lax.ppermute(jnp.concatenate([latent_own, query_theirs], axis=1), 'core',...]
    ppermute x3 -> x0, starting transfers between devices: 10.7 us -> none  [local(): lax.ppermute(slab, 'dp', [(i, (i + d) % batches) for i in range(batches)])]
    ppermute x1, starting transfers between devices: 3.55 us -> 8.79 us  [local(): other_tokens = lax.ppermute(tokens_in, 'core', SWAP)]
    unnamed x22 -> x14, local copies, waits for them, and re-layouts: 6.83 us -> 2.58 us
  transfers between devices with their start and end apart: 10 -> 6, of which waited for: 7 -> 1; matrix products, arithmetic and copies ran while one was open for 2% -> 2% of each run, Pallas kernels for 2% -> 2%
where the time goes in v6:
time: 202 us; the launch traced here: 201 us
  blocking collectives  112 us (55%)
  starting transfers between devices  60.1 us (30%)
  Pallas kernels  19.2 us (10%)
  local copies, waits for them, and re-layouts  4.33 us (2%)
  other arithmetic  2.67 us (1%)
    all_to_all x3, starting transfers between devices, exchange(): return lax.all_to_all(x, axes, 0, 0, tiled=True)  33.8 us
    all_gather x1, blocking collectives, local(): first_rows = lax.all_gather(blocks[:, :cut], Z, axis=0, tiled=True)  28.8 us
    all_gather x1, blocking collectives, local(): every = lax.all_gather(share, Z, axis=0, tiled=True)  27.6 us
    all_gather x1, blocking collectives, local(): last_rows = lax.all_gather(rest, Z, axis=0, tiled=True)  26.8 us
    all_gather x1, blocking collectives, local(): weight_parts = lax.all_gather(weight_part, ('core', 'dp'))  24.1 us
    ppermute x1, starting transfers between devices, local(): lax.ppermute(jnp.concatenate([latent_own, query_theirs], axis=1), 'core',...  15.6 us
    pallas_call x1, Pallas kernels, attend(): pl.pallas_call(kernel, grid=(tokens // block,), in_specs=[pl.BlockSpec((b...  9.53 us
    ppermute x1, starting transfers between devices, local(): other_tokens = lax.ppermute(tokens_in, 'core', SWAP)  8.79 us
  transfers between devices with their start and end apart: 6, of which 1 were waited for; matrix products, arithmetic and copies ran while one was open for 2% of the time, Pallas kernels for 2%

profile of v6, /device:TPU:1, one launch (start us, length us, event | category | flops | bytes accessed | tf_op | source)
XLA Modules:
  0.0 200.8 jit_solution(3495737718491756210)
XLA Ops:
  0.6 8.8 %collective-permute-start = (bf16[512,2048]{1,0:T(8,128)(2,1)}, bf16[512,2048]{1,0:T(8,128)(2,1)}, u32[]{:S(2)}, u32[]{:S(2)}) collective-permute-start(bf16[512,2048]{1,0:T(8,128)(2,1)} %bitcast.38), channel_id=1, source_target_pairs={{0,16},{16,0},{1,17},{17,1},{2,18},{18,2},{3,19},{19,3},{4,20},{20... | collective-permute-start | bytes 6291464 | tf_op jit(solution)/shard_map/ppermute | solution.py:305
  9.4 0.6 pad_add_fusion.place_ref
  10.0 2.4 %shard_map.120 = bf16[2,208,128]{2,1,0:T(8,128)(2,1)} custom-call(s32[3]{0:T(128)} %pad_add_fusion.place_ref, bf16[64,512]{1,0:T(8,128)(2,1)} %refs_0_.1, bf16[64,512]{1,0:T(8,128)(2,1)} %refs_1_.1, bf16[32,512]{1,0:T(8,128)(2,1)} %bitcast.48, bf16[32,512]{1,0:T(8,128)(2,1)} %bitcast.49, bf16[32,512]{1,0:T(8,128)(2,1)} %bitcast.50, f32[4,32]{1,0:T(4,128)} %bitcast.51), custom_call_target="tpu_custom_call" | custom-call | bytes 524288 | tf_op jit(solution)/shard_map/pallas_call | solution.py:80
  12.5 4.5 %all_to_all.20 = bf16[2,208,128]{2,1,0:T(8,128)(2,1)S(1)} all-to-all(bf16[2,208,128]{2,1,0:T(8,128)(2,1)} %shard_map.120), channel_id=1, replica_groups=mesh['zh'=4,'zl'=4,'core'=2,'tensor'=4,'dp'=4] {'core'}, dimensions={0} | all-to-all | bytes 212992 | tf_op jit(solution)/shard_map/all_to_all | solution.py:283
  16.9 28.8 %all_gather.15.head_ref.stat_ref = bf16[32,112,128]{2,1,0:T(8,128)(2,1)S(1)} all-gather(bf16[2,112,128]{2,1,0:T(8,128)(2,1)S(1)} %slice.46), channel_id=1, replica_groups=mesh['zh'=4,'zl'=4,'core'=2,'tensor'=4,'dp'=4] {'zh','zl'}, dimensions={0}, use_global_device_ids=true | all-gather | bytes 974848 | tf_op jit(solution)/shard_map/all_gather | solution.py:325
  45.7 0.1 slice.47
  45.8 1.6 broadcast_in_dim.13
  47.4 4.2 %all-to-all-start.1 = ((bf16[4,2048,128]{2,1,0:T(8,128)(2,1)}), bf16[4,2048,128]{2,1,0:T(8,128)(2,1)S(1)}, u32[]{:S(2)}, u32[]{:S(2)}) async-start(bf16[4,2048,128]{2,1,0:T(8,128)(2,1)} %broadcast_in_dim.13), calls=%async_computation.1 | async-start | bytes 4194304 | tf_op jit(solution)/shard_map/all_to_all | solution.py:283
  51.6 26.8 %all_gather.16.rest_ref = bf16[32,96,128]{2,1,0:T(8,128)(2,1)} all-gather(bf16[2,96,128]{2,1,0:T(8,128)(2,1)S(1)} %slice.48), channel_id=1, replica_groups=mesh['zh'=4,'zl'=4,'core'=2,'tensor'=4,'dp'=4] {'zh','zl'}, dimensions={0}, use_global_device_ids=true | all-gather | bytes 835584 | tf_op jit(solution)/shard_map/all_gather | solution.py:330
  78.4 0.0 all-to-all-done.1.slab_ref
  78.4 0.0 collective-permute-done.other_ref
  78.4 1.6 copy-done
  80.0 5.0 %shard_map.121.kv_ref = bf16[1024,512]{1,0:T(8,128)(2,1)S(1)} custom-call(bf16[512,2048]{1,0:T(8,128)(2,1)S(1)} %bitcast.39, bf16[512,2048]{1,0:T(8,128)(2,1)} %collective-permute-done.other_ref, bf16[4,2048,128]{2,1,0:T(8,128)(2,1)S(1)} %all-to-all-done.1.slab_ref), custom_call_target="tpu_custom_call" | custom-call | bytes 1048576 | tf_op jit(solution)/shard_map/pallas_call | solution.py:117
  85.0 1.0 copy-done.1
  86.0 9.5 %shard_map.122 = (bf16[512,512]{1,0:T(8,128)(2,1)}, bf16[512,512]{1,0:T(8,128)(2,1)}, bf16[256,1024]{1,0:T(8,128)(2,1)}) custom-call(bf16[1024,512]{1,0:T(8,128)(2,1)} %copy-done.1, bf16[32,112,128]{2,1,0:T(8,128)(2,1)} %copy-done.3, bf16[32,112,128]{2,1,0:T(8,128)(2,1)} %copy-done.3, bf16[32,96,128]{2,1,0:T(8,128)(2,1)} %all_gather.16.rest_ref), custom_call_target="tpu_custom_call" | custom-call | flops 2684354560 | bytes 6291456 | tf_op jit(solution)/shard_map/pallas_call | solution.py:199
  95.5 7.3 %all-to-all-start.2 = ((bf16[16,16,1024]{2,1,0:T(8,128)(2,1)}), bf16[16,16,1024]{2,1,0:T(8,128)(2,1)S(1)}, u32[]{:S(2)}, u32[]{:S(2)}) async-start(bf16[16,16,1024]{2,1,0:T(8,128)(2,1)} %bitcast.44), calls=%async_computation.2 | async-start | bytes 1048576 | tf_op jit(solution)/shard_map/all_to_all | solution.py:283
  102.9 0.0 copy-done.4
  102.9 15.6 %collective-permute-start.2 = (bf16[64,1280]{1,0:T(8,128)(2,1)S(1)}, bf16[64,1280]{1,0:T(8,128)(2,1)S(1)}, u32[]{:S(2)}, u32[]{:S(2)}) collective-permute-start(bf16[64,1280]{1,0:T(8,128)(2,1)S(1)} %pad_maximum_fusion), channel_id=1, source_target_pairs={{0,16},{16,0},{1,17},{17,1},{2,18},{18,2},{3,19},{19,3},{4,20},{20... | collective-permute-start | bytes 491528 | tf_op jit(solution)/shard_map/ppermute | solution.py:310
  118.5 1.9 collective-permute-start.1
  120.5 0.0 collective-permute-done.2
  120.5 0.1 maximum_select_fusion.2.latent_ref
  120.6 1.9 collective-permute-done.1
  122.6 1.2 maximum_select_fusion
  123.8 0.0 all-to-all-done.2
  123.9 0.1 reduce_sum.24
  123.9 27.6 %all_gather.17.every_ref = bf16[256,1024]{1,0:T(8,128)(2,1)S(1)} all-gather(bf16[16,1024]{1,0:T(8,128)(2,1)S(1)} %reduce_sum.24), channel_id=1, replica_groups=mesh['zh'=4,'zl'=4,'core'=2,'tensor'=4,'dp'=4] {'zh','zl'}, dimensions={0}, use_global_device_ids=true | all-gather | bytes 557056 | tf_op jit(solution)/shard_map/all_gather | solution.py:345
  151.5 1.1 shard_map.123
  152.6 22.3 %all-to-all-start.3 = ((bf16[8,64,256]{2,1,0:T(8,128)(2,1)}), bf16[8,64,256]{2,1,0:T(8,128)(2,1)S(1)}, u32[]{:S(2)}, u32[]{:S(2)}) async-start(bf16[8,64,256]{2,1,0:T(8,128)(2,1)} %get-tuple-element.16), calls=%async_computation.3 | async-start | bytes 524288 | tf_op jit(solution)/shard_map/all_to_all | solution.py:283
  174.9 24.1 %all-gather = bf16[1024,256]{1,0:T(8,128)(2,1)S(1)} all-gather(bf16[128,256]{1,0:T(8,128)(2,1)S(1)} %get-tuple-element.17), channel_id=2, replica_groups=mesh['zh'=4,'zl'=4,'core'=2,'tensor'=4,'dp'=4] {'core','dp'}, dimensions={0}, use_global_device_ids=true | all-gather | bytes 589824 | tf_op jit(solution)/shard_map/all_gather | solution.py:351
  198.9 1.2 shard_map.124
  200.2 0.0 all-to-all-done.3
  200.2 0.7 reduce_sum.25
  (21 shorter events, 0.2 us)
Async XLA Ops:
  0.6 77.8 %collective-permute-start = (bf16[512,2048]{1,0:T(8,128)(2,1)}, bf16[512,2048]{1,0:T(8,128)(2,1)}, u32[]{:S(2)}, u32[]{:S(2)}) collective-permute-start(bf16[512,2048]{1,0:T(8,128)(2,1)} %bitcast.38), channel_id=1, source_target_pairs={{0,16},{16,0},{1,17},{17,1},{2,18},{18,2},{3,19},{19,3},{4,20},{20... | collective-permute-start | bytes 6291464 | tf_op jit(solution)/shard_map/ppermute | solution.py:305
  45.7 1.7 copy-start.3
  47.4 31.0 %all-to-all-start.1 = ((bf16[4,2048,128]{2,1,0:T(8,128)(2,1)}), bf16[4,2048,128]{2,1,0:T(8,128)(2,1)S(1)}, u32[]{:S(2)}, u32[]{:S(2)}) async-start(bf16[4,2048,128]{2,1,0:T(8,128)(2,1)} %broadcast_in_dim.13), calls=%async_computation.1 | async-start | bytes 4194304 | tf_op jit(solution)/shard_map/all_to_all | solution.py:283
  78.4 1.6 copy-start
  85.0 1.0 copy-start.1
  86.0 16.9 %copy-start.6 = (bf16[64,512]{1,0:T(8,128)(2,1)S(1)}, bf16[64,512]{1,0:T(8,128)(2,1)}, u32[]{:S(2)}) copy-start(bf16[64,512]{1,0:T(8,128)(2,1)} %param.12) | copy-start | bytes 196612
  86.0 16.9 %copy-start.4 = (bf16[1,1024,64]{1,2,0:T(8,128)(2,1)S(1)}, bf16[1,1024,64]{1,2,0:T(8,128)(2,1)}, u32[]{:S(2)}) copy-start(bf16[1,1024,64]{1,2,0:T(8,128)(2,1)} %param.17) | copy-start | bytes 393220
  95.5 25.1 %copy-start.5 = (bf16[512,512]{1,0:T(8,128)(2,1)S(1)}, bf16[512,512]{1,0:T(8,128)(2,1)}, u32[]{:S(2)}) copy-start(bf16[512,512]{1,0:T(8,128)(2,1)} %get-tuple-element.13) | copy-start | bytes 1572868
  95.5 28.3 %all-to-all-start.2 = ((bf16[16,16,1024]{2,1,0:T(8,128)(2,1)}), bf16[16,16,1024]{2,1,0:T(8,128)(2,1)S(1)}, u32[]{:S(2)}, u32[]{:S(2)}) async-start(bf16[16,16,1024]{2,1,0:T(8,128)(2,1)} %bitcast.44), calls=%async_computation.2 | async-start | bytes 1048576 | tf_op jit(solution)/shard_map/all_to_all | solution.py:283
  102.9 17.6 %collective-permute-start.2 = (bf16[64,1280]{1,0:T(8,128)(2,1)S(1)}, bf16[64,1280]{1,0:T(8,128)(2,1)S(1)}, u32[]{:S(2)}, u32[]{:S(2)}) collective-permute-start(bf16[64,1280]{1,0:T(8,128)(2,1)S(1)} %pad_maximum_fusion), channel_id=1, source_target_pairs={{0,16},{16,0},{1,17},{17,1},{2,18},{18,2},{3,19},{19,3},{4,20},{20... | collective-permute-start | bytes 491528 | tf_op jit(solution)/shard_map/ppermute | solution.py:310
  118.5 4.0 %collective-permute-start.1 = (bf16[512,512]{1,0:T(8,128)(2,1)}, bf16[512,512]{1,0:T(8,128)(2,1)S(1)}, u32[]{:S(2)}, u32[]{:S(2)}) collective-permute-start(bf16[512,512]{1,0:T(8,128)(2,1)} %get-tuple-element.14), channel_id=1, source_target_pairs={{0,16},{16,0},{1,17},{17,1},{2,18},{18,2},{3,19},{19,3},{4,20},{20... | collective-permute-start | bytes 1572872 | tf_op jit(solution)/shard_map/ppermute | solution.py:334
  122.6 76.3 %copy-start.2 = (s32[3]{0:T(128)S(1)}, s32[3]{0:T(128)}, u32[]{:S(2)}) copy-start(s32[3]{0:T(128)} %pad_add_fusion.place_ref) | copy-start | bytes 40
  152.6 47.6 %all-to-all-start.3 = ((bf16[8,64,256]{2,1,0:T(8,128)(2,1)}), bf16[8,64,256]{2,1,0:T(8,128)(2,1)S(1)}, u32[]{:S(2)}, u32[]{:S(2)}) async-start(bf16[8,64,256]{2,1,0:T(8,128)(2,1)} %get-tuple-element.16), calls=%async_computation.3 | async-start | bytes 524288 | tf_op jit(solution)/shard_map/all_to_all | solution.py:283

commit v7 on v6

--- a/solution.py
+++ b/solution.py
@@ -90,48 +90,9 @@
     )(place, *sources)
 
 
-def project_kernel(own_ref, other_ref, slab_ref, out_ref, weight):
-    step = pl.program_id(0)
-    half = pl.num_programs(0) // 2
-    slabs, _, size = slab_ref.shape
-
-    @pl.when(step == 0)
-    def _():
-        for slab in range(slabs):
-            weight[:, slab * size : (slab + 1) * size] = slab_ref[slab]
-
-    @pl.when(step < half)
-    def _():
-        out_ref[...] = dot(own_ref[...], weight[...]).astype(BF)
-
-    @pl.when(step >= half)
-    def _():
-        out_ref[...] = dot(other_ref[...], weight[...]).astype(BF)
-
-
-def project(own, other, slabs):
-    rows, width = own.shape
-    columns = slabs.shape[0] * slabs.shape[2]
-    block = 256
-    half = rows // block
-    return pl.pallas_call(
-        project_kernel,
-        grid=(2 * half,),
-        in_specs=[
-            pl.BlockSpec((block, width), lambda t: (jnp.minimum(t, half - 1), 0)),
-            pl.BlockSpec((block, width), lambda t: (jnp.maximum(t - half, 0), 0)),
-            pl.BlockSpec(slabs.shape, lambda t: (0, 0, 0)),
-        ],
-        out_specs=pl.BlockSpec((block, columns), lambda t: (t, 0)),
-        out_shape=jax.ShapeDtypeStruct((2 * rows, columns), BF),
-        scratch_shapes=[pltpu.VMEM((width, columns), BF)],
-        compiler_params=pltpu.CompilerParams(vmem_limit_bytes=32 * 2**20),
-        cost_estimate=pl.CostEstimate(flops=0, bytes_accessed=2**20, transcendentals=0),
-    )(own, other, slabs)
-
-
 def attend_kernel(
-    kv_ref, head_ref, stat_ref, rest_ref, own_ref, other_ref, part_ref, query, grad, qt, gt, pieces, stats, total,
+    own_in, other_in, slab_ref, head_ref, stat_ref, rest_ref, own_ref, other_ref, part_ref,
+    weight, kv, query, grad, qt, gt, pieces, stats, total,
     size, scaling, latent_factor, prefix_factor,
 ):
     step = pl.program_id(0)
@@ -142,6 +103,8 @@
 
     @pl.when(step == 0)
     def _():
+        for slab in range(slab_ref.shape[0]):
+            weight[:, slab * size : (slab + 1) * size] = slab_ref[slab]
         for rank in range(ranks):
             here = slice(rank * rows, (rank + 1) * rows)
             query[here, :size] = head_ref[rank]
@@ -154,11 +117,19 @@
         gt[...] = grad[...].T
         total[...] = jnp.zeros_like(total)
 
+    @pl.when(step < half)
+    def _():
+        kv[...] = dot(own_in[...], weight[...]).astype(BF)
+
+    @pl.when(step >= half)
+    def _():
+        kv[...] = dot(other_in[...], weight[...]).astype(BF)
+
     key_out, value_out = [], []
     for head in range(2):
         cols = slice(head * size, (head + 1) * size)
-        keys = kv_ref[:, cols]
-        values = kv_ref[:, (2 + head) * size : (3 + head) * size]
+        keys = kv[:, cols]
+        values = kv[:, (2 + head) * size : (3 + head) * size]
         scores = dot(keys, qt[cols, :]) * scaling
         weights = jnp.exp(scores - stats[head : head + 1, :])
         probs = dot(values, gt[cols, :])
@@ -181,14 +152,15 @@
         part_ref[...] = (total[...] * (scaling * prefix_factor)).astype(BF)
 
 
-def attend(kv, first_rows, last_rows, latents, prefix_count):
-    tokens, columns = kv.shape
+def attend(own, other, slabs, first_rows, last_rows, latents, prefix_count):
+    tokens, width = own.shape
+    count, _, size = slabs.shape
+    columns = count * size
     ranks = first_rows.shape[0]
     rows = latents // ranks
     depth = first_rows.shape[1] - 16 - rows
-    size = columns // 4
     block = 256
-    half = tokens // block // 2
+    half = tokens // block
     kernel = functools.partial(
         attend_kernel,
         size=size,
@@ -198,9 +170,11 @@
     )
     return pl.pallas_call(
         kernel,
-        grid=(tokens // block,),
+        grid=(2 * half,),
         in_specs=[
-            pl.BlockSpec((block, columns), lambda t: (t, 0)),
+            pl.BlockSpec((block, width), lambda t: (jnp.minimum(t, half - 1), 0)),
+            pl.BlockSpec((block, width), lambda t: (jnp.maximum(t - half, 0), 0)),
+            pl.BlockSpec(slabs.shape, lambda t: (0, 0, 0)),
             pl.BlockSpec((ranks, rows, size), lambda t: (0, depth // rows, 0)),
             pl.BlockSpec((ranks, 16, size), lambda t: (0, (depth + rows) // 16, 0)),
             pl.BlockSpec(last_rows.shape, lambda t: (0, 0, 0)),
@@ -211,11 +185,13 @@
             pl.BlockSpec((2 * size, latents), lambda t: (0, 0)),
         ],
         out_shape=[
-            jax.ShapeDtypeStruct((tokens // 2, columns), BF),
-            jax.ShapeDtypeStruct((tokens // 2, columns), BF),
+            jax.ShapeDtypeStruct((tokens, columns), BF),
+            jax.ShapeDtypeStruct((tokens, columns), BF),
             jax.ShapeDtypeStruct((2 * size, latents), BF),
         ],
         scratch_shapes=[
+            pltpu.VMEM((width, columns), BF),
+            pltpu.VMEM((block, columns), BF),
             pltpu.VMEM((latents, 2 * size), BF),
             pltpu.VMEM((latents, 2 * size), BF),
             pltpu.VMEM((2 * size, latents), BF),
@@ -224,59 +200,68 @@
             pltpu.VMEM((4, latents), F32),
             pltpu.VMEM((2 * size, latents), F32),
         ],
-        compiler_params=pltpu.CompilerParams(vmem_limit_bytes=56 * 2**20),
+        compiler_params=pltpu.CompilerParams(vmem_limit_bytes=52 * 2**20),
         cost_estimate=pl.CostEstimate(
-            flops=20 * tokens * latents * size,
+            flops=40 * tokens * latents * size,
             bytes_accessed=6 * 2**20,
-            transcendentals=2 * tokens * latents,
+            transcendentals=4 * tokens * latents,
         ),
-    )(kv, first_rows, first_rows, last_rows)
-
-
-def tail_kernel(query_ref, latent_ref, every_ref, latent_out, weight_out):
+    )(own, other, slabs, first_rows, first_rows, last_rows)
+
+
+def tail_kernel(place_ref, query_ref, latent_ref, every_ref, latent_out, mine_out, theirs_out):
+    core = place_ref[0]
     count, rows, width = latent_out.shape
-    weight_out[...] = dot_nt(latent_ref[...], every_ref[...]).astype(BF)
+    weight = dot_nt(latent_ref[...], every_ref[...]).astype(BF)
+    for one, out in enumerate((mine_out, theirs_out)):
+
+        @pl.when(core == 0)
+        def _():
+            out[...] = weight[one * rows : (one + 1) * rows]
+
+        @pl.when(core == 1)
+        def _():
+            out[...] = weight[(1 - one) * rows : (2 - one) * rows]
+
     latent = dot(query_ref[...], every_ref[...]).astype(BF)
     for i in range(count):
         half, group = divmod(i, count // 2)
         latent_out[i] = latent[half * rows : (half + 1) * rows, group * width : (group + 1) * width]
 
 
-def tail(query, latent, every, tensors):
+def tail(place, query, latent, every, tensors):
     both, half = query.shape
+    rows = both // 2
     latents = latent.shape[1]
     return pl.pallas_call(
         tail_kernel,
-        in_specs=[pl.BlockSpec(memory_space=pltpu.VMEM)] * 3,
-        out_specs=[pl.BlockSpec(memory_space=pltpu.VMEM)] * 2,
+        in_specs=[pl.BlockSpec(memory_space=pltpu.SMEM)]
+        + [pl.BlockSpec(memory_space=pltpu.VMEM)] * 3,
+        out_specs=[pl.BlockSpec(memory_space=pltpu.VMEM)] * 3,
         out_shape=[
-            jax.ShapeDtypeStruct((2 * tensors, both // 2, latents // tensors), BF),
-            jax.ShapeDtypeStruct((both, half), BF),
+            jax.ShapeDtypeStruct((2 * tensors, rows, latents // tensors), BF),
+            jax.ShapeDtypeStruct((rows, half), BF),
+            jax.ShapeDtypeStruct((rows, half), BF),
         ],
         compiler_params=pltpu.CompilerParams(vmem_limit_bytes=32 * 2**20),
         cost_estimate=pl.CostEstimate(flops=0, bytes_accessed=2**20, transcendentals=0),
-    )(query, latent, every)
-
-
-def total_kernel(place_ref, part_ref, out_ref, *, factor):
-    rows = out_ref.shape[0]
-    here = pl.ds(pl.multiple_of(place_ref[0] * rows, rows), rows)
-    count, _, width = part_ref.shape
-    for half in range(2):
-        parts = [part_ref[i, here, :].astype(F32) for i in range(half * count // 2, (half + 1) * count // 2)]
-        out_ref[:, half * width : (half + 1) * width] = sum(parts[1:], parts[0]) * factor
-
-
-def total(place, parts, factor):
-    _, rows, width = parts.shape
+    )(place, query, latent, every)
+
+
+def total_kernel(part_ref, out_ref, *, factor):
+    parts = [part_ref[i].astype(F32) for i in range(part_ref.shape[0])]
+    out_ref[...] = sum(parts[1:], parts[0]) * factor
+
+
+def total(parts, factor):
     return pl.pallas_call(
         functools.partial(total_kernel, factor=factor),
-        in_specs=[pl.BlockSpec(memory_space=pltpu.SMEM), pl.BlockSpec(memory_space=pltpu.VMEM)],
+        in_specs=[pl.BlockSpec(memory_space=pltpu.VMEM)],
         out_specs=pl.BlockSpec(memory_space=pltpu.VMEM),
-        out_shape=jax.ShapeDtypeStruct((rows // 2, 2 * width), F32),
+        out_shape=jax.ShapeDtypeStruct(parts.shape[1:], F32),
         compiler_params=pltpu.CompilerParams(vmem_limit_bytes=32 * 2**20),
         cost_estimate=pl.CostEstimate(flops=0, bytes_accessed=2**10, transcendentals=0),
-    )(place, parts)
+    )(parts)
 
 
 def exchange(x, axes):
@@ -329,8 +314,9 @@
     slabs = exchange(slabs, "dp")
     last_rows = lax.all_gather(rest, Z, axis=0, tiled=True)
 
-    kv = project(tokens_in, other_tokens, slabs)
-    own_grads, other_grads, part = attend(kv, first_rows, last_rows, latents, token_count * ranks)
+    own_grads, other_grads, part = attend(
+        tokens_in, other_tokens, slabs, first_rows, last_rows, latents, token_count * ranks
+    )
     theirs = lax.ppermute(other_grads, "core", SWAP)
     half = columns // 2
 
@@ -343,13 +329,22 @@
     share = exchange(part.reshape(lax.axis_size(Z), -1, latents), Z)
     share = jnp.sum(share.astype(F32), axis=0).astype(BF)
     every = lax.all_gather(share, Z, axis=0, tiled=True)
-    latent_part, weight_part = tail(query_both, latent_both, every, lax.axis_size("tensor"))
+    latent_part, weight_mine, weight_theirs = tail(
+        place, query_both, latent_both, every, lax.axis_size("tensor")
+    )
 
     latent_sum = jnp.sum(exchange(latent_part, ("core", "tensor")).astype(F32), axis=0)
     latent_grad = latent_sum.astype(BF).T[None]
 
-    weight_parts = lax.all_gather(weight_part, ("core", "dp"))
-    weight_grad = total(place, weight_parts, 1.0 / math.sqrt(latents * batches))
+    weight_other = lax.ppermute(weight_theirs, "core", SWAP)
+    weight_rows = jnp.where(
+        first,
+        jnp.concatenate([weight_mine, weight_other], 1),
+        jnp.concatenate([weight_other, weight_mine], 1),
+    )
+    weight_grad = total(
+        lax.all_gather(weight_rows, "dp"), 1.0 / math.sqrt(latents * batches)
+    )
     return (whole(0), whole(half), latent_grad, weight_grad)
 
 

time: 202 us -> 189 us (0.936)
  blocking collectives: 112 us -> 99.4 us
  local copies, waits for them, and re-layouts: 4.33 us -> 1.78 us
    ppermute x0 -> x1, starting transfers between devices: none -> 20.4 us  [local(): weight_other = lax.ppermute(weight_theirs, 'core', SWAP)]
    all_to_all x3, starting transfers between devices: 33.8 us -> 16.3 us  [exchange(): return lax.all_to_all(x, axes, 0, 0, tiled=True)]
    all_gather x1, blocking collectives: 24.1 us -> 10.3 us  [local(): lax.all_gather(weight_rows, 'dp')]
    unnamed x14 -> x8, local copies, waits for them, and re-layouts: 2.58 us -> 0.02 us
    pallas_call x3 -> x2, Pallas kernels: 15.6 us -> 15.5 us  [the longest x1 13.6 us: attend(): pl.pallas_call(kernel, grid=(2 * half,), in_specs=[pl.BlockSpec((block, w...]
  transfers between devices with their start and end apart: 6 -> 7, of which waited for: 1 -> 1; matrix products, arithmetic and copies ran while one was open for 2% -> 2% of each run, Pallas kernels for 2% -> 2%
where the time goes in v7:
time: 189 us; the launch traced here: 187 us
  blocking collectives  99.4 us (53%)
  starting transfers between devices  61.8 us (33%)
  Pallas kernels  18.6 us (10%)
  other arithmetic  2.61 us (1%)
    all_gather x1, blocking collectives, local(): first_rows = lax.all_gather(blocks[:, :cut], Z, axis=0, tiled=True)  28.8 us
    all_gather x1, blocking collectives, local(): every = lax.all_gather(share, Z, axis=0, tiled=True)  28.5 us
    all_gather x1, blocking collectives, local(): last_rows = lax.all_gather(rest, Z, axis=0, tiled=True)  27.4 us
    ppermute x1, starting transfers between devices, local(): weight_other = lax.ppermute(weight_theirs, 'core', SWAP)  20.4 us
    all_to_all x3, starting transfers between devices, exchange(): return lax.all_to_all(x, axes, 0, 0, tiled=True)  16.3 us
    ppermute x1, starting transfers between devices, local(): lax.ppermute(jnp.concatenate([latent_own, query_theirs], axis=1), 'core',...  14.4 us
    pallas_call x1, Pallas kernels, attend(): pl.pallas_call(kernel, grid=(2 * half,), in_specs=[pl.BlockSpec((block, w...  13.6 us
    all_gather x1, blocking collectives, local(): lax.all_gather(weight_rows, 'dp')  10.3 us
  transfers between devices with their start and end apart: 7, of which 1 were waited for; matrix products, arithmetic and copies ran while one was open for 2% of the time, Pallas kernels for 2%

profile of v7, /device:TPU:1, one launch (start us, length us, event | category | flops | bytes accessed | tf_op | source)
XLA Modules:
  0.0 186.8 jit_solution(4681821965314964790)
XLA Ops:
  0.6 8.8 %collective-permute-start = (bf16[512,2048]{1,0:T(8,128)(2,1)}, bf16[512,2048]{1,0:T(8,128)(2,1)}, u32[]{:S(2)}, u32[]{:S(2)}) collective-permute-start(bf16[512,2048]{1,0:T(8,128)(2,1)} %bitcast.51), channel_id=1, source_target_pairs={{0,16},{16,0},{1,17},{17,1},{2,18},{18,2},{3,19},{19,3},{4,20},{20... | collective-permute-start | bytes 6291464 | tf_op jit(solution)/shard_map/ppermute | solution.py:290
  9.4 0.6 pad_add_fusion.place_ref
  10.0 2.4 %shard_map.120 = bf16[2,208,128]{2,1,0:T(8,128)(2,1)} custom-call(s32[3]{0:T(128)} %pad_add_fusion.place_ref, bf16[64,512]{1,0:T(8,128)(2,1)} %refs_0_.1, bf16[64,512]{1,0:T(8,128)(2,1)} %refs_1_.1, bf16[32,512]{1,0:T(8,128)(2,1)} %bitcast.47, bf16[32,512]{1,0:T(8,128)(2,1)} %bitcast.48, bf16[32,512]{1,0:T(8,128)(2,1)} %bitcast.49, f32[4,32]{1,0:T(4,128)} %bitcast.50), custom_call_target="tpu_custom_call" | custom-call | bytes 524288 | tf_op jit(solution)/shard_map/pallas_call | solution.py:80
  12.4 4.5 %all_to_all.20 = bf16[2,208,128]{2,1,0:T(8,128)(2,1)S(1)} all-to-all(bf16[2,208,128]{2,1,0:T(8,128)(2,1)} %shard_map.120), channel_id=1, replica_groups=mesh['zh'=4,'zl'=4,'core'=2,'tensor'=4,'dp'=4] {'core'}, dimensions={0} | all-to-all | bytes 212992 | tf_op jit(solution)/shard_map/all_to_all | solution.py:268
  16.9 28.8 %all_gather.13.head_ref.stat_ref = bf16[32,112,128]{2,1,0:T(8,128)(2,1)S(1)} all-gather(bf16[2,112,128]{2,1,0:T(8,128)(2,1)S(1)} %slice.46), channel_id=1, replica_groups=mesh['zh'=4,'zl'=4,'core'=2,'tensor'=4,'dp'=4] {'zh','zl'}, dimensions={0}, use_global_device_ids=true | all-gather | bytes 974848 | tf_op jit(solution)/shard_map/all_gather | solution.py:310
  45.7 0.1 slice.47
  45.7 1.6 broadcast_in_dim.13
  47.4 0.0 copy-done.1
  47.4 4.4 %all-to-all-start.1 = ((bf16[4,2048,128]{2,1,0:T(8,128)(2,1)}), bf16[4,2048,128]{2,1,0:T(8,128)(2,1)}, u32[]{:S(2)}, u32[]{:S(2)}) async-start(bf16[4,2048,128]{2,1,0:T(8,128)(2,1)} %broadcast_in_dim.13), calls=%async_computation.1 | async-start | bytes 4194304 | tf_op jit(solution)/shard_map/all_to_all | solution.py:268
  51.8 27.4 %all_gather.14.rest_ref = bf16[32,96,128]{2,1,0:T(8,128)(2,1)} all-gather(bf16[2,96,128]{2,1,0:T(8,128)(2,1)S(1)} %slice.48), channel_id=1, replica_groups=mesh['zh'=4,'zl'=4,'core'=2,'tensor'=4,'dp'=4] {'zh','zl'}, dimensions={0}, use_global_device_ids=true | all-gather | bytes 835584 | tf_op jit(solution)/shard_map/all_gather | solution.py:315
  79.2 0.0 all-to-all-done.1.slab_ref
  79.2 0.0 collective-permute-done.other_in
  79.2 13.6 %shard_map.121 = (bf16[512,512]{1,0:T(8,128)(2,1)S(1)}, bf16[512,512]{1,0:T(8,128)(2,1)S(1)}, bf16[256,1024]{1,0:T(8,128)(2,1)}) custom-call(bf16[512,2048]{1,0:T(8,128)(2,1)} %bitcast.52, bf16[512,2048]{1,0:T(8,128)(2,1)} %collective-permute-done.other_in, bf16[4,2048,128]{2,1,0:T(8,128)(2,1)} %all-to-all-done.1.slab_ref, bf16[32,112,128]{2,1,0:T(8,128)(2,1)} %copy-done.1, ...), custom_call_target="tpu_custom_call" | custom-call | flops 2684354560 | bytes 6291456 | tf_op jit(solution)/shard_map/pallas_call | solution.py:171
  92.8 7.4 %all-to-all-start.2 = ((bf16[16,16,1024]{2,1,0:T(8,128)(2,1)}), bf16[16,16,1024]{2,1,0:T(8,128)(2,1)S(1)}, u32[]{:S(2)}, u32[]{:S(2)}) async-start(bf16[16,16,1024]{2,1,0:T(8,128)(2,1)} %bitcast.20), calls=%async_computation.2 | async-start | bytes 1048576 | tf_op jit(solution)/shard_map/all_to_all | solution.py:268
  100.3 0.0 copy-done.3
  100.3 14.4 %collective-permute-start.2 = (bf16[64,1280]{1,0:T(8,128)(2,1)S(1)}, bf16[64,1280]{1,0:T(8,128)(2,1)S(1)}, u32[]{:S(2)}, u32[]{:S(2)}) collective-permute-start(bf16[64,1280]{1,0:T(8,128)(2,1)S(1)} %pad_maximum_fusion), channel_id=1, source_target_pairs={{0,16},{16,0},{1,17},{17,1},{2,18},{18,2},{3,19},{19,3},{4,20},{20... | collective-permute-start | bytes 491528 | tf_op jit(solution)/shard_map/ppermute | solution.py:295
  114.7 1.9 %collective-permute-start.1 = (bf16[512,512]{1,0:T(8,128)(2,1)S(1)}, bf16[512,512]{1,0:T(8,128)(2,1)S(1)}, u32[]{:S(2)}, u32[]{:S(2)}) collective-permute-start(bf16[512,512]{1,0:T(8,128)(2,1)S(1)} %get-tuple-element.15), channel_id=1, source_target_pairs={{0,16},{16,0},{1,17},{17,1},{2,18},{18,2},{3,19},{19,3},{4,20},{20... | collective-permute-start | bytes 1572872 | tf_op jit(solution)/shard_map/ppermute | solution.py:320
  116.6 0.0 collective-permute-done.2
  116.7 0.1 maximum_select_fusion.2.latent_ref
  116.8 1.7 collective-permute-done.1
  118.6 0.0 all-to-all-done.2
  118.6 0.1 reduce_sum.24
  118.7 28.5 %all_gather.15.every_ref = bf16[256,1024]{1,0:T(8,128)(2,1)S(1)} all-gather(bf16[16,1024]{1,0:T(8,128)(2,1)S(1)} %reduce_sum.24), channel_id=1, replica_groups=mesh['zh'=4,'zl'=4,'core'=2,'tensor'=4,'dp'=4] {'zh','zl'}, dimensions={0}, use_global_device_ids=true | all-gather | bytes 557056 | tf_op jit(solution)/shard_map/all_gather | solution.py:331
  147.2 1.9 %shard_map.122 = (bf16[8,64,256]{2,1,0:T(8,128)(2,1)}, bf16[64,256]{1,0:T(8,128)(2,1)S(1)}, bf16[64,256]{1,0:T(8,128)(2,1)S(1)}) custom-call(s32[3]{0:T(128)S(1)} %copy-done, bf16[128,256]{1,0:T(8,128)(2,1)S(1)} %maximum_select_fusion.3.query_ref, bf16[128,1024]{1,0:T(8,128)(2,1)S(1)} %maximum_select_fusion.2.latent_ref, ...), custom_call_target="tpu_custom_call" | custom-call | bytes 1048576 | tf_op jit(solution)/shard_map/pallas_call | solution.py:236
  149.1 20.4 %collective-permute-start.3 = (bf16[64,256]{1,0:T(8,128)(2,1)S(1)}, bf16[64,256]{1,0:T(8,128)(2,1)S(1)}, u32[]{:S(2)}, u32[]{:S(2)}) collective-permute-start(bf16[64,256]{1,0:T(8,128)(2,1)S(1)} %get-tuple-element.19), channel_id=1, source_target_pairs={{0,16},{16,0},{1,17},{17,1},{2,18},{18,2},{3,19},{19,3},{4,20},{20... | collective-permute-start | bytes 98312 | tf_op jit(solution)/shard_map/ppermute | solution.py:339
  169.5 4.4 %all-to-all-start.3 = ((bf16[8,64,256]{2,1,0:T(8,128)(2,1)}), bf16[8,64,256]{2,1,0:T(8,128)(2,1)S(1)}, u32[]{:S(2)}, u32[]{:S(2)}) async-start(bf16[8,64,256]{2,1,0:T(8,128)(2,1)} %get-tuple-element.17), calls=%async_computation.3 | async-start | bytes 524288 | tf_op jit(solution)/shard_map/all_to_all | solution.py:268
  173.9 1.2 maximum_select_fusion
  175.1 0.0 collective-permute-done.3
  175.2 10.3 %all_gather.16.part_ref = bf16[4,64,512]{2,1,0:T(8,128)(2,1)S(1)} all-gather(bf16[1,64,512]{2,1,0:T(8,128)(2,1)S(1)} %maximum_select_fusion.4), channel_id=1, replica_groups=mesh['zh'=4,'zl'=4,'core'=2,'tensor'=4,'dp'=4] {'dp'}, dimensions={0}, use_global_device_ids=true | all-gather | bytes 327680 | tf_op jit(solution)/shard_map/all_gather | solution.py:346
  185.5 0.7 shard_map.123
  186.2 0.0 all-to-all-done.3
  186.2 0.7 reduce_sum.25
  (17 shorter events, 0.2 us)
Async XLA Ops:
  0.6 78.6 %collective-permute-start = (bf16[512,2048]{1,0:T(8,128)(2,1)}, bf16[512,2048]{1,0:T(8,128)(2,1)}, u32[]{:S(2)}, u32[]{:S(2)}) collective-permute-start(bf16[512,2048]{1,0:T(8,128)(2,1)} %bitcast.51), channel_id=1, source_target_pairs={{0,16},{16,0},{1,17},{17,1},{2,18},{18,2},{3,19},{19,3},{4,20},{20... | collective-permute-start | bytes 6291464 | tf_op jit(solution)/shard_map/ppermute | solution.py:290
  45.7 1.7 copy-start.1
  47.4 31.8 %all-to-all-start.1 = ((bf16[4,2048,128]{2,1,0:T(8,128)(2,1)}), bf16[4,2048,128]{2,1,0:T(8,128)(2,1)}, u32[]{:S(2)}, u32[]{:S(2)}) async-start(bf16[4,2048,128]{2,1,0:T(8,128)(2,1)} %broadcast_in_dim.13), calls=%async_computation.1 | async-start | bytes 4194304 | tf_op jit(solution)/shard_map/all_to_all | solution.py:268
  79.2 21.1 %copy-start.3 = (bf16[64,512]{1,0:T(8,128)(2,1)S(1)}, bf16[64,512]{1,0:T(8,128)(2,1)}, u32[]{:S(2)}) copy-start(bf16[64,512]{1,0:T(8,128)(2,1)} %param.12) | copy-start | bytes 196612
  79.2 21.1 %copy-start.2 = (bf16[1,1024,64]{1,2,0:T(8,128)(2,1)S(1)}, bf16[1,1024,64]{1,2,0:T(8,128)(2,1)}, u32[]{:S(2)}) copy-start(bf16[1,1024,64]{1,2,0:T(8,128)(2,1)} %param.17) | copy-start | bytes 393220
  92.8 25.7 %all-to-all-start.2 = ((bf16[16,16,1024]{2,1,0:T(8,128)(2,1)}), bf16[16,16,1024]{2,1,0:T(8,128)(2,1)S(1)}, u32[]{:S(2)}, u32[]{:S(2)}) async-start(bf16[16,16,1024]{2,1,0:T(8,128)(2,1)} %bitcast.20), calls=%async_computation.2 | async-start | bytes 1048576 | tf_op jit(solution)/shard_map/all_to_all | solution.py:268
  100.3 16.3 %collective-permute-start.2 = (bf16[64,1280]{1,0:T(8,128)(2,1)S(1)}, bf16[64,1280]{1,0:T(8,128)(2,1)S(1)}, u32[]{:S(2)}, u32[]{:S(2)}) collective-permute-start(bf16[64,1280]{1,0:T(8,128)(2,1)S(1)} %pad_maximum_fusion), channel_id=1, source_target_pairs={{0,16},{16,0},{1,17},{17,1},{2,18},{18,2},{3,19},{19,3},{4,20},{20... | collective-permute-start | bytes 491528 | tf_op jit(solution)/shard_map/ppermute | solution.py:295
  114.7 32.5 %copy-start = (s32[3]{0:T(128)S(1)}, s32[3]{0:T(128)}, u32[]{:S(2)}) copy-start(s32[3]{0:T(128)} %pad_add_fusion.place_ref) | copy-start | bytes 40
  114.7 3.8 %collective-permute-start.1 = (bf16[512,512]{1,0:T(8,128)(2,1)S(1)}, bf16[512,512]{1,0:T(8,128)(2,1)S(1)}, u32[]{:S(2)}, u32[]{:S(2)}) collective-permute-start(bf16[512,512]{1,0:T(8,128)(2,1)S(1)} %get-tuple-element.15), channel_id=1, source_target_pairs={{0,16},{16,0},{1,17},{17,1},{2,18},{18,2},{3,19},{19,3},{4,20},{20... | collective-permute-start | bytes 1572872 | tf_op jit(solution)/shard_map/ppermute | solution.py:320
  149.1 26.1 %collective-permute-start.3 = (bf16[64,256]{1,0:T(8,128)(2,1)S(1)}, bf16[64,256]{1,0:T(8,128)(2,1)S(1)}, u32[]{:S(2)}, u32[]{:S(2)}) collective-permute-start(bf16[64,256]{1,0:T(8,128)(2,1)S(1)} %get-tuple-element.19), channel_id=1, source_target_pairs={{0,16},{16,0},{1,17},{17,1},{2,18},{18,2},{3,19},{19,3},{4,20},{20... | collective-permute-start | bytes 98312 | tf_op jit(solution)/shard_map/ppermute | solution.py:339
  169.5 16.7 %all-to-all-start.3 = ((bf16[8,64,256]{2,1,0:T(8,128)(2,1)}), bf16[8,64,256]{2,1,0:T(8,128)(2,1)S(1)}, u32[]{:S(2)}, u32[]{:S(2)}) async-start(bf16[8,64,256]{2,1,0:T(8,128)(2,1)} %get-tuple-element.17), calls=%async_computation.3 | async-start | bytes 524288 | tf_op jit(solution)/shard_map/all_to_all | solution.py:268

commit v8 on v7

--- a/solution.py
+++ b/solution.py
@@ -24,7 +24,7 @@
 
 
 def pack_kernel(place_ref, *refs):
-    sources, block_ref, landing, arrived = refs[:6], refs[6], refs[7:13], refs[13]
+    sources, outs, landing, arrived = refs[:6], refs[6:8], refs[8:14], refs[14]
     copies = [
         pltpu.make_async_copy(source, target, arrived.at[i])
         for i, (source, target) in enumerate(zip(sources, landing))
@@ -34,10 +34,10 @@
     for copy in copies:
         copy.wait()
     key_ref, value_ref, query_ref, grad_ref, out_ref, lse_ref = landing
-    batch = place_ref[2]
+    batch = place_ref[1]
     depth, columns = key_ref.shape
     rows = query_ref.shape[0]
-    size = block_ref.shape[2]
+    size = outs[0].shape[1]
     heads = columns // size
     half = columns // 2
     product = grad_ref[...].astype(F32) * out_ref[...].astype(F32)
@@ -47,29 +47,34 @@
         one = jnp.sum(product[:, head * size : (head + 1) * size], axis=1, keepdims=True)
         delta = jnp.where(lane == head, one, delta)
     lse, delta = lse_ref[...], delta.T[:heads]
-    for core in range(2):
+    exact = [
+        jnp.concatenate([lse[lo : lo + heads // 2], delta[lo : lo + heads // 2]], axis=0)
+        for lo in (0, heads // 2)
+    ]
+    for other, block_ref in enumerate(outs):
+        core = lax.rem(place_ref[0] + other, 2)
         column = pl.multiple_of(core * half + lax.rem(batch, 2) * size, size)
-        mine = slice(core * heads // 2, (core + 1) * heads // 2)
-        exact = jnp.concatenate([lse[mine], delta[mine]], axis=0)
-        high = exact.astype(BF).astype(F32)
-        stats = jnp.concatenate([high, exact - high], axis=0).astype(BF)
+        mine = jnp.where(core == 0, exact[0], exact[1])
+        high = mine.astype(BF).astype(F32)
+        stats = jnp.concatenate([high, mine - high], axis=0).astype(BF)
 
         @pl.when(batch < 2)
         def _():
-            block_ref[core, :depth] = key_ref[:, pl.ds(column, size)]
+            block_ref[:depth] = key_ref[:, pl.ds(column, size)]
 
         @pl.when(batch >= 2)
         def _():
-            block_ref[core, :depth] = value_ref[:, pl.ds(column, size)]
+            block_ref[:depth] = value_ref[:, pl.ds(column, size)]
 
         first = depth
         for ref in (query_ref, grad_ref):
-            for lo in range(core * half, (core + 1) * half, size):
-                block_ref[core, first : first + rows] = ref[:, lo : lo + size]
+            for lo in range(0, half, size):
+                here = pl.ds(pl.multiple_of(core * half + lo, size), size)
+                block_ref[first : first + rows] = ref[:, here]
                 first += rows
                 if first == depth + rows:
-                    block_ref[core, first : first + 16] = jnp.zeros((16, size), BF)
-                    block_ref[core, first : first + 2 * heads, :rows] = stats
+                    block_ref[first : first + 16] = jnp.zeros((16, size), BF)
+                    block_ref[first : first + 2 * heads, :rows] = stats
                     first += 16
 
 
@@ -81,8 +86,8 @@
         pack_kernel,
         in_specs=[pl.BlockSpec(memory_space=pltpu.SMEM)]
         + [pl.BlockSpec(memory_space=pltpu.HBM)] * len(sources),
-        out_specs=pl.BlockSpec(memory_space=pltpu.VMEM),
-        out_shape=jax.ShapeDtypeStruct((2, depth + 16 + 4 * query.shape[0], size), BF),
+        out_specs=[pl.BlockSpec(memory_space=pltpu.VMEM)] * 2,
+        out_shape=[jax.ShapeDtypeStruct((depth + 16 + 4 * query.shape[0], size), BF)] * 2,
         scratch_shapes=[pltpu.VMEM(x.shape, x.dtype) for x in sources]
         + [pltpu.SemaphoreType.DMA((len(sources),))],
         compiler_params=pltpu.CompilerParams(vmem_limit_bytes=60 * 2**20),
@@ -91,7 +96,7 @@
 
 
 def attend_kernel(
-    own_in, other_in, slab_ref, head_ref, stat_ref, rest_ref, own_ref, other_ref, part_ref,
+    place_ref, own_in, other_in, slab_ref, head_ref, stat_ref, rest_ref, own_ref, other_ref, part_ref,
     weight, kv, query, grad, qt, gt, pieces, stats, total,
     size, scaling, latent_factor, prefix_factor,
 ):
@@ -103,15 +108,20 @@
 
     @pl.when(step == 0)
     def _():
-        for slab in range(slab_ref.shape[0]):
-            weight[:, slab * size : (slab + 1) * size] = slab_ref[slab]
+        depth = weight.shape[0] // ranks
         for rank in range(ranks):
+            at = rank - rank % 2 + lax.rem(rank + place_ref[0], 2)
+            there = pl.ds(pl.multiple_of(at * depth, depth), depth)
+            for slab in range(slab_ref.shape[0]):
+                weight[rank * depth : (rank + 1) * depth, slab * size : (slab + 1) * size] = slab_ref[
+                    slab, there
+                ]
             here = slice(rank * rows, (rank + 1) * rows)
-            query[here, :size] = head_ref[rank]
-            query[here, size:] = rest_ref[rank, :rows]
-            grad[here, :size] = rest_ref[rank, rows : 2 * rows]
-            grad[here, size:] = rest_ref[rank, 2 * rows :]
-            pieces[:, here] = stat_ref[rank].astype(F32)[:8, :rows]
+            query[here, :size] = head_ref[at]
+            query[here, size:] = rest_ref[at, :rows]
+            grad[here, :size] = rest_ref[at, rows : 2 * rows]
+            grad[here, size:] = rest_ref[at, 2 * rows :]
+            pieces[:, here] = stat_ref[at].astype(F32)[:8, :rows]
         stats[...] = pieces[:4] + pieces[4:]
         qt[...] = query[...].T
         gt[...] = grad[...].T
@@ -152,7 +162,7 @@
         part_ref[...] = (total[...] * (scaling * prefix_factor)).astype(BF)
 
 
-def attend(own, other, slabs, first_rows, last_rows, latents, prefix_count):
+def attend(place, own, other, slabs, first_rows, last_rows, latents, prefix_count):
     tokens, width = own.shape
     count, _, size = slabs.shape
     columns = count * size
@@ -172,6 +182,7 @@
         kernel,
         grid=(2 * half,),
         in_specs=[
+            pl.BlockSpec(memory_space=pltpu.SMEM),
             pl.BlockSpec((block, width), lambda t: (jnp.minimum(t, half - 1), 0)),
             pl.BlockSpec((block, width), lambda t: (jnp.maximum(t - half, 0), 0)),
             pl.BlockSpec(slabs.shape, lambda t: (0, 0, 0)),
@@ -206,7 +217,7 @@
             bytes_accessed=6 * 2**20,
             transcendentals=4 * tokens * latents,
         ),
-    )(own, other, slabs, first_rows, first_rows, last_rows)
+    )(place, own, other, slabs, first_rows, first_rows, last_rows)
 
 
 def tail_kernel(place_ref, query_ref, latent_ref, every_ref, latent_out, mine_out, theirs_out):
@@ -302,10 +313,11 @@
     query_both = in_order(query_mine, query_other)
 
     depth = key_weight.shape[0]
-    place = jnp.stack([core, lax.axis_index("zl"), batch]).astype(jnp.int32)
-    blocks = exchange(
-        pack(place, key_weight, value_weight, queries[0], out_grad[0], attn_out[0], shifted_lse[0].T), "core"
-    )
+    place = jnp.stack([core, batch]).astype(jnp.int32)
+    mine, theirs = pack(
+        place, key_weight, value_weight, queries[0], out_grad[0], attn_out[0], shifted_lse[0].T
+    )
+    blocks = jnp.stack([mine, lax.ppermute(theirs, "core", SWAP)])
     cut = depth + 16 + rows
     first_rows = lax.all_gather(blocks[:, :cut], Z, axis=0, tiled=True)
     slab = first_rows[:, :depth].reshape(-1, size)
@@ -315,7 +327,7 @@
     last_rows = lax.all_gather(rest, Z, axis=0, tiled=True)
 
     own_grads, other_grads, part = attend(
-        tokens_in, other_tokens, slabs, first_rows, last_rows, latents, token_count * ranks
+        place, tokens_in, other_tokens, slabs, first_rows, last_rows, latents, token_count * ranks
     )
     theirs = lax.ppermute(other_grads, "core", SWAP)
     half = columns // 2
@@ -328,7 +340,8 @@
 
     share = exchange(part.reshape(lax.axis_size(Z), -1, latents), Z)
     share = jnp.sum(share.astype(F32), axis=0).astype(BF)
-    every = lax.all_gather(share, Z, axis=0, tiled=True)
+    share, key_grad, value_grad = lax.optimization_barrier((share, whole(0), whole(half)))
+    every = exchange(jnp.broadcast_to(share, (lax.axis_size(Z),) + share.shape), Z).reshape(part.shape)
     latent_part, weight_mine, weight_theirs = tail(
         place, query_both, latent_both, every, lax.axis_size("tensor")
     )
@@ -345,7 +358,7 @@
     weight_grad = total(
         lax.all_gather(weight_rows, "dp"), 1.0 / math.sqrt(latents * batches)
     )
-    return (whole(0), whole(half), latent_grad, weight_grad)
+    return (key_grad, value_grad, latent_grad, weight_grad)
 
 
 def solution(mesh):

time: 189 us -> 181 us (0.958)
  blocking collectives: 99.4 us -> 66.3 us
  starting transfers between devices: 61.8 us -> 78.9 us
  waiting for transfers between devices: 1.73 us -> 7.13 us
    all_gather x1 -> x0, blocking collectives: 28.5 us -> none  [local(): every = lax.all_gather(share, Z, axis=0, tiled=True)]
    ppermute x1, starting transfers between devices: 1.92 us -> 14.7 us  [local(): theirs = lax.ppermute(other_grads, 'core', SWAP)]
    all_to_all x3 -> x4, starting transfers between devices: 16.3 us -> 28.5 us  [exchange(): return lax.all_to_all(x, axes, 0, 0, tiled=True)]
    ppermute x0 -> x1, starting transfers between devices: none -> 8.92 us  [local(): blocks = jnp.stack([mine, lax.ppermute(theirs, 'core', SWAP)])]
    ppermute x1, starting transfers between devices: 8.79 us -> 1.92 us  [local(): other_tokens = lax.ppermute(tokens_in, 'core', SWAP)]
    ppermute x1, starting transfers between devices: 20.4 us -> 13.9 us  [local(): weight_other = lax.ppermute(weight_theirs, 'core', SWAP)]
    all_to_all x3 -> x4, waiting for transfers between devices: 0.01 us -> 4.65 us  [exchange(): return lax.all_to_all(x, axes, 0, 0, tiled=True)]
    all_to_all x1 -> x0, blocking collectives: 4.45 us -> none  [exchange(): return lax.all_to_all(x, axes, 0, 0, tiled=True)]
  transfers between devices with their start and end apart: 7 -> 9, of which waited for: 1 -> 3; matrix products, arithmetic and copies ran while one was open for 2% -> 2% of each run, Pallas kernels for 2% -> 0%
where the time goes in v8:
time: 181 us; the launch traced here: 178 us
  starting transfers between devices  78.9 us (44%)
  blocking collectives  66.3 us (37%)
  Pallas kernels  18.8 us (10%)
  waiting for transfers between devices  7.13 us (4%)
  other arithmetic  3.45 us (2%)
  local copies, waits for them, and re-layouts  2.66 us (1%)
    all_gather x1, blocking collectives, local(): first_rows = lax.all_gather(blocks[:, :cut], Z, axis=0, tiled=True)  28.5 us
    all_to_all x4, starting transfers between devices, exchange(): return lax.all_to_all(x, axes, 0, 0, tiled=True)  28.5 us
    all_gather x1, blocking collectives, local(): last_rows = lax.all_gather(rest, Z, axis=0, tiled=True)  27 us
    ppermute x1, starting transfers between devices, local(): theirs = lax.ppermute(other_grads, 'core', SWAP)  14.7 us
    ppermute x1, starting transfers between devices, local(): weight_other = lax.ppermute(weight_theirs, 'core', SWAP)  13.9 us
    pallas_call x1, Pallas kernels, attend(): pl.pallas_call(kernel, grid=(2 * half,), in_specs=[pl.BlockSpec(memory_sp...  13.8 us
    ppermute x1, starting transfers between devices, local(): lax.ppermute(jnp.concatenate([latent_own, query_theirs], axis=1), 'core',...  11 us
    all_gather x1, blocking collectives, local(): lax.all_gather(weight_rows, 'dp')  10.8 us
  transfers between devices with their start and end apart: 9, of which 3 were waited for; matrix products, arithmetic and copies ran while one was open for 2% of the time, Pallas kernels for 0%

profile of v8, /device:TPU:1, one launch (start us, length us, event | category | flops | bytes accessed | tf_op | source)
XLA Modules:
  0.0 178.1 jit_solution(11626026018315009190)
XLA Ops:
  0.6 0.6 pad_add_fusion.place_ref
  1.2 2.4 %shard_map.120 = (bf16[208,128]{1,0:T(8,128)(2,1)}, bf16[208,128]{1,0:T(8,128)(2,1)}) custom-call(s32[2]{0:T(128)} %pad_add_fusion.place_ref, bf16[64,512]{1,0:T(8,128)(2,1)} %refs_0_.1, bf16[64,512]{1,0:T(8,128)(2,1)} %refs_1_.1, bf16[32,512]{1,0:T(8,128)(2,1)} %bitcast.52, bf16[32,512]{1,0:T(8,128)(2,1)} %bitcast.53, bf16[32,512]{1,0:T(8,128)(2,1)} %bitcast.54, ...), custom_call_target="tpu_custom_call" | custom-call | bytes 524288 | tf_op jit(solution)/shard_map/pallas_call | solution.py:85
  3.6 0.0 copy-start.3
  3.7 8.9 %collective-permute-start.1 = (bf16[208,128]{1,0:T(8,128)(2,1)}, bf16[208,128]{1,0:T(8,128)(2,1)S(1)}, u32[]{:S(2)}, u32[]{:S(2)}) collective-permute-start(bf16[208,128]{1,0:T(8,128)(2,1)} %get-tuple-element.18), channel_id=1, source_target_pairs={{0,16},{16,0},{1,17},{17,1},{2,18},{18,2},{3,19},{19,3},{4,20},{20... | collective-permute-start | bytes 159752 | tf_op jit(solution)/shard_map/ppermute | solution.py:320
  12.6 1.9 %collective-permute-start = (bf16[512,2048]{1,0:T(8,128)(2,1)}, bf16[512,2048]{1,0:T(8,128)(2,1)}, u32[]{:S(2)}, u32[]{:S(2)}) collective-permute-start(bf16[512,2048]{1,0:T(8,128)(2,1)} %bitcast.58), channel_id=1, source_target_pairs={{0,16},{16,0},{1,17},{17,1},{2,18},{18,2},{3,19},{19,3},{4,20},{20... | collective-permute-start | bytes 6291464 | tf_op jit(solution)/shard_map/ppermute | solution.py:301
  14.5 0.8 fusion
  15.3 28.5 %all_gather.10.head_ref.stat_ref = bf16[32,112,128]{2,1,0:T(8,128)(2,1)S(1)} all-gather(bf16[2,112,128]{2,1,0:T(8,128)(2,1)S(1)} %fusion), channel_id=1, replica_groups=mesh['zh'=4,'zl'=4,'core'=2,'tensor'=4,'dp'=4] {'zh','zl'}, dimensions={0}, use_global_device_ids=true | all-gather | bytes 974848 | tf_op jit(solution)/shard_map/all_gather | solution.py:322
  43.8 0.1 slice.48
  43.9 1.6 broadcast_in_dim.16
  45.5 4.4 %all-to-all-start = ((bf16[4,2048,128]{2,1,0:T(8,128)(2,1)}), bf16[4,2048,128]{2,1,0:T(8,128)(2,1)}, u32[]{:S(2)}, u32[]{:S(2)}) async-start(bf16[4,2048,128]{2,1,0:T(8,128)(2,1)} %broadcast_in_dim.16), calls=%async_computation | async-start | bytes 4194304 | tf_op jit(solution)/shard_map/all_to_all | solution.py:279
  50.0 27.0 %all_gather.11.rest_ref = bf16[32,96,128]{2,1,0:T(8,128)(2,1)} all-gather(bf16[2,96,128]{2,1,0:T(8,128)(2,1)S(1)} %pad_maximum_fusion.1), channel_id=1, replica_groups=mesh['zh'=4,'zl'=4,'core'=2,'tensor'=4,'dp'=4] {'zh','zl'}, dimensions={0}, use_global_device_ids=true | all-gather | bytes 835584 | tf_op jit(solution)/shard_map/all_gather | solution.py:327
  77.0 0.0 all-to-all-done.slab_ref
  77.1 13.8 %shard_map.121 = (bf16[512,512]{1,0:T(8,128)(2,1)S(1)}, bf16[512,512]{1,0:T(8,128)(2,1)S(1)}, bf16[256,1024]{1,0:T(8,128)(2,1)}) custom-call(s32[2]{0:T(128)S(1)} %copy-done, bf16[512,2048]{1,0:T(8,128)(2,1)} %bitcast.59, bf16[512,2048]{1,0:T(8,128)(2,1)} %collective-permute-done.other_in, bf16[4,2048,128]{2,1,0:T(8,128)(2,1)} %all-to-all-done.slab_ref, ...), custom_call_target="tpu_custom_call" | custom-call | flops 2684354560 | bytes 6291456 | tf_op jit(solution)/shard_map/pallas_call | solution.py:181
  90.8 7.9 %all-to-all-start.1 = ((bf16[16,16,1024]{2,1,0:T(8,128)(2,1)}), bf16[16,16,1024]{2,1,0:T(8,128)(2,1)S(1)}, u32[]{:S(2)}, u32[]{:S(2)}) async-start(bf16[16,16,1024]{2,1,0:T(8,128)(2,1)} %bitcast.11), calls=%async_computation.1 | async-start | bytes 1048576 | tf_op jit(solution)/shard_map/all_to_all | solution.py:279
  98.7 14.7 %collective-permute-start.2 = (bf16[512,512]{1,0:T(8,128)(2,1)S(1)}, bf16[512,512]{1,0:T(8,128)(2,1)S(1)}, u32[]{:S(2)}, u32[]{:S(2)}) collective-permute-start(bf16[512,512]{1,0:T(8,128)(2,1)S(1)} %get-tuple-element.23), channel_id=1, source_target_pairs={{0,16},{16,0},{1,17},{17,1},{2,18},{18,2},{3,19},{19,3},{4,20},{20... | collective-permute-start | bytes 1572872 | tf_op jit(solution)/shard_map/ppermute | solution.py:332
  113.5 1.5 collective-permute-done.2
  115.0 0.0 copy-start.4
  115.0 0.0 copy-start.2
  115.0 1.3 maximum_select_fusion
  116.3 0.1 reduce_sum.24
  116.3 0.9 broadcast_in_dim.17
  117.2 11.7 %all-to-all-start.2 = ((bf16[16,16,1024]{2,1,0:T(8,128)(2,1)}), bf16[16,16,1024]{2,1,0:T(8,128)(2,1)S(1)}, u32[]{:S(2)}, u32[]{:S(2)}) async-start(bf16[16,16,1024]{2,1,0:T(8,128)(2,1)} %broadcast_in_dim.17), calls=%async_computation.2 | async-start | bytes 1048576 | tf_op jit(solution)/shard_map/all_to_all | solution.py:279
  129.0 11.0 %collective-permute-start.3 = (bf16[64,1280]{1,0:T(8,128)(2,1)S(1)}, bf16[64,1280]{1,0:T(8,128)(2,1)S(1)}, u32[]{:S(2)}, u32[]{:S(2)}) collective-permute-start(bf16[64,1280]{1,0:T(8,128)(2,1)S(1)} %pad_maximum_fusion), channel_id=1, source_target_pairs={{0,16},{16,0},{1,17},{17,1},{2,18},{18,2},{3,19},{19,3},{4,20},{20... | collective-permute-start | bytes 491528 | tf_op jit(solution)/shard_map/ppermute | solution.py:306
  140.0 1.0 collective-permute-done.3
  141.0 0.1 maximum_select_fusion.2.latent_ref
  141.1 4.6 %all-to-all-done.2 = bf16[16,16,1024]{2,1,0:T(8,128)(2,1)S(1)} async-done(((bf16[16,16,1024]{2,1,0:T(8,128)(2,1)}), bf16[16,16,1024]{2,1,0:T(8,128)(2,1)S(1)}, u32[]{:S(2)}, u32[]{:S(2)}) %all-to-all-start.2) | async-done | bytes 524320 | tf_op jit(solution)/shard_map/all_to_all | solution.py:279
  145.7 1.9 %shard_map.122 = (bf16[8,64,256]{2,1,0:T(8,128)(2,1)}, bf16[64,256]{1,0:T(8,128)(2,1)S(1)}, bf16[64,256]{1,0:T(8,128)(2,1)S(1)}) custom-call(s32[2]{0:T(128)S(1)} %copy-done, bf16[128,256]{1,0:T(8,128)(2,1)S(1)} %maximum_select_fusion.3.query_ref, bf16[128,1024]{1,0:T(8,128)(2,1)S(1)} %maximum_select_fusion.2.latent_ref, bf16[256,1024]{1,0:T(8,128)(2,1)S(1)} %bitcast.41), custom_call_target="tpu_custom_call" | custom-call | bytes 1048576 | tf_op jit(solution)/shard_map/pallas_call | solution.py:247
  147.6 13.9 %collective-permute-start.4 = (bf16[64,256]{1,0:T(8,128)(2,1)S(1)}, bf16[64,256]{1,0:T(8,128)(2,1)S(1)}, u32[]{:S(2)}, u32[]{:S(2)}) collective-permute-start(bf16[64,256]{1,0:T(8,128)(2,1)S(1)} %get-tuple-element.29), channel_id=1, source_target_pairs={{0,16},{16,0},{1,17},{17,1},{2,18},{18,2},{3,19},{19,3},{4,20},{20... | collective-permute-start | bytes 98312 | tf_op jit(solution)/shard_map/ppermute | solution.py:352
  161.6 4.4 %all-to-all-start.3 = ((bf16[8,64,256]{2,1,0:T(8,128)(2,1)}), bf16[8,64,256]{2,1,0:T(8,128)(2,1)S(1)}, u32[]{:S(2)}, u32[]{:S(2)}) async-start(bf16[8,64,256]{2,1,0:T(8,128)(2,1)} %get-tuple-element.27), calls=%async_computation.3 | async-start | bytes 524288 | tf_op jit(solution)/shard_map/all_to_all | solution.py:279
  166.0 10.8 %all_gather.12.part_ref = bf16[4,64,512]{2,1,0:T(8,128)(2,1)S(1)} all-gather(bf16[1,64,512]{2,1,0:T(8,128)(2,1)S(1)} %maximum_select_fusion.4), channel_id=1, replica_groups=mesh['zh'=4,'zl'=4,'core'=2,'tensor'=4,'dp'=4] {'dp'}, dimensions={0}, use_global_device_ids=true | all-gather | bytes 327680 | tf_op jit(solution)/shard_map/all_gather | solution.py:359
  176.8 0.7 shard_map.123
  177.5 0.7 reduce_sum.25
  (22 shorter events, 0.2 us)
Async XLA Ops:
  3.6 40.2 %copy-start.3 = (bf16[208,128]{1,0:T(8,128)(2,1)S(1)}, bf16[208,128]{1,0:T(8,128)(2,1)}, u32[]{:S(2)}) copy-start(bf16[208,128]{1,0:T(8,128)(2,1)} %get-tuple-element.17) | copy-start | bytes 159748
  3.7 10.9 %collective-permute-start.1 = (bf16[208,128]{1,0:T(8,128)(2,1)}, bf16[208,128]{1,0:T(8,128)(2,1)S(1)}, u32[]{:S(2)}, u32[]{:S(2)}) collective-permute-start(bf16[208,128]{1,0:T(8,128)(2,1)} %get-tuple-element.18), channel_id=1, source_target_pairs={{0,16},{16,0},{1,17},{17,1},{2,18},{18,2},{3,19},{19,3},{4,20},{20... | collective-permute-start | bytes 159752 | tf_op jit(solution)/shard_map/ppermute | solution.py:320
  12.6 64.5 %collective-permute-start = (bf16[512,2048]{1,0:T(8,128)(2,1)}, bf16[512,2048]{1,0:T(8,128)(2,1)}, u32[]{:S(2)}, u32[]{:S(2)}) collective-permute-start(bf16[512,2048]{1,0:T(8,128)(2,1)} %bitcast.58), channel_id=1, source_target_pairs={{0,16},{16,0},{1,17},{17,1},{2,18},{18,2},{3,19},{19,3},{4,20},{20... | collective-permute-start | bytes 6291464 | tf_op jit(solution)/shard_map/ppermute | solution.py:301
  43.8 1.7 copy-start.1
  45.5 31.5 %copy-start = (s32[2]{0:T(128)S(1)}, s32[2]{0:T(128)}, u32[]{:S(2)}) copy-start(s32[2]{0:T(128)} %pad_add_fusion.place_ref) | copy-start | bytes 28
  45.5 31.5 %all-to-all-start = ((bf16[4,2048,128]{2,1,0:T(8,128)(2,1)}), bf16[4,2048,128]{2,1,0:T(8,128)(2,1)}, u32[]{:S(2)}, u32[]{:S(2)}) async-start(bf16[4,2048,128]{2,1,0:T(8,128)(2,1)} %broadcast_in_dim.16), calls=%async_computation | async-start | bytes 4194304 | tf_op jit(solution)/shard_map/all_to_all | solution.py:279
  90.8 25.4 %all-to-all-start.1 = ((bf16[16,16,1024]{2,1,0:T(8,128)(2,1)}), bf16[16,16,1024]{2,1,0:T(8,128)(2,1)S(1)}, u32[]{:S(2)}, u32[]{:S(2)}) async-start(bf16[16,16,1024]{2,1,0:T(8,128)(2,1)} %bitcast.11), calls=%async_computation.1 | async-start | bytes 1048576 | tf_op jit(solution)/shard_map/all_to_all | solution.py:279
  98.7 16.2 %collective-permute-start.2 = (bf16[512,512]{1,0:T(8,128)(2,1)S(1)}, bf16[512,512]{1,0:T(8,128)(2,1)S(1)}, u32[]{:S(2)}, u32[]{:S(2)}) collective-permute-start(bf16[512,512]{1,0:T(8,128)(2,1)S(1)} %get-tuple-element.23), channel_id=1, source_target_pairs={{0,16},{16,0},{1,17},{17,1},{2,18},{18,2},{3,19},{19,3},{4,20},{20... | collective-permute-start | bytes 1572872 | tf_op jit(solution)/shard_map/ppermute | solution.py:332
  115.0 14.0 %copy-start.4 = (bf16[64,512]{1,0:T(8,128)(2,1)S(1)}, bf16[64,512]{1,0:T(8,128)(2,1)}, u32[]{:S(2)}) copy-start(bf16[64,512]{1,0:T(8,128)(2,1)} %param.12) | copy-start | bytes 196612
  115.0 14.0 %copy-start.2 = (bf16[1,1024,64]{1,2,0:T(8,128)(2,1)S(1)}, bf16[1,1024,64]{1,2,0:T(8,128)(2,1)}, u32[]{:S(2)}) copy-start(bf16[1,1024,64]{1,2,0:T(8,128)(2,1)} %param.17) | copy-start | bytes 393220
  117.2 28.6 %all-to-all-start.2 = ((bf16[16,16,1024]{2,1,0:T(8,128)(2,1)}), bf16[16,16,1024]{2,1,0:T(8,128)(2,1)S(1)}, u32[]{:S(2)}, u32[]{:S(2)}) async-start(bf16[16,16,1024]{2,1,0:T(8,128)(2,1)} %broadcast_in_dim.17), calls=%async_computation.2 | async-start | bytes 1048576 | tf_op jit(solution)/shard_map/all_to_all | solution.py:279
  129.0 12.0 %collective-permute-start.3 = (bf16[64,1280]{1,0:T(8,128)(2,1)S(1)}, bf16[64,1280]{1,0:T(8,128)(2,1)S(1)}, u32[]{:S(2)}, u32[]{:S(2)}) collective-permute-start(bf16[64,1280]{1,0:T(8,128)(2,1)S(1)} %pad_maximum_fusion), channel_id=1, source_target_pairs={{0,16},{16,0},{1,17},{17,1},{2,18},{18,2},{3,19},{19,3},{4,20},{20... | collective-permute-start | bytes 491528 | tf_op jit(solution)/shard_map/ppermute | solution.py:306
  147.6 18.4 %collective-permute-start.4 = (bf16[64,256]{1,0:T(8,128)(2,1)S(1)}, bf16[64,256]{1,0:T(8,128)(2,1)S(1)}, u32[]{:S(2)}, u32[]{:S(2)}) collective-permute-start(bf16[64,256]{1,0:T(8,128)(2,1)S(1)} %get-tuple-element.29), channel_id=1, source_target_pairs={{0,16},{16,0},{1,17},{17,1},{2,18},{18,2},{3,19},{19,3},{4,20},{20... | collective-permute-start | bytes 98312 | tf_op jit(solution)/shard_map/ppermute | solution.py:352
  161.6 15.9 %all-to-all-start.3 = ((bf16[8,64,256]{2,1,0:T(8,128)(2,1)}), bf16[8,64,256]{2,1,0:T(8,128)(2,1)S(1)}, u32[]{:S(2)}, u32[]{:S(2)}) async-start(bf16[8,64,256]{2,1,0:T(8,128)(2,1)} %get-tuple-element.27), calls=%async_computation.3 | async-start | bytes 524288 | tf_op jit(solution)/shard_map/all_to_all | solution.py:279

commit v9 on v8

--- a/solution.py
+++ b/solution.py
@@ -24,7 +24,7 @@
 
 
 def pack_kernel(place_ref, *refs):
-    sources, outs, landing, arrived = refs[:6], refs[6:8], refs[8:14], refs[14]
+    sources, outs, landing, tile, arrived = refs[:6], refs[6:8], refs[8:14], refs[14], refs[15]
     copies = [
         pltpu.make_async_copy(source, target, arrived.at[i])
         for i, (source, target) in enumerate(zip(sources, landing))
@@ -56,7 +56,12 @@
         column = pl.multiple_of(core * half + lax.rem(batch, 2) * size, size)
         mine = jnp.where(core == 0, exact[0], exact[1])
         high = mine.astype(BF).astype(F32)
-        stats = jnp.concatenate([high, mine - high], axis=0).astype(BF)
+        last = pl.ds(pl.multiple_of(core * half + half - size, size), size)
+        tile[...] = grad_ref[rows - 16 :, last].astype(F32)
+        for i in range(heads):
+            tile[0:1, i * rows : (i + 1) * rows] = high[i : i + 1]
+            tile[1:2, i * rows : (i + 1) * rows] = (mine - high)[i : i + 1]
+        block_ref[depth : depth + 16] = tile[...].astype(BF)
 
         @pl.when(batch < 2)
         def _():
@@ -66,16 +71,12 @@
         def _():
             block_ref[:depth] = value_ref[:, pl.ds(column, size)]
 
-        first = depth
+        first = depth + 16
         for ref in (query_ref, grad_ref):
             for lo in range(0, half, size):
                 here = pl.ds(pl.multiple_of(core * half + lo, size), size)
                 block_ref[first : first + rows] = ref[:, here]
                 first += rows
-                if first == depth + rows:
-                    block_ref[first : first + 16] = jnp.zeros((16, size), BF)
-                    block_ref[first : first + 2 * heads, :rows] = stats
-                    first += 16
 
 
 def pack(place, key_weight, value_weight, query, grad, out, lse):
@@ -89,21 +90,21 @@
         out_specs=[pl.BlockSpec(memory_space=pltpu.VMEM)] * 2,
         out_shape=[jax.ShapeDtypeStruct((depth + 16 + 4 * query.shape[0], size), BF)] * 2,
         scratch_shapes=[pltpu.VMEM(x.shape, x.dtype) for x in sources]
-        + [pltpu.SemaphoreType.DMA((len(sources),))],
+        + [pltpu.VMEM((16, size), F32), pltpu.SemaphoreType.DMA((len(sources),))],
         compiler_params=pltpu.CompilerParams(vmem_limit_bytes=60 * 2**20),
         cost_estimate=pl.CostEstimate(flops=0, bytes_accessed=2**19, transcendentals=0),
     )(place, *sources)
 
 
 def attend_kernel(
-    place_ref, own_in, other_in, slab_ref, head_ref, stat_ref, rest_ref, own_ref, other_ref, part_ref,
-    weight, kv, query, grad, qt, gt, pieces, stats, total,
+    place_ref, own_in, other_in, slab_ref, tile_ref, rest_ref, own_ref, other_ref, part_ref,
+    weight, kv, query, grad, qt, gt, stats, total,
     size, scaling, latent_factor, prefix_factor,
 ):
     step = pl.program_id(0)
     last = pl.num_programs(0) - 1
     half = pl.num_programs(0) // 2
-    ranks = head_ref.shape[0]
+    ranks = tile_ref.shape[0]
     rows = query.shape[0] // ranks
 
     @pl.when(step == 0)
@@ -117,12 +118,17 @@
                     slab, there
                 ]
             here = slice(rank * rows, (rank + 1) * rows)
-            query[here, :size] = head_ref[at]
-            query[here, size:] = rest_ref[at, :rows]
-            grad[here, :size] = rest_ref[at, rows : 2 * rows]
-            grad[here, size:] = rest_ref[at, 2 * rows :]
-            pieces[:, here] = stat_ref[at].astype(F32)[:8, :rows]
-        stats[...] = pieces[:4] + pieces[4:]
+            query[here, :size] = rest_ref[at, :rows]
+            query[here, size:] = rest_ref[at, rows : 2 * rows]
+            grad[here, :size] = rest_ref[at, 2 * rows : 3 * rows]
+            end = rank * rows + rows - 16
+            grad[rank * rows : end, size:] = rest_ref[at, 3 * rows : 4 * rows - 16]
+            grad[end : end + 16, size:] = tile_ref[at]
+            grad[end : end + 2, size:] = rest_ref[at, 4 * rows - 16 :]
+            tile = tile_ref[at].astype(F32)
+            dense = tile[0:1] + tile[1:2]
+            for i in range(4):
+                stats[i : i + 1, here] = dense[:, i * rows : (i + 1) * rows]
         qt[...] = query[...].T
         gt[...] = grad[...].T
         total[...] = jnp.zeros_like(total)
@@ -168,7 +174,7 @@
     columns = count * size
     ranks = first_rows.shape[0]
     rows = latents // ranks
-    depth = first_rows.shape[1] - 16 - rows
+    depth = first_rows.shape[1] - 16
     block = 256
     half = tokens // block
     kernel = functools.partial(
@@ -186,8 +192,7 @@
             pl.BlockSpec((block, width), lambda t: (jnp.minimum(t, half - 1), 0)),
             pl.BlockSpec((block, width), lambda t: (jnp.maximum(t - half, 0), 0)),
             pl.BlockSpec(slabs.shape, lambda t: (0, 0, 0)),
-            pl.BlockSpec((ranks, rows, size), lambda t: (0, depth // rows, 0)),
-            pl.BlockSpec((ranks, 16, size), lambda t: (0, (depth + rows) // 16, 0)),
+            pl.BlockSpec((ranks, 16, size), lambda t: (0, depth // 16, 0)),
             pl.BlockSpec(last_rows.shape, lambda t: (0, 0, 0)),
         ],
         out_specs=[
@@ -207,7 +212,6 @@
             pltpu.VMEM((latents, 2 * size), BF),
             pltpu.VMEM((2 * size, latents), BF),
             pltpu.VMEM((2 * size, latents), BF),
-            pltpu.VMEM((8, latents), F32),
             pltpu.VMEM((4, latents), F32),
             pltpu.VMEM((2 * size, latents), F32),
         ],
@@ -217,7 +221,7 @@
             bytes_accessed=6 * 2**20,
             transcendentals=4 * tokens * latents,
         ),
-    )(place, own, other, slabs, first_rows, first_rows, last_rows)
+    )(place, own, other, slabs, first_rows, last_rows)
 
 
 def tail_kernel(place_ref, query_ref, latent_ref, every_ref, latent_out, mine_out, theirs_out):
@@ -318,11 +322,12 @@
         place, key_weight, value_weight, queries[0], out_grad[0], attn_out[0], shifted_lse[0].T
     )
     blocks = jnp.stack([mine, lax.ppermute(theirs, "core", SWAP)])
-    cut = depth + 16 + rows
-    first_rows = lax.all_gather(blocks[:, :cut], Z, axis=0, tiled=True)
+    cut = depth + 16
+    ranks_z = lax.axis_size(Z)
+    first_rows = exchange(jnp.broadcast_to(blocks[:, :cut], (ranks_z, 2, cut, size)), Z).reshape(ranks, cut, size)
     slab = first_rows[:, :depth].reshape(-1, size)
     slabs = jnp.broadcast_to(slab[None], (batches,) + slab.shape)
-    slabs, rest = lax.optimization_barrier((slabs, blocks[:, cut:]))
+    slabs, rest = lax.optimization_barrier((slabs, blocks[:, cut : cut + 4 * rows - 14]))
     slabs = exchange(slabs, "dp")
     last_rows = lax.all_gather(rest, Z, axis=0, tiled=True)
 
@@ -341,7 +346,7 @@
     share = exchange(part.reshape(lax.axis_size(Z), -1, latents), Z)
     share = jnp.sum(share.astype(F32), axis=0).astype(BF)
     share, key_grad, value_grad = lax.optimization_barrier((share, whole(0), whole(half)))
-    every = exchange(jnp.broadcast_to(share, (lax.axis_size(Z),) + share.shape), Z).reshape(part.shape)
+    every = exchange(jnp.broadcast_to(share, (ranks_z,) + share.shape), Z).reshape(part.shape)
     latent_part, weight_mine, weight_theirs = tail(
         place, query_both, latent_both, every, lax.axis_size("tensor")
     )

time: 181 us -> 204 us (1.13)
  waiting for transfers between devices: 7.13 us -> 53.1 us
  blocking collectives: 66.3 us -> 45.1 us
  starting transfers between devices: 78.9 us -> 75.8 us
    all_to_all x4 -> x5, waiting for transfers between devices: 4.65 us -> 49.5 us  [exchange(): return lax.all_to_all(x, axes, 0, 0, tiled=True)]
    all_gather x1 -> x0, blocking collectives: 28.5 us -> none  [local(): first_rows = lax.all_gather(blocks[:, :cut], Z, axis=0, tiled=True)]
    all_to_all x4 -> x5, starting transfers between devices: 28.5 us -> 41.5 us  [exchange(): return lax.all_to_all(x, axes, 0, 0, tiled=True)]
    all_gather x1, blocking collectives: 27 us -> 34.8 us  [local(): last_rows = lax.all_gather(rest, Z, axis=0, tiled=True)]
    ppermute x1, starting transfers between devices: 14.7 us -> 7.56 us  [local(): theirs = lax.ppermute(other_grads, 'core', SWAP)]
    ppermute x1, starting transfers between devices: 11 us -> 5.2 us  [local(): lax.ppermute(jnp.concatenate([latent_own, query_theirs], axis=1), 'core',...]
    ppermute x1, starting transfers between devices: 13.9 us -> 10.1 us  [local(): weight_other = lax.ppermute(weight_theirs, 'core', SWAP)]
  transfers between devices with their start and end apart: 9 -> 10, of which waited for: 3 -> 6; matrix products, arithmetic and copies ran while one was open for 2% -> 2% of each run, Pallas kernels for 0% -> 0%
where the time goes in v9:
time: 204 us; the launch traced here: 201 us
  starting transfers between devices  75.8 us (37%)
  waiting for transfers between devices  53.1 us (26%)
  blocking collectives  45.1 us (22%)
  Pallas kernels  19.1 us (9%)
  local copies, waits for them, and re-layouts  3.61 us (2%)
  other arithmetic  3.43 us (2%)
    all_to_all x5, waiting for transfers between devices, exchange(): return lax.all_to_all(x, axes, 0, 0, tiled=True)  49.5 us
    all_to_all x5, starting transfers between devices, exchange(): return lax.all_to_all(x, axes, 0, 0, tiled=True)  41.5 us
    all_gather x1, blocking collectives, local(): last_rows = lax.all_gather(rest, Z, axis=0, tiled=True)  34.8 us
    pallas_call x1, Pallas kernels, attend(): pl.pallas_call(kernel, grid=(2 * half,), in_specs=[pl.BlockSpec(memory_sp...  13.8 us
    all_gather x1, blocking collectives, local(): lax.all_gather(weight_rows, 'dp')  10.3 us
    ppermute x1, starting transfers between devices, local(): weight_other = lax.ppermute(weight_theirs, 'core', SWAP)  10.1 us
    ppermute x1, starting transfers between devices, local(): blocks = jnp.stack([mine, lax.ppermute(theirs, 'core', SWAP)])  8.92 us
    ppermute x1, starting transfers between devices, local(): theirs = lax.ppermute(other_grads, 'core', SWAP)  7.56 us
  transfers between devices with their start and end apart: 10, of which 6 were waited for; matrix products, arithmetic and copies ran while one was open for 2% of the time, Pallas kernels for 0%

profile of v9, /device:TPU:1, one launch (start us, length us, event | category | flops | bytes accessed | tf_op | source)
XLA Modules:
  0.0 201.1 jit_solution(7604955951457290134)
XLA Ops:
  0.6 0.6 pad_add_fusion.place_ref
  1.3 2.7 %shard_map.120 = (bf16[208,128]{1,0:T(8,128)(2,1)}, bf16[208,128]{1,0:T(8,128)(2,1)}) custom-call(s32[2]{0:T(128)} %pad_add_fusion.place_ref, bf16[64,512]{1,0:T(8,128)(2,1)} %refs_0_.1, bf16[64,512]{1,0:T(8,128)(2,1)} %refs_1_.1, bf16[32,512]{1,0:T(8,128)(2,1)} %bitcast.55, bf16[32,512]{1,0:T(8,128)(2,1)} %bitcast.56, bf16[32,512]{1,0:T(8,128)(2,1)} %bitcast.57, ...), custom_call_target="tpu_custom_call" | custom-call | bytes 524288 | tf_op jit(solution)/shard_map/pallas_call | solution.py:86
  4.0 8.9 %collective-permute-start.1 = (bf16[208,128]{1,0:T(8,128)(2,1)}, bf16[208,128]{1,0:T(8,128)(2,1)S(1)}, u32[]{:S(2)}, u32[]{:S(2)}) collective-permute-start(bf16[208,128]{1,0:T(8,128)(2,1)} %get-tuple-element.18), channel_id=1, source_target_pairs={{0,16},{16,0},{1,17},{17,1},{2,18},{18,2},{3,19},{19,3},{4,20},{20... | collective-permute-start | bytes 159752 | tf_op jit(solution)/shard_map/ppermute | solution.py:324
  12.9 1.1 collective-permute-done.1
  14.0 0.7 pad_maximum_fusion.2
  14.7 0.9 broadcast_in_dim.18
  15.7 9.5 %all-to-all-start = ((bf16[16,2,80,128]{3,2,1,0:T(8,128)(2,1)}), bf16[16,2,80,128]{3,2,1,0:T(8,128)(2,1)S(1)}, u32[]{:S(2)}, u32[]{:S(2)}) async-start(bf16[16,2,80,128]{3,2,1,0:T(8,128)(2,1)} %broadcast_in_dim.18), calls=%async_computation | async-start | bytes 1310720 | tf_op jit(solution)/shard_map/all_to_all | solution.py:283
  25.2 2.5 %collective-permute-start = (bf16[512,2048]{1,0:T(8,128)(2,1)S(1)}, bf16[512,2048]{1,0:T(8,128)(2,1)}, u32[]{:S(2)}, u32[]{:S(2)}) collective-permute-start(bf16[512,2048]{1,0:T(8,128)(2,1)S(1)} %bitcast.62), channel_id=1, source_target_pairs={{0,16},{16,0},{1,17},{17,1},{2,18},{18,2},{3,19},{19,3},{4,20},{20... | collective-permute-start | bytes 6291464 | tf_op jit(solution)/shard_map/ppermute | solution.py:305
  27.8 26.3 %all-to-all-done = bf16[16,2,80,128]{3,2,1,0:T(8,128)(2,1)S(1)} async-done(((bf16[16,2,80,128]{3,2,1,0:T(8,128)(2,1)}), bf16[16,2,80,128]{3,2,1,0:T(8,128)(2,1)S(1)}, u32[]{:S(2)}, u32[]{:S(2)}) %all-to-all-start) | async-done | bytes 655392 | tf_op jit(solution)/shard_map/all_to_all | solution.py:283
  54.1 0.1 slice.46
  54.2 1.6 broadcast_in_dim.20
  55.8 4.4 %all-to-all-start.1 = ((bf16[4,2048,128]{2,1,0:T(8,128)(2,1)}), bf16[4,2048,128]{2,1,0:T(8,128)(2,1)}, u32[]{:S(2)}, u32[]{:S(2)}) async-start(bf16[4,2048,128]{2,1,0:T(8,128)(2,1)} %broadcast_in_dim.20), calls=%async_computation.1 | async-start | bytes 4194304 | tf_op jit(solution)/shard_map/all_to_all | solution.py:283
  60.3 34.8 %all_gather.7.rest_ref = bf16[32,114,128]{2,1,0:T(8,128)(2,1)} all-gather(bf16[2,114,128]{2,1,0:T(8,128)(2,1)S(1)} %pad_maximum_fusion.1), channel_id=1, replica_groups=mesh['zh'=4,'zl'=4,'core'=2,'tensor'=4,'dp'=4] {'zh','zl'}, dimensions={0}, use_global_device_ids=true | all-gather | bytes 992256 | tf_op jit(solution)/shard_map/all_gather | solution.py:332
  95.1 13.8 %shard_map.121 = (bf16[512,512]{1,0:T(8,128)(2,1)S(1)}, bf16[512,512]{1,0:T(8,128)(2,1)S(1)}, bf16[256,1024]{1,0:T(8,128)(2,1)}) custom-call(s32[2]{0:T(128)S(1)} %copy-done, bf16[512,2048]{1,0:T(8,128)(2,1)} %bitcast.61, bf16[512,2048]{1,0:T(8,128)(2,1)} %collective-permute-done.other_in, bf16[4,2048,128]{2,1,0:T(8,128)(2,1)} %all-to-all-done.1.slab_ref, ...), custom_call_target="tpu_custom_call" | custom-call | flops 2684354560 | bytes 6291456 | tf_op jit(solution)/shard_map/pallas_call | solution.py:187
  108.9 9.5 %all-to-all-start.2 = ((bf16[16,16,1024]{2,1,0:T(8,128)(2,1)}), bf16[16,16,1024]{2,1,0:T(8,128)(2,1)S(1)}, u32[]{:S(2)}, u32[]{:S(2)}) async-start(bf16[16,16,1024]{2,1,0:T(8,128)(2,1)} %bitcast.12), calls=%async_computation.2 | async-start | bytes 1048576 | tf_op jit(solution)/shard_map/all_to_all | solution.py:283
  118.4 7.6 %collective-permute-start.2 = (bf16[512,512]{1,0:T(8,128)(2,1)S(1)}, bf16[512,512]{1,0:T(8,128)(2,1)S(1)}, u32[]{:S(2)}, u32[]{:S(2)}) collective-permute-start(bf16[512,512]{1,0:T(8,128)(2,1)S(1)} %get-tuple-element.23), channel_id=1, source_target_pairs={{0,16},{16,0},{1,17},{17,1},{2,18},{18,2},{3,19},{19,3},{4,20},{20... | collective-permute-start | bytes 1572872 | tf_op jit(solution)/shard_map/ppermute | solution.py:337
  126.0 1.5 collective-permute-done.2
  127.5 1.2 maximum_select_fusion
  128.8 9.0 %all-to-all-done.2 = bf16[16,16,1024]{2,1,0:T(8,128)(2,1)S(1)} async-done(((bf16[16,16,1024]{2,1,0:T(8,128)(2,1)}), bf16[16,16,1024]{2,1,0:T(8,128)(2,1)S(1)}, u32[]{:S(2)}, u32[]{:S(2)}) %all-to-all-start.2) | async-done | bytes 524320 | tf_op jit(solution)/shard_map/all_to_all | solution.py:283
  137.7 0.1 reduce_sum.24
  137.8 0.9 broadcast_in_dim.21
  138.7 13.7 %all-to-all-start.3 = ((bf16[16,16,1024]{2,1,0:T(8,128)(2,1)}), bf16[16,16,1024]{2,1,0:T(8,128)(2,1)S(1)}, u32[]{:S(2)}, u32[]{:S(2)}) async-start(bf16[16,16,1024]{2,1,0:T(8,128)(2,1)} %broadcast_in_dim.21), calls=%async_computation.3 | async-start | bytes 1048576 | tf_op jit(solution)/shard_map/all_to_all | solution.py:283
  152.5 5.2 %collective-permute-start.3 = (bf16[64,1280]{1,0:T(8,128)(2,1)S(1)}, bf16[64,1280]{1,0:T(8,128)(2,1)S(1)}, u32[]{:S(2)}, u32[]{:S(2)}) collective-permute-start(bf16[64,1280]{1,0:T(8,128)(2,1)S(1)} %pad_maximum_fusion), channel_id=1, source_target_pairs={{0,16},{16,0},{1,17},{17,1},{2,18},{18,2},{3,19},{19,3},{4,20},{20... | collective-permute-start | bytes 491528 | tf_op jit(solution)/shard_map/ppermute | solution.py:310
  157.7 1.0 collective-permute-done.3
  158.7 0.1 maximum_select_fusion.2.latent_ref
  158.8 14.2 %all-to-all-done.3 = bf16[16,16,1024]{2,1,0:T(8,128)(2,1)S(1)} async-done(((bf16[16,16,1024]{2,1,0:T(8,128)(2,1)}), bf16[16,16,1024]{2,1,0:T(8,128)(2,1)S(1)}, u32[]{:S(2)}, u32[]{:S(2)}) %all-to-all-start.3) | async-done | bytes 524320 | tf_op jit(solution)/shard_map/all_to_all | solution.py:283
  173.0 1.9 shard_map.122
  174.9 10.1 %collective-permute-start.4 = (bf16[64,256]{1,0:T(8,128)(2,1)S(1)}, bf16[64,256]{1,0:T(8,128)(2,1)S(1)}, u32[]{:S(2)}, u32[]{:S(2)}) collective-permute-start(bf16[64,256]{1,0:T(8,128)(2,1)S(1)} %get-tuple-element.29), channel_id=1, source_target_pairs={{0,16},{16,0},{1,17},{17,1},{2,18},{18,2},{3,19},{19,3},{4,20},{20... | collective-permute-start | bytes 98312 | tf_op jit(solution)/shard_map/ppermute | solution.py:357
  185.0 4.4 %all-to-all-start.4 = ((bf16[8,64,256]{2,1,0:T(8,128)(2,1)}), bf16[8,64,256]{2,1,0:T(8,128)(2,1)S(1)}, u32[]{:S(2)}, u32[]{:S(2)}) async-start(bf16[8,64,256]{2,1,0:T(8,128)(2,1)} %get-tuple-element.27), calls=%async_computation.4 | async-start | bytes 524288 | tf_op jit(solution)/shard_map/all_to_all | solution.py:283
  189.4 10.3 %all_gather.8.part_ref = bf16[4,64,512]{2,1,0:T(8,128)(2,1)S(1)} all-gather(bf16[1,64,512]{2,1,0:T(8,128)(2,1)S(1)} %maximum_select_fusion.4), channel_id=1, replica_groups=mesh['zh'=4,'zl'=4,'core'=2,'tensor'=4,'dp'=4] {'dp'}, dimensions={0}, use_global_device_ids=true | all-gather | bytes 327680 | tf_op jit(solution)/shard_map/all_gather | solution.py:364
  199.8 0.7 shard_map.123
  200.5 0.7 reduce_sum.25
  (26 shorter events, 0.2 us)
Async XLA Ops:
  0.6 24.6 %copy-start.5 = (bf16[1,512,2048]{2,1,0:T(8,128)(2,1)S(1)}, bf16[1,512,2048]{2,1,0:T(8,128)(2,1)}, u32[]{:S(2)}) copy-start(bf16[1,512,2048]{2,1,0:T(8,128)(2,1)} %param.9) | copy-start | bytes 6291460
  4.0 23.8 %copy-start.3 = (bf16[208,128]{1,0:T(8,128)(2,1)S(1)}, bf16[208,128]{1,0:T(8,128)(2,1)}, u32[]{:S(2)}) copy-start(bf16[208,128]{1,0:T(8,128)(2,1)} %get-tuple-element.17) | copy-start | bytes 159748
  4.0 10.0 %collective-permute-start.1 = (bf16[208,128]{1,0:T(8,128)(2,1)}, bf16[208,128]{1,0:T(8,128)(2,1)S(1)}, u32[]{:S(2)}, u32[]{:S(2)}) collective-permute-start(bf16[208,128]{1,0:T(8,128)(2,1)} %get-tuple-element.18), channel_id=1, source_target_pairs={{0,16},{16,0},{1,17},{17,1},{2,18},{18,2},{3,19},{19,3},{4,20},{20... | collective-permute-start | bytes 159752 | tf_op jit(solution)/shard_map/ppermute | solution.py:324
  15.7 38.5 %all-to-all-start = ((bf16[16,2,80,128]{3,2,1,0:T(8,128)(2,1)}), bf16[16,2,80,128]{3,2,1,0:T(8,128)(2,1)S(1)}, u32[]{:S(2)}, u32[]{:S(2)}) async-start(bf16[16,2,80,128]{3,2,1,0:T(8,128)(2,1)} %broadcast_in_dim.18), calls=%async_computation | async-start | bytes 1310720 | tf_op jit(solution)/shard_map/all_to_all | solution.py:283
  25.2 69.9 %collective-permute-start = (bf16[512,2048]{1,0:T(8,128)(2,1)S(1)}, bf16[512,2048]{1,0:T(8,128)(2,1)}, u32[]{:S(2)}, u32[]{:S(2)}) collective-permute-start(bf16[512,2048]{1,0:T(8,128)(2,1)S(1)} %bitcast.62), channel_id=1, source_target_pairs={{0,16},{16,0},{1,17},{17,1},{2,18},{18,2},{3,19},{19,3},{4,20},{20... | collective-permute-start | bytes 6291464 | tf_op jit(solution)/shard_map/ppermute | solution.py:305
  54.1 1.7 copy-start.1
  55.8 39.3 %copy-start = (s32[2]{0:T(128)S(1)}, s32[2]{0:T(128)}, u32[]{:S(2)}) copy-start(s32[2]{0:T(128)} %pad_add_fusion.place_ref) | copy-start | bytes 28
  55.8 39.3 %all-to-all-start.1 = ((bf16[4,2048,128]{2,1,0:T(8,128)(2,1)}), bf16[4,2048,128]{2,1,0:T(8,128)(2,1)}, u32[]{:S(2)}, u32[]{:S(2)}) async-start(bf16[4,2048,128]{2,1,0:T(8,128)(2,1)} %broadcast_in_dim.20), calls=%async_computation.1 | async-start | bytes 4194304 | tf_op jit(solution)/shard_map/all_to_all | solution.py:283
  108.9 28.8 %all-to-all-start.2 = ((bf16[16,16,1024]{2,1,0:T(8,128)(2,1)}), bf16[16,16,1024]{2,1,0:T(8,128)(2,1)S(1)}, u32[]{:S(2)}, u32[]{:S(2)}) async-start(bf16[16,16,1024]{2,1,0:T(8,128)(2,1)} %bitcast.12), calls=%async_computation.2 | async-start | bytes 1048576 | tf_op jit(solution)/shard_map/all_to_all | solution.py:283
  118.4 9.1 %collective-permute-start.2 = (bf16[512,512]{1,0:T(8,128)(2,1)S(1)}, bf16[512,512]{1,0:T(8,128)(2,1)S(1)}, u32[]{:S(2)}, u32[]{:S(2)}) collective-permute-start(bf16[512,512]{1,0:T(8,128)(2,1)S(1)} %get-tuple-element.23), channel_id=1, source_target_pairs={{0,16},{16,0},{1,17},{17,1},{2,18},{18,2},{3,19},{19,3},{4,20},{20... | collective-permute-start | bytes 1572872 | tf_op jit(solution)/shard_map/ppermute | solution.py:337
  127.5 24.9 %copy-start.4 = (bf16[64,512]{1,0:T(8,128)(2,1)S(1)}, bf16[64,512]{1,0:T(8,128)(2,1)}, u32[]{:S(2)}) copy-start(bf16[64,512]{1,0:T(8,128)(2,1)} %param.12) | copy-start | bytes 196612
  127.5 24.9 %copy-start.2 = (bf16[1,1024,64]{1,2,0:T(8,128)(2,1)S(1)}, bf16[1,1024,64]{1,2,0:T(8,128)(2,1)}, u32[]{:S(2)}) copy-start(bf16[1,1024,64]{1,2,0:T(8,128)(2,1)} %param.17) | copy-start | bytes 393220
  138.7 34.3 %all-to-all-start.3 = ((bf16[16,16,1024]{2,1,0:T(8,128)(2,1)}), bf16[16,16,1024]{2,1,0:T(8,128)(2,1)S(1)}, u32[]{:S(2)}, u32[]{:S(2)}) async-start(bf16[16,16,1024]{2,1,0:T(8,128)(2,1)} %broadcast_in_dim.21), calls=%async_computation.3 | async-start | bytes 1048576 | tf_op jit(solution)/shard_map/all_to_all | solution.py:283
  152.5 6.2 %collective-permute-start.3 = (bf16[64,1280]{1,0:T(8,128)(2,1)S(1)}, bf16[64,1280]{1,0:T(8,128)(2,1)S(1)}, u32[]{:S(2)}, u32[]{:S(2)}) collective-permute-start(bf16[64,1280]{1,0:T(8,128)(2,1)S(1)} %pad_maximum_fusion), channel_id=1, source_target_pairs={{0,16},{16,0},{1,17},{17,1},{2,18},{18,2},{3,19},{19,3},{4,20},{20... | collective-permute-start | bytes 491528 | tf_op jit(solution)/shard_map/ppermute | solution.py:310
  174.9 14.5 %collective-permute-start.4 = (bf16[64,256]{1,0:T(8,128)(2,1)S(1)}, bf16[64,256]{1,0:T(8,128)(2,1)S(1)}, u32[]{:S(2)}, u32[]{:S(2)}) collective-permute-start(bf16[64,256]{1,0:T(8,128)(2,1)S(1)} %get-tuple-element.29), channel_id=1, source_target_pairs={{0,16},{16,0},{1,17},{17,1},{2,18},{18,2},{3,19},{19,3},{4,20},{20... | collective-permute-start | bytes 98312 | tf_op jit(solution)/shard_map/ppermute | solution.py:357
  185.0 15.5 %all-to-all-start.4 = ((bf16[8,64,256]{2,1,0:T(8,128)(2,1)}), bf16[8,64,256]{2,1,0:T(8,128)(2,1)S(1)}, u32[]{:S(2)}, u32[]{:S(2)}) async-start(bf16[8,64,256]{2,1,0:T(8,128)(2,1)} %get-tuple-element.27), calls=%async_computation.4 | async-start | bytes 524288 | tf_op jit(solution)/shard_map/all_to_all | solution.py:283

commit v10 on v8

--- a/solution.py
+++ b/solution.py
@@ -9,6 +9,7 @@
 from jax.sharding import Mesh, PartitionSpec as P
 
 BF = jnp.bfloat16
+F16 = jnp.float16
 F32 = jnp.float32
 SEQ = ("zh", "zl", "core")
 Z = ("zh", "zl")
@@ -23,8 +24,20 @@
     return lax.dot_general(a, b, (((1,), (1,)), ((), ())), preferred_element_type=F32)
 
 
+def power(*arrays):
+    most = jnp.full((1, 1), 1e-38, F32)
+    for x in arrays:
+        peak = jnp.max(jnp.abs(x.astype(F32)), axis=0, keepdims=True)
+        most = jnp.maximum(most, jnp.max(peak, axis=1, keepdims=True))
+    return jnp.clip(13.0 - jnp.floor(jnp.log(most) * (1.0 / math.log(2.0))), -126.0, 126.0)
+
+
+def scaled(x, exponent):
+    return (x.astype(F32) * jnp.exp2(exponent)).astype(BF)
+
+
 def pack_kernel(place_ref, *refs):
-    sources, outs, landing, arrived = refs[:6], refs[6:8], refs[8:14], refs[14]
+    sources, outs, landing, tile, arrived = refs[:6], refs[6:8], refs[8:14], refs[14], refs[15]
     copies = [
         pltpu.make_async_copy(source, target, arrived.at[i])
         for i, (source, target) in enumerate(zip(sources, landing))
@@ -47,6 +60,11 @@
         one = jnp.sum(product[:, head * size : (head + 1) * size], axis=1, keepdims=True)
         delta = jnp.where(lane == head, one, delta)
     lse, delta = lse_ref[...], delta.T[:heads]
+    weight_power = power(key_ref[...], value_ref[...])
+    query_power = power(query_ref[...])
+    grad_power = power(grad_ref[...])
+    delta_power = power(delta)
+    delta = delta * jnp.exp2(delta_power)
     exact = [
         jnp.concatenate([lse[lo : lo + heads // 2], delta[lo : lo + heads // 2]], axis=0)
         for lo in (0, heads // 2)
@@ -56,26 +74,27 @@
         column = pl.multiple_of(core * half + lax.rem(batch, 2) * size, size)
         mine = jnp.where(core == 0, exact[0], exact[1])
         high = mine.astype(BF).astype(F32)
-        stats = jnp.concatenate([high, mine - high], axis=0).astype(BF)
+        tile[...] = jnp.zeros_like(tile)
+        tile[:heads, :rows] = high
+        tile[heads : 2 * heads, :rows] = mine - high
+        for i, exponent in enumerate((weight_power, query_power, grad_power, delta_power)):
+            tile[2 * heads : 2 * heads + 1, i * rows : (i + 1) * rows] = jnp.broadcast_to(exponent, (1, rows))
+        block_ref[depth + 4 * rows :] = tile[...].astype(BF)
 
         @pl.when(batch < 2)
         def _():
-            block_ref[:depth] = key_ref[:, pl.ds(column, size)]
+            block_ref[:depth] = scaled(key_ref[:, pl.ds(column, size)], weight_power)
 
         @pl.when(batch >= 2)
         def _():
-            block_ref[:depth] = value_ref[:, pl.ds(column, size)]
+            block_ref[:depth] = scaled(value_ref[:, pl.ds(column, size)], weight_power)
 
         first = depth
-        for ref in (query_ref, grad_ref):
+        for ref, exponent in ((query_ref, query_power), (grad_ref, grad_power)):
             for lo in range(0, half, size):
                 here = pl.ds(pl.multiple_of(core * half + lo, size), size)
-                block_ref[first : first + rows] = ref[:, here]
+                block_ref[first : first + rows] = scaled(ref[:, here], exponent)
                 first += rows
-                if first == depth + rows:
-                    block_ref[first : first + 16] = jnp.zeros((16, size), BF)
-                    block_ref[first : first + 2 * heads, :rows] = stats
-                    first += 16
 
 
 def pack(place, key_weight, value_weight, query, grad, out, lse):
@@ -89,21 +108,21 @@
         out_specs=[pl.BlockSpec(memory_space=pltpu.VMEM)] * 2,
         out_shape=[jax.ShapeDtypeStruct((depth + 16 + 4 * query.shape[0], size), BF)] * 2,
         scratch_shapes=[pltpu.VMEM(x.shape, x.dtype) for x in sources]
-        + [pltpu.SemaphoreType.DMA((len(sources),))],
+        + [pltpu.VMEM((16, size), F32), pltpu.SemaphoreType.DMA((len(sources),))],
         compiler_params=pltpu.CompilerParams(vmem_limit_bytes=60 * 2**20),
         cost_estimate=pl.CostEstimate(flops=0, bytes_accessed=2**19, transcendentals=0),
     )(place, *sources)
 
 
 def attend_kernel(
-    place_ref, own_in, other_in, slab_ref, head_ref, stat_ref, rest_ref, own_ref, other_ref, part_ref,
-    weight, kv, query, grad, qt, gt, pieces, stats, total,
+    place_ref, own_in, other_in, slab_ref, rows_ref, tile_ref, own_ref, other_ref, part_ref,
+    weight, kv, query, grad, qt, gt, pieces, exponents, stats, total,
     size, scaling, latent_factor, prefix_factor,
 ):
     step = pl.program_id(0)
     last = pl.num_programs(0) - 1
     half = pl.num_programs(0) // 2
-    ranks = head_ref.shape[0]
+    ranks = tile_ref.shape[0]
     rows = query.shape[0] // ranks
 
     @pl.when(step == 0)
@@ -117,12 +136,12 @@
                     slab, there
                 ]
             here = slice(rank * rows, (rank + 1) * rows)
-            query[here, :size] = head_ref[at]
-            query[here, size:] = rest_ref[at, :rows]
-            grad[here, :size] = rest_ref[at, rows : 2 * rows]
-            grad[here, size:] = rest_ref[at, 2 * rows :]
-            pieces[:, here] = stat_ref[at].astype(F32)[:8, :rows]
+            for i, to in enumerate((query, query, grad, grad)):
+                to[here, i % 2 * size : (i % 2 + 1) * size] = rows_ref[at, i * rows : (i + 1) * rows]
+            pieces[:, here] = tile_ref[at, :8, :rows]
+            exponents[:, here] = tile_ref[at, 8:, 3 * rows : 4 * rows]
         stats[...] = pieces[:4] + pieces[4:]
+        stats[2:] = stats[2:] * jnp.exp2(-exponents[:1])
         qt[...] = query[...].T
         gt[...] = grad[...].T
         total[...] = jnp.zeros_like(total)
@@ -162,13 +181,10 @@
         part_ref[...] = (total[...] * (scaling * prefix_factor)).astype(BF)
 
 
-def attend(place, own, other, slabs, first_rows, last_rows, latents, prefix_count):
+def attend(place, own, other, slabs, rows_all, tiles, latents, prefix_count):
     tokens, width = own.shape
     count, _, size = slabs.shape
     columns = count * size
-    ranks = first_rows.shape[0]
-    rows = latents // ranks
-    depth = first_rows.shape[1] - 16 - rows
     block = 256
     half = tokens // block
     kernel = functools.partial(
@@ -186,9 +202,8 @@
             pl.BlockSpec((block, width), lambda t: (jnp.minimum(t, half - 1), 0)),
             pl.BlockSpec((block, width), lambda t: (jnp.maximum(t - half, 0), 0)),
             pl.BlockSpec(slabs.shape, lambda t: (0, 0, 0)),
-            pl.BlockSpec((ranks, rows, size), lambda t: (0, depth // rows, 0)),
-            pl.BlockSpec((ranks, 16, size), lambda t: (0, (depth + rows) // 16, 0)),
-            pl.BlockSpec(last_rows.shape, lambda t: (0, 0, 0)),
+            pl.BlockSpec(rows_all.shape, lambda t: (0, 0, 0)),
+            pl.BlockSpec(tiles.shape, lambda t: (0, 0, 0)),
         ],
         out_specs=[
             pl.BlockSpec((block, columns), lambda t: (jnp.minimum(t, half - 1), 0)),
@@ -208,6 +223,7 @@
             pltpu.VMEM((2 * size, latents), BF),
             pltpu.VMEM((2 * size, latents), BF),
             pltpu.VMEM((8, latents), F32),
+            pltpu.VMEM((8, latents), F32),
             pltpu.VMEM((4, latents), F32),
             pltpu.VMEM((2 * size, latents), F32),
         ],
@@ -217,7 +233,7 @@
             bytes_accessed=6 * 2**20,
             transcendentals=4 * tokens * latents,
         ),
-    )(place, own, other, slabs, first_rows, first_rows, last_rows)
+    )(place, own, other, slabs, rows_all, tiles)
 
 
 def tail_kernel(place_ref, query_ref, latent_ref, every_ref, latent_out, mine_out, theirs_out):
@@ -318,16 +334,16 @@
         place, key_weight, value_weight, queries[0], out_grad[0], attn_out[0], shifted_lse[0].T
     )
     blocks = jnp.stack([mine, lax.ppermute(theirs, "core", SWAP)])
-    cut = depth + 16 + rows
-    first_rows = lax.all_gather(blocks[:, :cut], Z, axis=0, tiled=True)
-    slab = first_rows[:, :depth].reshape(-1, size)
-    slabs = jnp.broadcast_to(slab[None], (batches,) + slab.shape)
-    slabs, rest = lax.optimization_barrier((slabs, blocks[:, cut:]))
-    slabs = exchange(slabs, "dp")
-    last_rows = lax.all_gather(rest, Z, axis=0, tiled=True)
+    gathered = lax.all_gather(blocks.astype(F16), Z, axis=0, tiled=True)
+    slabs = lax.all_gather(gathered[:, :depth], "dp")
+    tiles = gathered[:, -16:].astype(F32)
+    back = jnp.exp2(-tiles[:, 8, :])
+    slabs = (slabs.astype(F32) * back[None, :, :1, None]).astype(BF).reshape(batches, -1, size)
+    rows_back = jnp.repeat(back[:, rows : 3 * rows : rows], 2 * rows, axis=1)
+    rows_all = (gathered[:, depth:-16].astype(F32) * rows_back[:, :, None]).astype(BF)
 
     own_grads, other_grads, part = attend(
-        place, tokens_in, other_tokens, slabs, first_rows, last_rows, latents, token_count * ranks
+        place, tokens_in, other_tokens, slabs, rows_all, tiles, latents, token_count * ranks
     )
     theirs = lax.ppermute(other_grads, "core", SWAP)
     half = columns // 2

time: 181 us -> 176 us (0.972)
  starting transfers between devices: 78.9 us -> 62.6 us
  waiting for transfers between devices: 7.13 us -> 20.8 us
  blocking collectives: 66.3 us -> 61.6 us
  other arithmetic: 3.45 us -> 7.08 us
    all_to_all x4 -> x3, waiting for transfers between devices: 4.65 us -> 18.3 us  [exchange(): return lax.all_to_all(x, axes, 0, 0, tiled=True)]
    all_to_all x4 -> x3, starting transfers between devices: 28.5 us -> 22.8 us  [exchange(): return lax.all_to_all(x, axes, 0, 0, tiled=True)]
    ppermute x1, starting transfers between devices: 14.7 us -> 10.3 us  [local(): theirs = lax.ppermute(other_grads, 'core', SWAP)]
    convert_element_type x0 -> x4, other arithmetic: none -> 4.35 us  [the longest x1 1.99 us: local(): (slabs.astype(F32) * back[None, :, :1, None]).astype(BF)]
    ppermute x1, starting transfers between devices: 11 us -> 6.72 us  [local(): lax.ppermute(jnp.concatenate([latent_own, query_theirs], axis=1), 'core',...]
    all_gather x2, blocking collectives: 55.6 us -> 51.9 us  [the longest x1 34.8 us: local(): gathered = lax.all_gather(blocks.astype(F16), Z, axis=0, tiled=True)]
    ppermute x1, starting transfers between devices: 13.9 us -> 12.1 us  [local(): weight_other = lax.ppermute(weight_theirs, 'core', SWAP)]
  transfers between devices with their start and end apart: 9 -> 8, of which waited for: 3 -> 4; matrix products, arithmetic and copies ran while one was open for 2% -> 4% of each run, Pallas kernels for 0% -> 0%
where the time goes in v10:
time: 176 us; the launch traced here: 173 us
  starting transfers between devices  62.6 us (36%)
  blocking collectives  61.6 us (35%)
  waiting for transfers between devices  20.8 us (12%)
  Pallas kernels  18.9 us (11%)
  other arithmetic  7.08 us (4%)
    all_gather x1, blocking collectives, local(): gathered = lax.all_gather(blocks.astype(F16), Z, axis=0, tiled=True)  34.8 us
    all_to_all x3, starting transfers between devices, exchange(): return lax.all_to_all(x, axes, 0, 0, tiled=True)  22.8 us
    all_to_all x3, waiting for transfers between devices, exchange(): return lax.all_to_all(x, axes, 0, 0, tiled=True)  18.3 us
    all_gather x1, blocking collectives, local(): slabs = lax.all_gather(gathered[:, :depth], 'dp')  17.1 us
    pallas_call x1, Pallas kernels, attend(): pl.pallas_call(kernel, grid=(2 * half,), in_specs=[pl.BlockSpec(memory_sp...  13.7 us
    ppermute x1, starting transfers between devices, local(): weight_other = lax.ppermute(weight_theirs, 'core', SWAP)  12.1 us
    ppermute x1, starting transfers between devices, local(): theirs = lax.ppermute(other_grads, 'core', SWAP)  10.3 us
    all_gather x1, blocking collectives, local(): lax.all_gather(weight_rows, 'dp')  9.67 us
  transfers between devices with their start and end apart: 8, of which 4 were waited for; matrix products, arithmetic and copies ran while one was open for 4% of the time, Pallas kernels for 0%

profile of v10, /device:TPU:1, one launch (start us, length us, event | category | flops | bytes accessed | tf_op | source)
XLA Modules:
  0.0 173.3 jit_solution(5849825531650058931)
XLA Ops:
  0.6 0.6 pad_add_fusion.place_ref
  1.2 2.5 %shard_map.120 = (bf16[208,128]{1,0:T(8,128)(2,1)}, bf16[208,128]{1,0:T(8,128)(2,1)}) custom-call(s32[2]{0:T(128)} %pad_add_fusion.place_ref, bf16[64,512]{1,0:T(8,128)(2,1)} %refs_0_.1, bf16[64,512]{1,0:T(8,128)(2,1)} %refs_1_.1, bf16[32,512]{1,0:T(8,128)(2,1)} %bitcast.56, bf16[32,512]{1,0:T(8,128)(2,1)} %bitcast.57, bf16[32,512]{1,0:T(8,128)(2,1)} %bitcast.58, ...), custom_call_target="tpu_custom_call" | custom-call | bytes 524288 | tf_op jit(solution)/shard_map/pallas_call | solution.py:104
  3.8 8.8 %collective-permute-start.1 = (bf16[208,128]{1,0:T(8,128)(2,1)}, bf16[208,128]{1,0:T(8,128)(2,1)S(1)}, u32[]{:S(2)}, u32[]{:S(2)}) collective-permute-start(bf16[208,128]{1,0:T(8,128)(2,1)} %get-tuple-element.16), channel_id=1, source_target_pairs={{0,16},{16,0},{1,17},{17,1},{2,18},{18,2},{3,19},{19,3},{4,20},{20... | collective-permute-start | bytes 159752 | tf_op jit(solution)/shard_map/ppermute | solution.py:336
  12.6 1.9 %collective-permute-start = (bf16[512,2048]{1,0:T(8,128)(2,1)}, bf16[512,2048]{1,0:T(8,128)(2,1)}, u32[]{:S(2)}, u32[]{:S(2)}) collective-permute-start(bf16[512,2048]{1,0:T(8,128)(2,1)} %bitcast.62), channel_id=1, source_target_pairs={{0,16},{16,0},{1,17},{17,1},{2,18},{18,2},{3,19},{19,3},{4,20},{20... | collective-permute-start | bytes 6291464 | tf_op jit(solution)/shard_map/ppermute | solution.py:317
  14.5 0.8 maximum_convert_fusion
  15.4 34.8 %all-gather.3 = f16[32,208,128]{2,1,0:T(8,128)(2,1)S(1)} all-gather(f16[2,208,128]{2,1,0:T(8,128)(2,1)S(1)} %maximum_convert_fusion), channel_id=1, replica_groups=mesh['zh'=4,'zl'=4,'core'=2,'tensor'=4,'dp'=4] {'zh','zl'}, dimensions={0}, use_global_device_ids=true | all-gather | bytes 1810432 | tf_op jit(solution)/shard_map/all_gather | solution.py:337
  50.2 0.1 slice.58
  50.4 0.1 slice.49
  50.5 0.1 broadcast_in_dim.12
  50.6 0.1 mul.23
  50.7 0.1 slice_reduce_fusion
  50.8 1.5 multiply_convert_fusion.rows_ref
  52.3 17.1 %all-gather.4 = f16[128,64,128]{2,1,0:T(8,128)(2,1)S(1)} all-gather(f16[32,64,128]{2,1,0:T(8,128)(2,1)S(1)} %slice.58), channel_id=2, replica_groups=mesh['zh'=4,'zl'=4,'core'=2,'tensor'=4,'dp'=4] {'dp'}, dimensions={0}, use_global_device_ids=true | all-gather | bytes 2621440 | tf_op jit(solution)/shard_map/all_gather | solution.py:338
  69.4 2.0 %fusion = bf16[4,32,64,128]{3,2,1,0:T(8,128)(2,1)} fusion(f16[4,32,64,128]{3,2,1,0:T(8,128)(2,1)S(1)} %bitcast.46, f32[32]{0:T(128)S(1)} %slice_reduce_fusion), kind=kLoop, calls=%fused_computation.1 | loop fusion | flops 3145728 | bytes 4194432 | tf_op jit(solution)/shard_map/convert_element_type | solution.py:341
  71.4 13.7 %shard_map.121 = (bf16[512,512]{1,0:T(8,128)(2,1)S(1)}, bf16[512,512]{1,0:T(8,128)(2,1)S(1)}, bf16[256,1024]{1,0:T(8,128)(2,1)}) custom-call(s32[2]{0:T(128)S(1)} %copy-done, bf16[512,2048]{1,0:T(8,128)(2,1)} %bitcast.63, bf16[512,2048]{1,0:T(8,128)(2,1)} %collective-permute-done.other_in, bf16[4,2048,128]{2,1,0:T(8,128)(2,1)} %bitcast.47, ...), custom_call_target="tpu_custom_call" | custom-call | flops 2684354560 | bytes 6291456 | tf_op jit(solution)/shard_map/pallas_call | solution.py:197
  85.1 6.5 %all-to-all-start = ((bf16[16,16,1024]{2,1,0:T(8,128)(2,1)}), bf16[16,16,1024]{2,1,0:T(8,128)(2,1)S(1)}, u32[]{:S(2)}, u32[]{:S(2)}) async-start(bf16[16,16,1024]{2,1,0:T(8,128)(2,1)} %bitcast.13), calls=%async_computation | async-start | bytes 1048576 | tf_op jit(solution)/shard_map/all_to_all | solution.py:295
  91.6 10.3 %collective-permute-start.2 = (bf16[512,512]{1,0:T(8,128)(2,1)S(1)}, bf16[512,512]{1,0:T(8,128)(2,1)S(1)}, u32[]{:S(2)}, u32[]{:S(2)}) collective-permute-start(bf16[512,512]{1,0:T(8,128)(2,1)S(1)} %get-tuple-element.19), channel_id=1, source_target_pairs={{0,16},{16,0},{1,17},{17,1},{2,18},{18,2},{3,19},{19,3},{4,20},{20... | collective-permute-start | bytes 1572872 | tf_op jit(solution)/shard_map/ppermute | solution.py:348
  102.0 1.5 collective-permute-done.2
  103.5 1.3 maximum_select_fusion
  104.8 6.5 %all-to-all-done = bf16[16,16,1024]{2,1,0:T(8,128)(2,1)S(1)} async-done(((bf16[16,16,1024]{2,1,0:T(8,128)(2,1)}), bf16[16,16,1024]{2,1,0:T(8,128)(2,1)S(1)}, u32[]{:S(2)}, u32[]{:S(2)}) %all-to-all-start) | async-done | bytes 524320 | tf_op jit(solution)/shard_map/all_to_all | solution.py:295
  111.3 0.1 reduce_sum.24
  111.4 0.9 broadcast_in_dim.13
  112.2 11.8 %all-to-all-start.1 = ((bf16[16,16,1024]{2,1,0:T(8,128)(2,1)}), bf16[16,16,1024]{2,1,0:T(8,128)(2,1)S(1)}, u32[]{:S(2)}, u32[]{:S(2)}) async-start(bf16[16,16,1024]{2,1,0:T(8,128)(2,1)} %broadcast_in_dim.13), calls=%async_computation.1 | async-start | bytes 1048576 | tf_op jit(solution)/shard_map/all_to_all | solution.py:295
  124.2 6.7 %collective-permute-start.3 = (bf16[64,1280]{1,0:T(8,128)(2,1)S(1)}, bf16[64,1280]{1,0:T(8,128)(2,1)S(1)}, u32[]{:S(2)}, u32[]{:S(2)}) collective-permute-start(bf16[64,1280]{1,0:T(8,128)(2,1)S(1)} %pad_maximum_fusion), channel_id=1, source_target_pairs={{0,16},{16,0},{1,17},{17,1},{2,18},{18,2},{3,19},{19,3},{4,20},{20... | collective-permute-start | bytes 491528 | tf_op jit(solution)/shard_map/ppermute | solution.py:322
  130.9 1.0 collective-permute-done.3
  132.0 11.8 %all-to-all-done.1 = bf16[16,16,1024]{2,1,0:T(8,128)(2,1)S(1)} async-done(((bf16[16,16,1024]{2,1,0:T(8,128)(2,1)}), bf16[16,16,1024]{2,1,0:T(8,128)(2,1)S(1)}, u32[]{:S(2)}, u32[]{:S(2)}) %all-to-all-start.1) | async-done | bytes 524320 | tf_op jit(solution)/shard_map/all_to_all | solution.py:295
  143.8 1.9 %shard_map.122 = (bf16[8,64,256]{2,1,0:T(8,128)(2,1)}, bf16[64,256]{1,0:T(8,128)(2,1)S(1)}, bf16[64,256]{1,0:T(8,128)(2,1)S(1)}) custom-call(s32[2]{0:T(128)S(1)} %copy-done, bf16[128,256]{1,0:T(8,128)(2,1)S(1)} %maximum_select_fusion.3.query_ref, bf16[128,1024]{1,0:T(8,128)(2,1)S(1)} %maximum_select_fusion.2.latent_ref, bf16[256,1024]{1,0:T(8,128)(2,1)S(1)} %bitcast.44), custom_call_target="tpu_custom_call" | custom-call | bytes 1048576 | tf_op jit(solution)/shard_map/pallas_call | solution.py:263
  145.7 12.1 %collective-permute-start.4 = (bf16[64,256]{1,0:T(8,128)(2,1)S(1)}, bf16[64,256]{1,0:T(8,128)(2,1)S(1)}, u32[]{:S(2)}, u32[]{:S(2)}) collective-permute-start(bf16[64,256]{1,0:T(8,128)(2,1)S(1)} %get-tuple-element.25), channel_id=1, source_target_pairs={{0,16},{16,0},{1,17},{17,1},{2,18},{18,2},{3,19},{19,3},{4,20},{20... | collective-permute-start | bytes 98312 | tf_op jit(solution)/shard_map/ppermute | solution.py:368
  157.8 4.4 %all-to-all-start.2 = ((bf16[8,64,256]{2,1,0:T(8,128)(2,1)}), bf16[8,64,256]{2,1,0:T(8,128)(2,1)S(1)}, u32[]{:S(2)}, u32[]{:S(2)}) async-start(bf16[8,64,256]{2,1,0:T(8,128)(2,1)} %get-tuple-element.23), calls=%async_computation.2 | async-start | bytes 524288 | tf_op jit(solution)/shard_map/all_to_all | solution.py:295
  162.3 9.7 %all_gather.16.part_ref = bf16[4,64,512]{2,1,0:T(8,128)(2,1)S(1)} all-gather(bf16[1,64,512]{2,1,0:T(8,128)(2,1)S(1)} %maximum_select_fusion.4), channel_id=1, replica_groups=mesh['zh'=4,'zl'=4,'core'=2,'tensor'=4,'dp'=4] {'dp'}, dimensions={0}, use_global_device_ids=true | all-gather | bytes 327680 | tf_op jit(solution)/shard_map/all_gather | solution.py:375
  171.9 0.7 shard_map.123
  172.6 0.7 reduce_sum.25
  (22 shorter events, 0.3 us)
Async XLA Ops:
  3.8 10.7 %collective-permute-start.1 = (bf16[208,128]{1,0:T(8,128)(2,1)}, bf16[208,128]{1,0:T(8,128)(2,1)S(1)}, u32[]{:S(2)}, u32[]{:S(2)}) collective-permute-start(bf16[208,128]{1,0:T(8,128)(2,1)} %get-tuple-element.16), channel_id=1, source_target_pairs={{0,16},{16,0},{1,17},{17,1},{2,18},{18,2},{3,19},{19,3},{4,20},{20... | collective-permute-start | bytes 159752 | tf_op jit(solution)/shard_map/ppermute | solution.py:336
  12.6 58.8 %collective-permute-start = (bf16[512,2048]{1,0:T(8,128)(2,1)}, bf16[512,2048]{1,0:T(8,128)(2,1)}, u32[]{:S(2)}, u32[]{:S(2)}) collective-permute-start(bf16[512,2048]{1,0:T(8,128)(2,1)} %bitcast.62), channel_id=1, source_target_pairs={{0,16},{16,0},{1,17},{17,1},{2,18},{18,2},{3,19},{19,3},{4,20},{20... | collective-permute-start | bytes 6291464 | tf_op jit(solution)/shard_map/ppermute | solution.py:317
  69.4 2.0 %copy-start = (s32[2]{0:T(128)S(1)}, s32[2]{0:T(128)}, u32[]{:S(2)}) copy-start(s32[2]{0:T(128)} %pad_add_fusion.place_ref) | copy-start | bytes 28
  85.1 26.2 %all-to-all-start = ((bf16[16,16,1024]{2,1,0:T(8,128)(2,1)}), bf16[16,16,1024]{2,1,0:T(8,128)(2,1)S(1)}, u32[]{:S(2)}, u32[]{:S(2)}) async-start(bf16[16,16,1024]{2,1,0:T(8,128)(2,1)} %bitcast.13), calls=%async_computation | async-start | bytes 1048576 | tf_op jit(solution)/shard_map/all_to_all | solution.py:295
  91.6 11.9 %collective-permute-start.2 = (bf16[512,512]{1,0:T(8,128)(2,1)S(1)}, bf16[512,512]{1,0:T(8,128)(2,1)S(1)}, u32[]{:S(2)}, u32[]{:S(2)}) collective-permute-start(bf16[512,512]{1,0:T(8,128)(2,1)S(1)} %get-tuple-element.19), channel_id=1, source_target_pairs={{0,16},{16,0},{1,17},{17,1},{2,18},{18,2},{3,19},{19,3},{4,20},{20... | collective-permute-start | bytes 1572872 | tf_op jit(solution)/shard_map/ppermute | solution.py:348
  103.5 20.6 %copy-start.2 = (bf16[64,512]{1,0:T(8,128)(2,1)S(1)}, bf16[64,512]{1,0:T(8,128)(2,1)}, u32[]{:S(2)}) copy-start(bf16[64,512]{1,0:T(8,128)(2,1)} %param.12) | copy-start | bytes 196612
  103.5 20.6 %copy-start.1 = (bf16[1,1024,64]{1,2,0:T(8,128)(2,1)S(1)}, bf16[1,1024,64]{1,2,0:T(8,128)(2,1)}, u32[]{:S(2)}) copy-start(bf16[1,1024,64]{1,2,0:T(8,128)(2,1)} %param.17) | copy-start | bytes 393220
  112.2 31.6 %all-to-all-start.1 = ((bf16[16,16,1024]{2,1,0:T(8,128)(2,1)}), bf16[16,16,1024]{2,1,0:T(8,128)(2,1)S(1)}, u32[]{:S(2)}, u32[]{:S(2)}) async-start(bf16[16,16,1024]{2,1,0:T(8,128)(2,1)} %broadcast_in_dim.13), calls=%async_computation.1 | async-start | bytes 1048576 | tf_op jit(solution)/shard_map/all_to_all | solution.py:295
  124.2 7.7 %collective-permute-start.3 = (bf16[64,1280]{1,0:T(8,128)(2,1)S(1)}, bf16[64,1280]{1,0:T(8,128)(2,1)S(1)}, u32[]{:S(2)}, u32[]{:S(2)}) collective-permute-start(bf16[64,1280]{1,0:T(8,128)(2,1)S(1)} %pad_maximum_fusion), channel_id=1, source_target_pairs={{0,16},{16,0},{1,17},{17,1},{2,18},{18,2},{3,19},{19,3},{4,20},{20... | collective-permute-start | bytes 491528 | tf_op jit(solution)/shard_map/ppermute | solution.py:322
  145.7 16.5 %collective-permute-start.4 = (bf16[64,256]{1,0:T(8,128)(2,1)S(1)}, bf16[64,256]{1,0:T(8,128)(2,1)S(1)}, u32[]{:S(2)}, u32[]{:S(2)}) collective-permute-start(bf16[64,256]{1,0:T(8,128)(2,1)S(1)} %get-tuple-element.25), channel_id=1, source_target_pairs={{0,16},{16,0},{1,17},{17,1},{2,18},{18,2},{3,19},{19,3},{4,20},{20... | collective-permute-start | bytes 98312 | tf_op jit(solution)/shard_map/ppermute | solution.py:368
  157.8 14.8 %all-to-all-start.2 = ((bf16[8,64,256]{2,1,0:T(8,128)(2,1)}), bf16[8,64,256]{2,1,0:T(8,128)(2,1)S(1)}, u32[]{:S(2)}, u32[]{:S(2)}) async-start(bf16[8,64,256]{2,1,0:T(8,128)(2,1)} %get-tuple-element.23), calls=%async_computation.2 | async-start | bytes 524288 | tf_op jit(solution)/shard_map/all_to_all | solution.py:295

commit v11 on v10

--- a/solution.py
+++ b/solution.py
@@ -47,7 +47,7 @@
     for copy in copies:
         copy.wait()
     key_ref, value_ref, query_ref, grad_ref, out_ref, lse_ref = landing
-    batch = place_ref[1]
+    batch = lax.div(place_ref[0], 2)
     depth, columns = key_ref.shape
     rows = query_ref.shape[0]
     size = outs[0].shape[1]
@@ -70,7 +70,7 @@
         for lo in (0, heads // 2)
     ]
     for other, block_ref in enumerate(outs):
-        core = lax.rem(place_ref[0] + other, 2)
+        core = lax.rem(lax.rem(place_ref[0], 2) + other, 2)
         column = pl.multiple_of(core * half + lax.rem(batch, 2) * size, size)
         mine = jnp.where(core == 0, exact[0], exact[1])
         high = mine.astype(BF).astype(F32)
@@ -129,7 +129,7 @@
     def _():
         depth = weight.shape[0] // ranks
         for rank in range(ranks):
-            at = rank - rank % 2 + lax.rem(rank + place_ref[0], 2)
+            at = rank - rank % 2 + lax.rem(rank + lax.rem(place_ref[0], 2), 2)
             there = pl.ds(pl.multiple_of(at * depth, depth), depth)
             for slab in range(slab_ref.shape[0]):
                 weight[rank * depth : (rank + 1) * depth, slab * size : (slab + 1) * size] = slab_ref[
@@ -227,7 +227,7 @@
             pltpu.VMEM((4, latents), F32),
             pltpu.VMEM((2 * size, latents), F32),
         ],
-        compiler_params=pltpu.CompilerParams(vmem_limit_bytes=52 * 2**20),
+        compiler_params=pltpu.CompilerParams(vmem_limit_bytes=49 * 2**20),
         cost_estimate=pl.CostEstimate(
             flops=40 * tokens * latents * size,
             bytes_accessed=6 * 2**20,
@@ -237,7 +237,7 @@
 
 
 def tail_kernel(place_ref, query_ref, latent_ref, every_ref, latent_out, mine_out, theirs_out):
-    core = place_ref[0]
+    core = lax.rem(place_ref[0], 2)
     count, rows, width = latent_out.shape
     weight = dot_nt(latent_ref[...], every_ref[...]).astype(BF)
     for one, out in enumerate((mine_out, theirs_out)):
@@ -329,7 +329,7 @@
     query_both = in_order(query_mine, query_other)
 
     depth = key_weight.shape[0]
-    place = jnp.stack([core, batch]).astype(jnp.int32)
+    place = jnp.reshape(core + 2 * batch, (1,)).astype(jnp.int32)
     mine, theirs = pack(
         place, key_weight, value_weight, queries[0], out_grad[0], attn_out[0], shifted_lse[0].T
     )
@@ -356,7 +356,9 @@
 
     share = exchange(part.reshape(lax.axis_size(Z), -1, latents), Z)
     share = jnp.sum(share.astype(F32), axis=0).astype(BF)
-    share, key_grad, value_grad = lax.optimization_barrier((share, whole(0), whole(half)))
+    share, key_grad, value_grad, latent_both, query_both = lax.optimization_barrier(
+        (share, whole(0), whole(half), latent_both, query_both)
+    )
     every = exchange(jnp.broadcast_to(share, (lax.axis_size(Z),) + share.shape), Z).reshape(part.shape)
     latent_part, weight_mine, weight_theirs = tail(
         place, query_both, latent_both, every, lax.axis_size("tensor")

time: 176 us -> 171 us (0.972)
  blocking collectives: 61.6 us -> 96.1 us
  waiting for transfers between devices: 20.8 us -> 2.83 us
  starting transfers between devices: 62.6 us -> 45.7 us
  Pallas kernels: 18.9 us -> 17 us
    all_to_all x0 -> x1, blocking collectives: none -> 34.5 us  [exchange(): return lax.all_to_all(x, axes, 0, 0, tiled=True)]
    all_to_all x3 -> x2, waiting for transfers between devices: 18.3 us -> 1.11 us  [exchange(): return lax.all_to_all(x, axes, 0, 0, tiled=True)]
    all_to_all x3 -> x2, starting transfers between devices: 22.8 us -> 10.9 us  [exchange(): return lax.all_to_all(x, axes, 0, 0, tiled=True)]
    ppermute x1, starting transfers between devices: 10.3 us -> 1.92 us  [local(): theirs = lax.ppermute(other_grads, 'core', SWAP)]
    ppermute x1, starting transfers between devices: 6.72 us -> 10.5 us  [local(): lax.ppermute(jnp.concatenate([latent_own, query_theirs], axis=1), 'core',...]
  transfers between devices with their start and end apart: 8 -> 7, of which waited for: 4 -> 2; matrix products, arithmetic and copies ran while one was open for 4% -> 3% of each run, Pallas kernels for 0% -> 0%
where the time goes in v11:
time: 171 us; the launch traced here: 169 us
  blocking collectives  96.1 us (56%)
  starting transfers between devices  45.7 us (27%)
  Pallas kernels  17 us (10%)
  other arithmetic  5.69 us (3%)
  waiting for transfers between devices  2.83 us (2%)
    all_gather x1, blocking collectives, local(): gathered = lax.all_gather(blocks.astype(F16), Z, axis=0, tiled=True)  34.8 us
    all_to_all x1, blocking collectives, exchange(): return lax.all_to_all(x, axes, 0, 0, tiled=True)  34.5 us
    all_gather x1, blocking collectives, local(): slabs = lax.all_gather(gathered[:, :depth], 'dp')  17.1 us
    pallas_call x1, Pallas kernels, attend(): pl.pallas_call(kernel, grid=(2 * half,), in_specs=[pl.BlockSpec(memory_sp...  13.1 us
    ppermute x1, starting transfers between devices, local(): weight_other = lax.ppermute(weight_theirs, 'core', SWAP)  11.7 us
    all_to_all x2, starting transfers between devices, exchange(): return lax.all_to_all(x, axes, 0, 0, tiled=True)  10.9 us
    ppermute x1, starting transfers between devices, local(): lax.ppermute(jnp.concatenate([latent_own, query_theirs], axis=1), 'core',...  10.5 us
    all_gather x1, blocking collectives, local(): lax.all_gather(weight_rows, 'dp')  9.67 us
  transfers between devices with their start and end apart: 7, of which 2 were waited for; matrix products, arithmetic and copies ran while one was open for 3% of the time, Pallas kernels for 0%

profile of v11, /device:TPU:1, one launch (start us, length us, event | category | flops | bytes accessed | tf_op | source)
XLA Modules:
  0.0 168.8 jit_solution(13416622378758369635)
XLA Ops:
  0.6 1.9 %shard_map.120 = (bf16[208,128]{1,0:T(8,128)(2,1)}, bf16[208,128]{1,0:T(8,128)(2,1)}) custom-call(s32[1]{0:T(128)} %bitcast.place_ref, bf16[64,512]{1,0:T(8,128)(2,1)} %refs_0_.1, bf16[64,512]{1,0:T(8,128)(2,1)} %refs_1_.1, bf16[32,512]{1,0:T(8,128)(2,1)} %bitcast.57, bf16[32,512]{1,0:T(8,128)(2,1)} %bitcast.58, bf16[32,512]{1,0:T(8,128)(2,1)} %bitcast.59, ...), custom_call_target="tpu_custom_call" | custom-call | bytes 524288 | tf_op jit(solution)/shard_map/pallas_call | solution.py:104
  2.5 8.8 %collective-permute-start.1 = (bf16[208,128]{1,0:T(8,128)(2,1)}, bf16[208,128]{1,0:T(8,128)(2,1)S(1)}, u32[]{:S(2)}, u32[]{:S(2)}) collective-permute-start(bf16[208,128]{1,0:T(8,128)(2,1)} %get-tuple-element.18), channel_id=1, source_target_pairs={{0,16},{16,0},{1,17},{17,1},{2,18},{18,2},{3,19},{19,3},{4,20},{20... | collective-permute-start | bytes 159752 | tf_op jit(solution)/shard_map/ppermute | solution.py:336
  11.3 1.9 %collective-permute-start = (bf16[512,2048]{1,0:T(8,128)(2,1)}, bf16[512,2048]{1,0:T(8,128)(2,1)}, u32[]{:S(2)}, u32[]{:S(2)}) collective-permute-start(bf16[512,2048]{1,0:T(8,128)(2,1)} %bitcast.45), channel_id=1, source_target_pairs={{0,16},{16,0},{1,17},{17,1},{2,18},{18,2},{3,19},{19,3},{4,20},{20... | collective-permute-start | bytes 6291464 | tf_op jit(solution)/shard_map/ppermute | solution.py:317
  13.2 0.0 collective-permute-done.1
  13.3 0.8 maximum_convert_fusion
  14.1 34.8 %all-gather.3 = f16[32,208,128]{2,1,0:T(8,128)(2,1)S(1)} all-gather(f16[2,208,128]{2,1,0:T(8,128)(2,1)S(1)} %maximum_convert_fusion), channel_id=1, replica_groups=mesh['zh'=4,'zl'=4,'core'=2,'tensor'=4,'dp'=4] {'zh','zl'}, dimensions={0}, use_global_device_ids=true | all-gather | bytes 1810432 | tf_op jit(solution)/shard_map/all_gather | solution.py:337
  48.9 0.1 slice.58
  49.1 0.1 slice.49
  49.2 0.1 broadcast_in_dim.12
  49.3 0.1 mul.23
  49.4 0.1 slice_reduce_fusion
  49.5 0.7 multiply_convert_fusion.rows_ref
  50.2 17.1 %all-gather.4 = f16[128,64,128]{2,1,0:T(8,128)(2,1)S(1)} all-gather(f16[32,64,128]{2,1,0:T(8,128)(2,1)S(1)} %slice.58), channel_id=2, replica_groups=mesh['zh'=4,'zl'=4,'core'=2,'tensor'=4,'dp'=4] {'dp'}, dimensions={0}, use_global_device_ids=true | all-gather | bytes 2621440 | tf_op jit(solution)/shard_map/all_gather | solution.py:338
  67.3 2.0 %fusion = bf16[4,32,64,128]{3,2,1,0:T(8,128)(2,1)} fusion(f16[4,32,64,128]{3,2,1,0:T(8,128)(2,1)S(1)} %bitcast.47, f32[32]{0:T(128)S(1)} %slice_reduce_fusion), kind=kLoop, calls=%fused_computation.1 | loop fusion | flops 3145728 | bytes 4194432 | tf_op jit(solution)/shard_map/convert_element_type | solution.py:341
  69.4 13.1 %shard_map.121 = (bf16[512,512]{1,0:T(8,128)(2,1)S(1)}, bf16[512,512]{1,0:T(8,128)(2,1)S(1)}, bf16[256,1024]{1,0:T(8,128)(2,1)}) custom-call(s32[1]{0:T(128)} %bitcast.place_ref, bf16[512,2048]{1,0:T(8,128)(2,1)S(1)} %bitcast.46, bf16[512,2048]{1,0:T(8,128)(2,1)} %collective-permute-done.other_in, bf16[4,2048,128]{2,1,0:T(8,128)(2,1)} %bitcast.48, ...), custom_call_target="tpu_custom_call" | custom-call | flops 2684354560 | bytes 6291456 | tf_op jit(solution)/shard_map/pallas_call | solution.py:197
  82.5 6.5 %all-to-all-start = ((bf16[16,16,1024]{2,1,0:T(8,128)(2,1)}), bf16[16,16,1024]{2,1,0:T(8,128)(2,1)S(1)}, u32[]{:S(2)}, u32[]{:S(2)}) async-start(bf16[16,16,1024]{2,1,0:T(8,128)(2,1)} %bitcast.12), calls=%async_computation | async-start | bytes 1048576 | tf_op jit(solution)/shard_map/all_to_all | solution.py:295
  89.1 10.5 %collective-permute-start.3 = (bf16[64,1280]{1,0:T(8,128)(2,1)S(1)}, bf16[64,1280]{1,0:T(8,128)(2,1)S(1)}, u32[]{:S(2)}, u32[]{:S(2)}) collective-permute-start(bf16[64,1280]{1,0:T(8,128)(2,1)S(1)} %pad_maximum_fusion), channel_id=1, source_target_pairs={{0,16},{16,0},{1,17},{17,1},{2,18},{18,2},{3,19},{19,3},{4,20},{20... | collective-permute-start | bytes 491528 | tf_op jit(solution)/shard_map/ppermute | solution.py:322
  99.5 1.9 %collective-permute-start.2 = (bf16[512,512]{1,0:T(8,128)(2,1)S(1)}, bf16[512,512]{1,0:T(8,128)(2,1)S(1)}, u32[]{:S(2)}, u32[]{:S(2)}) collective-permute-start(bf16[512,512]{1,0:T(8,128)(2,1)S(1)} %get-tuple-element.21), channel_id=1, source_target_pairs={{0,16},{16,0},{1,17},{17,1},{2,18},{18,2},{3,19},{19,3},{4,20},{20... | collective-permute-start | bytes 1572872 | tf_op jit(solution)/shard_map/ppermute | solution.py:348
  101.5 0.1 maximum_select_fusion.2.latent_ref
  101.6 1.7 %collective-permute-done.2 = bf16[512,512]{1,0:T(8,128)(2,1)S(1)} collective-permute-done((bf16[512,512]{1,0:T(8,128)(2,1)S(1)}, bf16[512,512]{1,0:T(8,128)(2,1)S(1)}, u32[]{:S(2)}, u32[]{:S(2)}) %collective-permute-start.2) | collective-permute-done | bytes 524320 | tf_op jit(solution)/shard_map/ppermute | solution.py:348
  103.4 1.2 maximum_select_fusion
  104.6 1.1 all-to-all-done
  105.7 0.1 reduce_sum.24
  105.8 0.1 broadcast_in_dim.13
  105.9 34.5 %all_to_all.15 = bf16[16,16,1024]{2,1,0:T(8,128)(2,1)S(1)} all-to-all(bf16[16,16,1024]{2,1,0:T(8,128)(2,1)S(1)} %broadcast_in_dim.13), channel_id=1, replica_groups=mesh['zh'=4,'zl'=4,'core'=2,'tensor'=4,'dp'=4] {'zh','zl'}, dimensions={0} | all-to-all | bytes 1048576 | tf_op jit(solution)/shard_map/all_to_all | solution.py:295
  140.3 1.4 shard_map.122
  141.7 11.7 %collective-permute-start.4 = (bf16[64,256]{1,0:T(8,128)(2,1)S(1)}, bf16[64,256]{1,0:T(8,128)(2,1)S(1)}, u32[]{:S(2)}, u32[]{:S(2)}) collective-permute-start(bf16[64,256]{1,0:T(8,128)(2,1)S(1)} %get-tuple-element.29), channel_id=1, source_target_pairs={{0,16},{16,0},{1,17},{17,1},{2,18},{18,2},{3,19},{19,3},{4,20},{20... | collective-permute-start | bytes 98312 | tf_op jit(solution)/shard_map/ppermute | solution.py:370
  153.4 4.4 %all-to-all-start.2 = ((bf16[8,64,256]{2,1,0:T(8,128)(2,1)}), bf16[8,64,256]{2,1,0:T(8,128)(2,1)S(1)}, u32[]{:S(2)}, u32[]{:S(2)}) async-start(bf16[8,64,256]{2,1,0:T(8,128)(2,1)} %get-tuple-element.27), calls=%async_computation.2 | async-start | bytes 524288 | tf_op jit(solution)/shard_map/all_to_all | solution.py:295
  157.8 9.7 %all_gather.16.part_ref = bf16[4,64,512]{2,1,0:T(8,128)(2,1)S(1)} all-gather(bf16[1,64,512]{2,1,0:T(8,128)(2,1)S(1)} %maximum_select_fusion.4), channel_id=1, replica_groups=mesh['zh'=4,'zl'=4,'core'=2,'tensor'=4,'dp'=4] {'dp'}, dimensions={0}, use_global_device_ids=true | all-gather | bytes 327680 | tf_op jit(solution)/shard_map/all_gather | solution.py:377
  167.4 0.7 shard_map.123
  168.1 0.0 all-to-all-done.2
  168.1 0.7 reduce_sum.25
  (20 shorter events, 0.2 us)
Async XLA Ops:
  2.5 10.7 %collective-permute-start.1 = (bf16[208,128]{1,0:T(8,128)(2,1)}, bf16[208,128]{1,0:T(8,128)(2,1)S(1)}, u32[]{:S(2)}, u32[]{:S(2)}) collective-permute-start(bf16[208,128]{1,0:T(8,128)(2,1)} %get-tuple-element.18), channel_id=1, source_target_pairs={{0,16},{16,0},{1,17},{17,1},{2,18},{18,2},{3,19},{19,3},{4,20},{20... | collective-permute-start | bytes 159752 | tf_op jit(solution)/shard_map/ppermute | solution.py:336
  11.3 58.0 %collective-permute-start = (bf16[512,2048]{1,0:T(8,128)(2,1)}, bf16[512,2048]{1,0:T(8,128)(2,1)}, u32[]{:S(2)}, u32[]{:S(2)}) collective-permute-start(bf16[512,2048]{1,0:T(8,128)(2,1)} %bitcast.45), channel_id=1, source_target_pairs={{0,16},{16,0},{1,17},{17,1},{2,18},{18,2},{3,19},{19,3},{4,20},{20... | collective-permute-start | bytes 6291464 | tf_op jit(solution)/shard_map/ppermute | solution.py:317
  67.3 2.0 %copy-start = (bf16[1,512,2048]{2,1,0:T(8,128)(2,1)S(1)}, bf16[1,512,2048]{2,1,0:T(8,128)(2,1)}, u32[]{:S(2)}) copy-start(bf16[1,512,2048]{2,1,0:T(8,128)(2,1)} %param.9) | copy-start | bytes 6291460
  69.4 19.6 %copy-start.2 = (bf16[64,512]{1,0:T(8,128)(2,1)S(1)}, bf16[64,512]{1,0:T(8,128)(2,1)}, u32[]{:S(2)}) copy-start(bf16[64,512]{1,0:T(8,128)(2,1)} %param.12) | copy-start | bytes 196612
  69.4 19.7 %copy-start.1 = (bf16[1,1024,64]{1,2,0:T(8,128)(2,1)S(1)}, bf16[1,1024,64]{1,2,0:T(8,128)(2,1)}, u32[]{:S(2)}) copy-start(bf16[1,1024,64]{1,2,0:T(8,128)(2,1)} %param.17) | copy-start | bytes 393220
  82.5 23.3 %all-to-all-start = ((bf16[16,16,1024]{2,1,0:T(8,128)(2,1)}), bf16[16,16,1024]{2,1,0:T(8,128)(2,1)S(1)}, u32[]{:S(2)}, u32[]{:S(2)}) async-start(bf16[16,16,1024]{2,1,0:T(8,128)(2,1)} %bitcast.12), calls=%async_computation | async-start | bytes 1048576 | tf_op jit(solution)/shard_map/all_to_all | solution.py:295
  89.1 12.4 %collective-permute-start.3 = (bf16[64,1280]{1,0:T(8,128)(2,1)S(1)}, bf16[64,1280]{1,0:T(8,128)(2,1)S(1)}, u32[]{:S(2)}, u32[]{:S(2)}) collective-permute-start(bf16[64,1280]{1,0:T(8,128)(2,1)S(1)} %pad_maximum_fusion), channel_id=1, source_target_pairs={{0,16},{16,0},{1,17},{17,1},{2,18},{18,2},{3,19},{19,3},{4,20},{20... | collective-permute-start | bytes 491528 | tf_op jit(solution)/shard_map/ppermute | solution.py:322
  99.5 3.8 %collective-permute-start.2 = (bf16[512,512]{1,0:T(8,128)(2,1)S(1)}, bf16[512,512]{1,0:T(8,128)(2,1)S(1)}, u32[]{:S(2)}, u32[]{:S(2)}) collective-permute-start(bf16[512,512]{1,0:T(8,128)(2,1)S(1)} %get-tuple-element.21), channel_id=1, source_target_pairs={{0,16},{16,0},{1,17},{17,1},{2,18},{18,2},{3,19},{19,3},{4,20},{20... | collective-permute-start | bytes 1572872 | tf_op jit(solution)/shard_map/ppermute | solution.py:348
  141.7 16.1 %collective-permute-start.4 = (bf16[64,256]{1,0:T(8,128)(2,1)S(1)}, bf16[64,256]{1,0:T(8,128)(2,1)S(1)}, u32[]{:S(2)}, u32[]{:S(2)}) collective-permute-start(bf16[64,256]{1,0:T(8,128)(2,1)S(1)} %get-tuple-element.29), channel_id=1, source_target_pairs={{0,16},{16,0},{1,17},{17,1},{2,18},{18,2},{3,19},{19,3},{4,20},{20... | collective-permute-start | bytes 98312 | tf_op jit(solution)/shard_map/ppermute | solution.py:370
  153.4 14.7 %all-to-all-start.2 = ((bf16[8,64,256]{2,1,0:T(8,128)(2,1)}), bf16[8,64,256]{2,1,0:T(8,128)(2,1)S(1)}, u32[]{:S(2)}, u32[]{:S(2)}) async-start(bf16[8,64,256]{2,1,0:T(8,128)(2,1)} %get-tuple-element.27), calls=%async_computation.2 | async-start | bytes 524288 | tf_op jit(solution)/shard_map/all_to_all | solution.py:295

commit v12 on v11

--- a/solution.py
+++ b/solution.py
@@ -185,7 +185,7 @@
     tokens, width = own.shape
     count, _, size = slabs.shape
     columns = count * size
-    block = 256
+    block = 512
     half = tokens // block
     kernel = functools.partial(
         attend_kernel,

time: 171 us -> 170 us (level)
  no operation moved by 1% of the time
where the time goes in v12:
time: 170 us; the launch traced here: 168 us
  blocking collectives  96.1 us (57%)
  starting transfers between devices  45.7 us (27%)
  Pallas kernels  16.3 us (10%)
  other arithmetic  5.69 us (3%)
  waiting for transfers between devices  2.82 us (2%)
    all_gather x1, blocking collectives, local(): gathered = lax.all_gather(blocks.astype(F16), Z, axis=0, tiled=True)  34.8 us
    all_to_all x1, blocking collectives, exchange(): return lax.all_to_all(x, axes, 0, 0, tiled=True)  34.5 us
    all_gather x1, blocking collectives, local(): slabs = lax.all_gather(gathered[:, :depth], 'dp')  17.1 us
    pallas_call x1, Pallas kernels, attend(): pl.pallas_call(kernel, grid=(2 * half,), in_specs=[pl.BlockSpec(memory_sp...  12.4 us
    ppermute x1, starting transfers between devices, local(): weight_other = lax.ppermute(weight_theirs, 'core', SWAP)  11.6 us
    all_to_all x2, starting transfers between devices, exchange(): return lax.all_to_all(x, axes, 0, 0, tiled=True)  10.9 us
    ppermute x1, starting transfers between devices, local(): lax.ppermute(jnp.concatenate([latent_own, query_theirs], axis=1), 'core',...  10.5 us
    all_gather x1, blocking collectives, local(): lax.all_gather(weight_rows, 'dp')  9.67 us
  transfers between devices with their start and end apart: 7, of which 2 were waited for; matrix products, arithmetic and copies ran while one was open for 3% of the time, Pallas kernels for 0%

profile of v12, /device:TPU:1, one launch (start us, length us, event | category | flops | bytes accessed | tf_op | source)
XLA Modules:
  0.0 168.1 jit_solution(10515931276001217954)
XLA Ops:
  0.6 1.9 %shard_map.120 = (bf16[208,128]{1,0:T(8,128)(2,1)}, bf16[208,128]{1,0:T(8,128)(2,1)}) custom-call(s32[1]{0:T(128)} %bitcast.place_ref, bf16[64,512]{1,0:T(8,128)(2,1)} %refs_0_.1, bf16[64,512]{1,0:T(8,128)(2,1)} %refs_1_.1, bf16[32,512]{1,0:T(8,128)(2,1)} %bitcast.57, bf16[32,512]{1,0:T(8,128)(2,1)} %bitcast.58, bf16[32,512]{1,0:T(8,128)(2,1)} %bitcast.59, ...), custom_call_target="tpu_custom_call" | custom-call | bytes 524288 | tf_op jit(solution)/shard_map/pallas_call | solution.py:104
  2.5 8.8 %collective-permute-start.1 = (bf16[208,128]{1,0:T(8,128)(2,1)}, bf16[208,128]{1,0:T(8,128)(2,1)S(1)}, u32[]{:S(2)}, u32[]{:S(2)}) collective-permute-start(bf16[208,128]{1,0:T(8,128)(2,1)} %get-tuple-element.18), channel_id=1, source_target_pairs={{0,16},{16,0},{1,17},{17,1},{2,18},{18,2},{3,19},{19,3},{4,20},{20... | collective-permute-start | bytes 159752 | tf_op jit(solution)/shard_map/ppermute | solution.py:336
  11.3 1.9 %collective-permute-start = (bf16[512,2048]{1,0:T(8,128)(2,1)}, bf16[512,2048]{1,0:T(8,128)(2,1)}, u32[]{:S(2)}, u32[]{:S(2)}) collective-permute-start(bf16[512,2048]{1,0:T(8,128)(2,1)} %bitcast.45), channel_id=1, source_target_pairs={{0,16},{16,0},{1,17},{17,1},{2,18},{18,2},{3,19},{19,3},{4,20},{20... | collective-permute-start | bytes 6291464 | tf_op jit(solution)/shard_map/ppermute | solution.py:317
  13.3 0.8 maximum_convert_fusion
  14.1 34.8 %all-gather.3 = f16[32,208,128]{2,1,0:T(8,128)(2,1)S(1)} all-gather(f16[2,208,128]{2,1,0:T(8,128)(2,1)S(1)} %maximum_convert_fusion), channel_id=1, replica_groups=mesh['zh'=4,'zl'=4,'core'=2,'tensor'=4,'dp'=4] {'zh','zl'}, dimensions={0}, use_global_device_ids=true | all-gather | bytes 1810432 | tf_op jit(solution)/shard_map/all_gather | solution.py:337
  48.9 0.1 slice.58
  49.1 0.1 slice.49
  49.2 0.1 broadcast_in_dim.12
  49.3 0.1 mul.23
  49.4 0.1 slice_reduce_fusion
  49.5 0.7 multiply_convert_fusion.rows_ref
  50.2 17.1 %all-gather.4 = f16[128,64,128]{2,1,0:T(8,128)(2,1)S(1)} all-gather(f16[32,64,128]{2,1,0:T(8,128)(2,1)S(1)} %slice.58), channel_id=2, replica_groups=mesh['zh'=4,'zl'=4,'core'=2,'tensor'=4,'dp'=4] {'dp'}, dimensions={0}, use_global_device_ids=true | all-gather | bytes 2621440 | tf_op jit(solution)/shard_map/all_gather | solution.py:338
  67.3 2.0 %fusion = bf16[4,32,64,128]{3,2,1,0:T(8,128)(2,1)} fusion(f16[4,32,64,128]{3,2,1,0:T(8,128)(2,1)S(1)} %bitcast.47, f32[32]{0:T(128)S(1)} %slice_reduce_fusion), kind=kLoop, calls=%fused_computation.1 | loop fusion | flops 3145728 | bytes 4194432 | tf_op jit(solution)/shard_map/convert_element_type | solution.py:341
  69.4 12.4 %shard_map.121 = (bf16[512,512]{1,0:T(8,128)(2,1)S(1)}, bf16[512,512]{1,0:T(8,128)(2,1)S(1)}, bf16[256,1024]{1,0:T(8,128)(2,1)}) custom-call(s32[1]{0:T(128)} %bitcast.place_ref, bf16[512,2048]{1,0:T(8,128)(2,1)S(1)} %bitcast.46, bf16[512,2048]{1,0:T(8,128)(2,1)} %collective-permute-done.other_in, bf16[4,2048,128]{2,1,0:T(8,128)(2,1)} %bitcast.48, ...), custom_call_target="tpu_custom_call" | custom-call | flops 2684354560 | bytes 6291456 | tf_op jit(solution)/shard_map/pallas_call | solution.py:197
  81.7 6.5 %all-to-all-start = ((bf16[16,16,1024]{2,1,0:T(8,128)(2,1)}), bf16[16,16,1024]{2,1,0:T(8,128)(2,1)S(1)}, u32[]{:S(2)}, u32[]{:S(2)}) async-start(bf16[16,16,1024]{2,1,0:T(8,128)(2,1)} %bitcast.12), calls=%async_computation | async-start | bytes 1048576 | tf_op jit(solution)/shard_map/all_to_all | solution.py:295
  88.3 10.5 %collective-permute-start.3 = (bf16[64,1280]{1,0:T(8,128)(2,1)S(1)}, bf16[64,1280]{1,0:T(8,128)(2,1)S(1)}, u32[]{:S(2)}, u32[]{:S(2)}) collective-permute-start(bf16[64,1280]{1,0:T(8,128)(2,1)S(1)} %pad_maximum_fusion), channel_id=1, source_target_pairs={{0,16},{16,0},{1,17},{17,1},{2,18},{18,2},{3,19},{19,3},{4,20},{20... | collective-permute-start | bytes 491528 | tf_op jit(solution)/shard_map/ppermute | solution.py:322
  98.8 1.9 %collective-permute-start.2 = (bf16[512,512]{1,0:T(8,128)(2,1)S(1)}, bf16[512,512]{1,0:T(8,128)(2,1)S(1)}, u32[]{:S(2)}, u32[]{:S(2)}) collective-permute-start(bf16[512,512]{1,0:T(8,128)(2,1)S(1)} %get-tuple-element.21), channel_id=1, source_target_pairs={{0,16},{16,0},{1,17},{17,1},{2,18},{18,2},{3,19},{19,3},{4,20},{20... | collective-permute-start | bytes 1572872 | tf_op jit(solution)/shard_map/ppermute | solution.py:348
  100.7 0.0 collective-permute-done.3
  100.8 0.1 maximum_select_fusion.2.latent_ref
  100.9 1.7 %collective-permute-done.2 = bf16[512,512]{1,0:T(8,128)(2,1)S(1)} collective-permute-done((bf16[512,512]{1,0:T(8,128)(2,1)S(1)}, bf16[512,512]{1,0:T(8,128)(2,1)S(1)}, u32[]{:S(2)}, u32[]{:S(2)}) %collective-permute-start.2) | collective-permute-done | bytes 524320 | tf_op jit(solution)/shard_map/ppermute | solution.py:348
  102.6 1.2 maximum_select_fusion
  103.9 1.1 all-to-all-done
  105.0 0.1 reduce_sum.24
  105.1 0.1 broadcast_in_dim.13
  105.1 34.5 %all_to_all.15 = bf16[16,16,1024]{2,1,0:T(8,128)(2,1)S(1)} all-to-all(bf16[16,16,1024]{2,1,0:T(8,128)(2,1)S(1)} %broadcast_in_dim.13), channel_id=1, replica_groups=mesh['zh'=4,'zl'=4,'core'=2,'tensor'=4,'dp'=4] {'zh','zl'}, dimensions={0} | all-to-all | bytes 1048576 | tf_op jit(solution)/shard_map/all_to_all | solution.py:295
  139.6 1.4 shard_map.122
  141.0 11.6 %collective-permute-start.4 = (bf16[64,256]{1,0:T(8,128)(2,1)S(1)}, bf16[64,256]{1,0:T(8,128)(2,1)S(1)}, u32[]{:S(2)}, u32[]{:S(2)}) collective-permute-start(bf16[64,256]{1,0:T(8,128)(2,1)S(1)} %get-tuple-element.29), channel_id=1, source_target_pairs={{0,16},{16,0},{1,17},{17,1},{2,18},{18,2},{3,19},{19,3},{4,20},{20... | collective-permute-start | bytes 98312 | tf_op jit(solution)/shard_map/ppermute | solution.py:370
  152.6 4.4 %all-to-all-start.2 = ((bf16[8,64,256]{2,1,0:T(8,128)(2,1)}), bf16[8,64,256]{2,1,0:T(8,128)(2,1)S(1)}, u32[]{:S(2)}, u32[]{:S(2)}) async-start(bf16[8,64,256]{2,1,0:T(8,128)(2,1)} %get-tuple-element.27), calls=%async_computation.2 | async-start | bytes 524288 | tf_op jit(solution)/shard_map/all_to_all | solution.py:295
  157.1 9.7 %all_gather.16.part_ref = bf16[4,64,512]{2,1,0:T(8,128)(2,1)S(1)} all-gather(bf16[1,64,512]{2,1,0:T(8,128)(2,1)S(1)} %maximum_select_fusion.4), channel_id=1, replica_groups=mesh['zh'=4,'zl'=4,'core'=2,'tensor'=4,'dp'=4] {'dp'}, dimensions={0}, use_global_device_ids=true | all-gather | bytes 327680 | tf_op jit(solution)/shard_map/all_gather | solution.py:377
  166.7 0.7 shard_map.123
  167.4 0.0 all-to-all-done.2
  167.4 0.7 reduce_sum.25
  (20 shorter events, 0.2 us)
Async XLA Ops:
  2.5 10.7 %collective-permute-start.1 = (bf16[208,128]{1,0:T(8,128)(2,1)}, bf16[208,128]{1,0:T(8,128)(2,1)S(1)}, u32[]{:S(2)}, u32[]{:S(2)}) collective-permute-start(bf16[208,128]{1,0:T(8,128)(2,1)} %get-tuple-element.18), channel_id=1, source_target_pairs={{0,16},{16,0},{1,17},{17,1},{2,18},{18,2},{3,19},{19,3},{4,20},{20... | collective-permute-start | bytes 159752 | tf_op jit(solution)/shard_map/ppermute | solution.py:336
  11.3 58.0 %collective-permute-start = (bf16[512,2048]{1,0:T(8,128)(2,1)}, bf16[512,2048]{1,0:T(8,128)(2,1)}, u32[]{:S(2)}, u32[]{:S(2)}) collective-permute-start(bf16[512,2048]{1,0:T(8,128)(2,1)} %bitcast.45), channel_id=1, source_target_pairs={{0,16},{16,0},{1,17},{17,1},{2,18},{18,2},{3,19},{19,3},{4,20},{20... | collective-permute-start | bytes 6291464 | tf_op jit(solution)/shard_map/ppermute | solution.py:317
  67.3 2.0 %copy-start = (bf16[1,512,2048]{2,1,0:T(8,128)(2,1)S(1)}, bf16[1,512,2048]{2,1,0:T(8,128)(2,1)}, u32[]{:S(2)}) copy-start(bf16[1,512,2048]{2,1,0:T(8,128)(2,1)} %param.9) | copy-start | bytes 6291460
  69.4 18.9 %copy-start.2 = (bf16[64,512]{1,0:T(8,128)(2,1)S(1)}, bf16[64,512]{1,0:T(8,128)(2,1)}, u32[]{:S(2)}) copy-start(bf16[64,512]{1,0:T(8,128)(2,1)} %param.12) | copy-start | bytes 196612
  69.4 18.9 %copy-start.1 = (bf16[1,1024,64]{1,2,0:T(8,128)(2,1)S(1)}, bf16[1,1024,64]{1,2,0:T(8,128)(2,1)}, u32[]{:S(2)}) copy-start(bf16[1,1024,64]{1,2,0:T(8,128)(2,1)} %param.17) | copy-start | bytes 393220
  81.7 23.3 %all-to-all-start = ((bf16[16,16,1024]{2,1,0:T(8,128)(2,1)}), bf16[16,16,1024]{2,1,0:T(8,128)(2,1)S(1)}, u32[]{:S(2)}, u32[]{:S(2)}) async-start(bf16[16,16,1024]{2,1,0:T(8,128)(2,1)} %bitcast.12), calls=%async_computation | async-start | bytes 1048576 | tf_op jit(solution)/shard_map/all_to_all | solution.py:295
  88.3 12.4 %collective-permute-start.3 = (bf16[64,1280]{1,0:T(8,128)(2,1)S(1)}, bf16[64,1280]{1,0:T(8,128)(2,1)S(1)}, u32[]{:S(2)}, u32[]{:S(2)}) collective-permute-start(bf16[64,1280]{1,0:T(8,128)(2,1)S(1)} %pad_maximum_fusion), channel_id=1, source_target_pairs={{0,16},{16,0},{1,17},{17,1},{2,18},{18,2},{3,19},{19,3},{4,20},{20... | collective-permute-start | bytes 491528 | tf_op jit(solution)/shard_map/ppermute | solution.py:322
  98.8 3.8 %collective-permute-start.2 = (bf16[512,512]{1,0:T(8,128)(2,1)S(1)}, bf16[512,512]{1,0:T(8,128)(2,1)S(1)}, u32[]{:S(2)}, u32[]{:S(2)}) collective-permute-start(bf16[512,512]{1,0:T(8,128)(2,1)S(1)} %get-tuple-element.21), channel_id=1, source_target_pairs={{0,16},{16,0},{1,17},{17,1},{2,18},{18,2},{3,19},{19,3},{4,20},{20... | collective-permute-start | bytes 1572872 | tf_op jit(solution)/shard_map/ppermute | solution.py:348
  141.0 16.1 %collective-permute-start.4 = (bf16[64,256]{1,0:T(8,128)(2,1)S(1)}, bf16[64,256]{1,0:T(8,128)(2,1)S(1)}, u32[]{:S(2)}, u32[]{:S(2)}) collective-permute-start(bf16[64,256]{1,0:T(8,128)(2,1)S(1)} %get-tuple-element.29), channel_id=1, source_target_pairs={{0,16},{16,0},{1,17},{17,1},{2,18},{18,2},{3,19},{19,3},{4,20},{20... | collective-permute-start | bytes 98312 | tf_op jit(solution)/shard_map/ppermute | solution.py:370
  152.6 14.8 %all-to-all-start.2 = ((bf16[8,64,256]{2,1,0:T(8,128)(2,1)}), bf16[8,64,256]{2,1,0:T(8,128)(2,1)S(1)}, u32[]{:S(2)}, u32[]{:S(2)}) async-start(bf16[8,64,256]{2,1,0:T(8,128)(2,1)} %get-tuple-element.27), calls=%async_computation.2 | async-start | bytes 524288 | tf_op jit(solution)/shard_map/all_to_all | solution.py:295

commit v13 on v12

--- a/solution.py
+++ b/solution.py
@@ -14,6 +14,7 @@
 SEQ = ("zh", "zl", "core")
 Z = ("zh", "zl")
 SWAP = [(0, 1), (1, 0)]
+LOG2E = 1.0 / math.log(2.0)
 
 
 def dot(a, b):
@@ -142,6 +143,7 @@
             exponents[:, here] = tile_ref[at, 8:, 3 * rows : 4 * rows]
         stats[...] = pieces[:4] + pieces[4:]
         stats[2:] = stats[2:] * jnp.exp2(-exponents[:1])
+        stats[:2] = stats[:2] * LOG2E
         qt[...] = query[...].T
         gt[...] = grad[...].T
         total[...] = jnp.zeros_like(total)
@@ -159,8 +161,8 @@
         cols = slice(head * size, (head + 1) * size)
         keys = kv[:, cols]
         values = kv[:, (2 + head) * size : (3 + head) * size]
-        scores = dot(keys, qt[cols, :]) * scaling
-        weights = jnp.exp(scores - stats[head : head + 1, :])
+        scores = dot(keys, qt[cols, :]) * (scaling * LOG2E)
+        weights = jnp.exp2(scores - stats[head : head + 1, :])
         probs = dot(values, gt[cols, :])
         score_grad = (weights * (probs - stats[2 + head : 3 + head, :])).astype(BF)
         value_out.append(dot(weights.astype(BF), grad[:, cols]) * latent_factor)

time: 170 us -> 170 us (level)
  no operation moved by 1% of the time
where the time goes in v13:
time: 170 us; the launch traced here: 168 us
  blocking collectives  96.1 us (57%)
  starting transfers between devices  45.7 us (27%)
  Pallas kernels  15.9 us (9%)
  other arithmetic  5.69 us (3%)
  waiting for transfers between devices  2.82 us (2%)
    all_gather x1, blocking collectives, local(): gathered = lax.all_gather(blocks.astype(F16), Z, axis=0, tiled=True)  34.8 us
    all_to_all x1, blocking collectives, exchange(): return lax.all_to_all(x, axes, 0, 0, tiled=True)  34.5 us
    all_gather x1, blocking collectives, local(): slabs = lax.all_gather(gathered[:, :depth], 'dp')  17.1 us
    pallas_call x1, Pallas kernels, attend(): pl.pallas_call(kernel, grid=(2 * half,), in_specs=[pl.BlockSpec(memory_sp...  11.9 us
    ppermute x1, starting transfers between devices, local(): weight_other = lax.ppermute(weight_theirs, 'core', SWAP)  11.6 us
    all_to_all x2, starting transfers between devices, exchange(): return lax.all_to_all(x, axes, 0, 0, tiled=True)  10.9 us
    ppermute x1, starting transfers between devices, local(): lax.ppermute(jnp.concatenate([latent_own, query_theirs], axis=1), 'core',...  10.5 us
    all_gather x1, blocking collectives, local(): lax.all_gather(weight_rows, 'dp')  9.67 us
  transfers between devices with their start and end apart: 7, of which 2 were waited for; matrix products, arithmetic and copies ran while one was open for 3% of the time, Pallas kernels for 0%

profile of v13, /device:TPU:1, one launch (start us, length us, event | category | flops | bytes accessed | tf_op | source)
XLA Modules:
  0.0 167.7 jit_solution(5554742468819314942)
XLA Ops:
  0.6 1.9 %shard_map.120 = (bf16[208,128]{1,0:T(8,128)(2,1)}, bf16[208,128]{1,0:T(8,128)(2,1)}) custom-call(s32[1]{0:T(128)} %bitcast.place_ref, bf16[64,512]{1,0:T(8,128)(2,1)} %refs_0_.1, bf16[64,512]{1,0:T(8,128)(2,1)} %refs_1_.1, bf16[32,512]{1,0:T(8,128)(2,1)} %bitcast.57, bf16[32,512]{1,0:T(8,128)(2,1)} %bitcast.58, bf16[32,512]{1,0:T(8,128)(2,1)} %bitcast.59, ...), custom_call_target="tpu_custom_call" | custom-call | bytes 524288 | tf_op jit(solution)/shard_map/pallas_call | solution.py:105
  2.5 8.8 %collective-permute-start.1 = (bf16[208,128]{1,0:T(8,128)(2,1)}, bf16[208,128]{1,0:T(8,128)(2,1)S(1)}, u32[]{:S(2)}, u32[]{:S(2)}) collective-permute-start(bf16[208,128]{1,0:T(8,128)(2,1)} %get-tuple-element.18), channel_id=1, source_target_pairs={{0,16},{16,0},{1,17},{17,1},{2,18},{18,2},{3,19},{19,3},{4,20},{20... | collective-permute-start | bytes 159752 | tf_op jit(solution)/shard_map/ppermute | solution.py:338
  11.3 1.9 %collective-permute-start = (bf16[512,2048]{1,0:T(8,128)(2,1)}, bf16[512,2048]{1,0:T(8,128)(2,1)}, u32[]{:S(2)}, u32[]{:S(2)}) collective-permute-start(bf16[512,2048]{1,0:T(8,128)(2,1)} %bitcast.45), channel_id=1, source_target_pairs={{0,16},{16,0},{1,17},{17,1},{2,18},{18,2},{3,19},{19,3},{4,20},{20... | collective-permute-start | bytes 6291464 | tf_op jit(solution)/shard_map/ppermute | solution.py:319
  13.3 0.8 maximum_convert_fusion
  14.1 34.8 %all-gather.3 = f16[32,208,128]{2,1,0:T(8,128)(2,1)S(1)} all-gather(f16[2,208,128]{2,1,0:T(8,128)(2,1)S(1)} %maximum_convert_fusion), channel_id=1, replica_groups=mesh['zh'=4,'zl'=4,'core'=2,'tensor'=4,'dp'=4] {'zh','zl'}, dimensions={0}, use_global_device_ids=true | all-gather | bytes 1810432 | tf_op jit(solution)/shard_map/all_gather | solution.py:339
  48.9 0.1 slice.58
  49.1 0.1 slice.49
  49.2 0.1 broadcast_in_dim.12
  49.3 0.1 mul.23
  49.4 0.1 slice_reduce_fusion
  49.5 0.7 multiply_convert_fusion.rows_ref
  50.2 17.1 %all-gather.4 = f16[128,64,128]{2,1,0:T(8,128)(2,1)S(1)} all-gather(f16[32,64,128]{2,1,0:T(8,128)(2,1)S(1)} %slice.58), channel_id=2, replica_groups=mesh['zh'=4,'zl'=4,'core'=2,'tensor'=4,'dp'=4] {'dp'}, dimensions={0}, use_global_device_ids=true | all-gather | bytes 2621440 | tf_op jit(solution)/shard_map/all_gather | solution.py:340
  67.3 2.0 %fusion = bf16[4,32,64,128]{3,2,1,0:T(8,128)(2,1)} fusion(f16[4,32,64,128]{3,2,1,0:T(8,128)(2,1)S(1)} %bitcast.47, f32[32]{0:T(128)S(1)} %slice_reduce_fusion), kind=kLoop, calls=%fused_computation.1 | loop fusion | flops 3145728 | bytes 4194432 | tf_op jit(solution)/shard_map/convert_element_type | solution.py:343
  69.3 0.0 collective-permute-done.other_in
  69.4 11.9 %shard_map.121 = (bf16[512,512]{1,0:T(8,128)(2,1)S(1)}, bf16[512,512]{1,0:T(8,128)(2,1)S(1)}, bf16[256,1024]{1,0:T(8,128)(2,1)}) custom-call(s32[1]{0:T(128)} %bitcast.place_ref, bf16[512,2048]{1,0:T(8,128)(2,1)S(1)} %bitcast.46, bf16[512,2048]{1,0:T(8,128)(2,1)} %collective-permute-done.other_in, bf16[4,2048,128]{2,1,0:T(8,128)(2,1)} %bitcast.48, ...), custom_call_target="tpu_custom_call" | custom-call | flops 2684354560 | bytes 6291456 | tf_op jit(solution)/shard_map/pallas_call | solution.py:199
  81.3 6.5 %all-to-all-start = ((bf16[16,16,1024]{2,1,0:T(8,128)(2,1)}), bf16[16,16,1024]{2,1,0:T(8,128)(2,1)S(1)}, u32[]{:S(2)}, u32[]{:S(2)}) async-start(bf16[16,16,1024]{2,1,0:T(8,128)(2,1)} %bitcast.12), calls=%async_computation | async-start | bytes 1048576 | tf_op jit(solution)/shard_map/all_to_all | solution.py:297
  87.9 10.5 %collective-permute-start.3 = (bf16[64,1280]{1,0:T(8,128)(2,1)S(1)}, bf16[64,1280]{1,0:T(8,128)(2,1)S(1)}, u32[]{:S(2)}, u32[]{:S(2)}) collective-permute-start(bf16[64,1280]{1,0:T(8,128)(2,1)S(1)} %pad_maximum_fusion), channel_id=1, source_target_pairs={{0,16},{16,0},{1,17},{17,1},{2,18},{18,2},{3,19},{19,3},{4,20},{20... | collective-permute-start | bytes 491528 | tf_op jit(solution)/shard_map/ppermute | solution.py:324
  98.4 1.9 %collective-permute-start.2 = (bf16[512,512]{1,0:T(8,128)(2,1)S(1)}, bf16[512,512]{1,0:T(8,128)(2,1)S(1)}, u32[]{:S(2)}, u32[]{:S(2)}) collective-permute-start(bf16[512,512]{1,0:T(8,128)(2,1)S(1)} %get-tuple-element.21), channel_id=1, source_target_pairs={{0,16},{16,0},{1,17},{17,1},{2,18},{18,2},{3,19},{19,3},{4,20},{20... | collective-permute-start | bytes 1572872 | tf_op jit(solution)/shard_map/ppermute | solution.py:350
  100.4 0.1 maximum_select_fusion.2.latent_ref
  100.5 1.7 %collective-permute-done.2 = bf16[512,512]{1,0:T(8,128)(2,1)S(1)} collective-permute-done((bf16[512,512]{1,0:T(8,128)(2,1)S(1)}, bf16[512,512]{1,0:T(8,128)(2,1)S(1)}, u32[]{:S(2)}, u32[]{:S(2)}) %collective-permute-start.2) | collective-permute-done | bytes 524320 | tf_op jit(solution)/shard_map/ppermute | solution.py:350
  102.2 1.2 maximum_select_fusion
  103.5 1.1 all-to-all-done
  104.6 0.1 reduce_sum.24
  104.6 0.1 broadcast_in_dim.13
  104.7 34.5 %all_to_all.15 = bf16[16,16,1024]{2,1,0:T(8,128)(2,1)S(1)} all-to-all(bf16[16,16,1024]{2,1,0:T(8,128)(2,1)S(1)} %broadcast_in_dim.13), channel_id=1, replica_groups=mesh['zh'=4,'zl'=4,'core'=2,'tensor'=4,'dp'=4] {'zh','zl'}, dimensions={0} | all-to-all | bytes 1048576 | tf_op jit(solution)/shard_map/all_to_all | solution.py:297
  139.2 1.4 shard_map.122
  140.6 11.6 %collective-permute-start.4 = (bf16[64,256]{1,0:T(8,128)(2,1)S(1)}, bf16[64,256]{1,0:T(8,128)(2,1)S(1)}, u32[]{:S(2)}, u32[]{:S(2)}) collective-permute-start(bf16[64,256]{1,0:T(8,128)(2,1)S(1)} %get-tuple-element.29), channel_id=1, source_target_pairs={{0,16},{16,0},{1,17},{17,1},{2,18},{18,2},{3,19},{19,3},{4,20},{20... | collective-permute-start | bytes 98312 | tf_op jit(solution)/shard_map/ppermute | solution.py:372
  152.2 4.4 %all-to-all-start.2 = ((bf16[8,64,256]{2,1,0:T(8,128)(2,1)}), bf16[8,64,256]{2,1,0:T(8,128)(2,1)S(1)}, u32[]{:S(2)}, u32[]{:S(2)}) async-start(bf16[8,64,256]{2,1,0:T(8,128)(2,1)} %get-tuple-element.27), calls=%async_computation.2 | async-start | bytes 524288 | tf_op jit(solution)/shard_map/all_to_all | solution.py:297
  156.6 0.0 collective-permute-done.4
  156.6 9.7 %all_gather.16.part_ref = bf16[4,64,512]{2,1,0:T(8,128)(2,1)S(1)} all-gather(bf16[1,64,512]{2,1,0:T(8,128)(2,1)S(1)} %maximum_select_fusion.4), channel_id=1, replica_groups=mesh['zh'=4,'zl'=4,'core'=2,'tensor'=4,'dp'=4] {'dp'}, dimensions={0}, use_global_device_ids=true | all-gather | bytes 327680 | tf_op jit(solution)/shard_map/all_gather | solution.py:379
  166.3 0.7 shard_map.123
  167.0 0.7 reduce_sum.25
  (20 shorter events, 0.2 us)
Async XLA Ops:
  2.5 10.7 %collective-permute-start.1 = (bf16[208,128]{1,0:T(8,128)(2,1)}, bf16[208,128]{1,0:T(8,128)(2,1)S(1)}, u32[]{:S(2)}, u32[]{:S(2)}) collective-permute-start(bf16[208,128]{1,0:T(8,128)(2,1)} %get-tuple-element.18), channel_id=1, source_target_pairs={{0,16},{16,0},{1,17},{17,1},{2,18},{18,2},{3,19},{19,3},{4,20},{20... | collective-permute-start | bytes 159752 | tf_op jit(solution)/shard_map/ppermute | solution.py:338
  11.3 58.0 %collective-permute-start = (bf16[512,2048]{1,0:T(8,128)(2,1)}, bf16[512,2048]{1,0:T(8,128)(2,1)}, u32[]{:S(2)}, u32[]{:S(2)}) collective-permute-start(bf16[512,2048]{1,0:T(8,128)(2,1)} %bitcast.45), channel_id=1, source_target_pairs={{0,16},{16,0},{1,17},{17,1},{2,18},{18,2},{3,19},{19,3},{4,20},{20... | collective-permute-start | bytes 6291464 | tf_op jit(solution)/shard_map/ppermute | solution.py:319
  67.3 2.0 %copy-start = (bf16[1,512,2048]{2,1,0:T(8,128)(2,1)S(1)}, bf16[1,512,2048]{2,1,0:T(8,128)(2,1)}, u32[]{:S(2)}) copy-start(bf16[1,512,2048]{2,1,0:T(8,128)(2,1)} %param.9) | copy-start | bytes 6291460
  69.4 18.5 %copy-start.2 = (bf16[64,512]{1,0:T(8,128)(2,1)S(1)}, bf16[64,512]{1,0:T(8,128)(2,1)}, u32[]{:S(2)}) copy-start(bf16[64,512]{1,0:T(8,128)(2,1)} %param.12) | copy-start | bytes 196612
  69.4 18.5 %copy-start.1 = (bf16[1,1024,64]{1,2,0:T(8,128)(2,1)S(1)}, bf16[1,1024,64]{1,2,0:T(8,128)(2,1)}, u32[]{:S(2)}) copy-start(bf16[1,1024,64]{1,2,0:T(8,128)(2,1)} %param.17) | copy-start | bytes 393220
  81.3 23.3 %all-to-all-start = ((bf16[16,16,1024]{2,1,0:T(8,128)(2,1)}), bf16[16,16,1024]{2,1,0:T(8,128)(2,1)S(1)}, u32[]{:S(2)}, u32[]{:S(2)}) async-start(bf16[16,16,1024]{2,1,0:T(8,128)(2,1)} %bitcast.12), calls=%async_computation | async-start | bytes 1048576 | tf_op jit(solution)/shard_map/all_to_all | solution.py:297
  87.9 12.4 %collective-permute-start.3 = (bf16[64,1280]{1,0:T(8,128)(2,1)S(1)}, bf16[64,1280]{1,0:T(8,128)(2,1)S(1)}, u32[]{:S(2)}, u32[]{:S(2)}) collective-permute-start(bf16[64,1280]{1,0:T(8,128)(2,1)S(1)} %pad_maximum_fusion), channel_id=1, source_target_pairs={{0,16},{16,0},{1,17},{17,1},{2,18},{18,2},{3,19},{19,3},{4,20},{20... | collective-permute-start | bytes 491528 | tf_op jit(solution)/shard_map/ppermute | solution.py:324
  98.4 3.8 %collective-permute-start.2 = (bf16[512,512]{1,0:T(8,128)(2,1)S(1)}, bf16[512,512]{1,0:T(8,128)(2,1)S(1)}, u32[]{:S(2)}, u32[]{:S(2)}) collective-permute-start(bf16[512,512]{1,0:T(8,128)(2,1)S(1)} %get-tuple-element.21), channel_id=1, source_target_pairs={{0,16},{16,0},{1,17},{17,1},{2,18},{18,2},{3,19},{19,3},{4,20},{20... | collective-permute-start | bytes 1572872 | tf_op jit(solution)/shard_map/ppermute | solution.py:350
  140.6 16.1 %collective-permute-start.4 = (bf16[64,256]{1,0:T(8,128)(2,1)S(1)}, bf16[64,256]{1,0:T(8,128)(2,1)S(1)}, u32[]{:S(2)}, u32[]{:S(2)}) collective-permute-start(bf16[64,256]{1,0:T(8,128)(2,1)S(1)} %get-tuple-element.29), channel_id=1, source_target_pairs={{0,16},{16,0},{1,17},{17,1},{2,18},{18,2},{3,19},{19,3},{4,20},{20... | collective-permute-start | bytes 98312 | tf_op jit(solution)/shard_map/ppermute | solution.py:372
  152.2 14.8 %all-to-all-start.2 = ((bf16[8,64,256]{2,1,0:T(8,128)(2,1)}), bf16[8,64,256]{2,1,0:T(8,128)(2,1)S(1)}, u32[]{:S(2)}, u32[]{:S(2)}) async-start(bf16[8,64,256]{2,1,0:T(8,128)(2,1)} %get-tuple-element.27), calls=%async_computation.2 | async-start | bytes 524288 | tf_op jit(solution)/shard_map/all_to_all | solution.py:297
